TPU v7x, 32 devices: a whole 2x2x4 slice. The times are simulated.
32 devices in a mesh: grp: 1, wide: 8 (over z, y), nar: 4 (over x, core).
Axes of the slice: x: 2, y: 2, z: 4, core: 2. Of those that a mesh axis runs over, the one named last changes fastest.
Arguments:
- tokens: bfloat16 [512, 8192], P('grp', ('nar', 'wide')), may hold values from -6 to 6
- gate_weight: bfloat16 [8192, 26624], P('nar', 'wide'), may hold values from -0.0625 to 0.0625
- gate_scale: float32 [64, 26624], P('nar', 'wide'), may hold values from 0.5 to 2
- up_weight: bfloat16 [8192, 26624], P('nar', 'wide'), may hold values from -0.0625 to 0.0625
- up_scale: float32 [64, 26624], P('nar', 'wide'), may hold values from 0.5 to 2
- down_weight: bfloat16 [26624, 8192], P('wide', 'nar'), may hold values from -0.0390625 to 0.0390625
- down_scale: float32 [208, 8192], P('wide', 'nar'), may hold values from 0.5 to 2
Outputs:
- mixed: bfloat16 [512, 8192], P('grp', ('nar', 'wide'))
All inputs are finite; a program needn't handle non-finite values.
Results may differ from a plain program's by a relative error of at most 0.02.
Values may be sent and summed in bfloat16 or wider, within the bound.
No kernel may reach another device: no remote copies, remote signals or barrier semaphores. Data moves between devices by JAX's collectives and lax.ppermute only.
A program may use at most 128 MiB of HBM per device.

v0:
```python
import jax
import jax.numpy as jnp
from jax import lax
from jax.sharding import PartitionSpec as P


def decode_weight(codes, scales):
    rows, cols = codes.shape
    blocks = codes.astype(jnp.float32).reshape(rows // 128, 128, cols) * scales[:, None, :]
    return blocks.reshape(rows, cols).astype(jnp.bfloat16)


def on_device(tokens, gate_weight, gate_scale, up_weight, up_scale, down_weight, down_scale):
    gate_deq = decode_weight(gate_weight, gate_scale)
    up_deq = decode_weight(up_weight, up_scale)
    down_deq = decode_weight(down_weight, down_scale)
    segment = lax.all_gather(tokens, "wide", axis=1, tiled=True)
    gate_part = jnp.dot(segment, gate_deq, preferred_element_type=jnp.float32)
    up_part = jnp.dot(segment, up_deq, preferred_element_type=jnp.float32)
    gate_sum, up_sum = (
        lax.psum_scatter(
            gate_part.astype(jnp.bfloat16), "nar", scatter_dimension=1, tiled=True
        ).astype(jnp.float32),
        lax.psum_scatter(
            up_part.astype(jnp.bfloat16), "nar", scatter_dimension=1, tiled=True
        ).astype(jnp.float32),
    )
    hidden_share = (jax.nn.silu(gate_sum) * up_sum).astype(jnp.bfloat16)
    down_terms = jnp.dot(
        lax.all_gather(hidden_share, "nar", axis=1, tiled=True),
        down_deq,
        preferred_element_type=jnp.float32,
    )
    return lax.psum_scatter(
        down_terms.astype(jnp.bfloat16), "wide", scatter_dimension=1, tiled=True
    )


def solution(mesh):
    in_specs = (
        P("grp", ("nar", "wide")),
        P("nar", "wide"),
        P("nar", "wide"),
        P("nar", "wide"),
        P("nar", "wide"),
        P("wide", "nar"),
        P("wide", "nar"),
    )
    out_specs = P("grp", ("nar", "wide"))
    return jax.shard_map(
        on_device, mesh=mesh, in_specs=in_specs, out_specs=out_specs, check_vma=False
    )
```

profile of v0, /device:TPU:0, one launch (start us, length us, event | category | flops | bytes accessed | tf_op | source)
XLA Modules:
  0.0 278.0 jit_solution(9028096967075148821)
XLA Ops:
  6.5 0.0 all-gather.3.cloned.1.call-start
  6.5 0.7 all-gather.3.cloned.1.call-update
  7.3 0.0 reduce-scatter.4.cloned.1.call-start
  7.3 10.8 %fusion.2 = bf16[2048,3328]{1,0:T(8,128)(2,1)} fusion(bf16[2048,3328]{1,0:T(8,128)(2,1)} %param.8, f32[16,3328]{1,0:T(8,128)} %param.9), kind=kLoop, calls=%fused_computation.5 | loop fusion | flops 20447232 | bytes 27475968 | tf_op jit(solution)/shard_map/convert_element_type | solution.py:10
  18.1 0.0 copy-start.1
  18.1 45.1 %all-gather.3.cloned.1.call-done = bf16[512,2048]{1,0:T(8,128)(2,1)} async-done(((bf16[512,256]{1,0:T(8,128)(2,1)}), bf16[512,2048]{1,0:T(8,128)(2,1)}) %all-gather.3.cloned.1.call-update) | async-done | bytes 2097168 | tf_op jit(solution)/shard_map/all_gather | solution.py:17
  63.2 14.0 %fusion.3 = bf16[512,3328]{0,1:T(8,128)(2,1)} fusion(bf16[2048,3328]{1,0:T(8,128)(2,1)} %fusion.2, bf16[512,2048]{1,0:T(8,128)(2,1)} %all-gather.3.cloned.1.call-done), kind=kOutput, calls=%fused_computation.8 | convolution fusion | flops 6981025792 | bytes 19136512 | tf_op jit(solution)/shard_map/dot_general | solution.py:18
  77.2 0.0 reduce-scatter.4.cloned.1.call-update
  77.2 0.0 copy-start.2
  77.2 0.0 reduce-scatter.6.cloned.1.call-start
  77.2 0.0 copy-done.1
  77.3 8.6 %fusion.1 = bf16[2048,3328]{1,0:T(8,128)(2,1)S(1)} fusion(bf16[2048,3328]{1,0:T(8,128)(2,1)} %param.10, f32[16,3328]{1,0:T(8,128)S(1)} %copy-done.1), kind=kLoop, calls=%fused_computation.3 | loop fusion | flops 20447232 | bytes 27475968 | tf_op jit(solution)/shard_map/convert_element_type | solution.py:10
  85.9 0.0 copy-done.2
  85.9 0.0 copy-start
  85.9 9.1 %fusion.4 = bf16[512,3328]{0,1:T(8,128)(2,1)} fusion(bf16[2048,3328]{1,0:T(8,128)(2,1)S(1)} %fusion.1, bf16[512,2048]{1,0:T(8,128)(2,1)S(1)} %copy-done.2), kind=kOutput, calls=%fused_computation.9 | convolution fusion | flops 6981025792 | bytes 19136512 | tf_op jit(solution)/shard_map/dot_general | solution.py:19
  95.1 0.0 reduce-scatter.6.cloned.1.call-update
  95.1 0.0 all-gather.5.cloned.1.call-start
  95.1 20.0 %reduce-scatter.4.cloned.1.call-done = bf16[512,832]{0,1:T(8,128)(2,1)} async-done(((bf16[512,3328]{0,1:T(8,128)(2,1)}), bf16[512,832]{0,1:T(8,128)(2,1)}) %reduce-scatter.4.cloned.1.call-update) | async-done | bytes 851984 | tf_op jit(solution)/shard_map/reduce_scatter | solution.py:21
  115.1 42.4 %reduce-scatter.6.cloned.1.call-done = bf16[512,832]{0,1:T(8,128)(2,1)} async-done(((bf16[512,3328]{0,1:T(8,128)(2,1)}), bf16[512,832]{0,1:T(8,128)(2,1)}) %reduce-scatter.6.cloned.1.call-update) | async-done | bytes 851984 | tf_op jit(solution)/shard_map/reduce_scatter | solution.py:24
  157.5 2.9 %fusion.9 = bf16[512,832]{0,1:T(8,128)(2,1)} fusion(bf16[512,832]{0,1:T(8,128)(2,1)} %reduce-scatter.6.cloned.1.call-done, bf16[512,832]{0,1:T(8,128)(2,1)} %reduce-scatter.4.cloned.1.call-done), kind=kLoop, calls=%fused_computation.17 | loop fusion | flops 3407872 | bytes 2555904 | tf_op jit(solution)/shard_map/convert_element_type | solution.py:28
  160.4 0.0 all-gather.5.cloned.1.call-update
  160.4 0.2 reduce-scatter.8.cloned.1.call-start
  160.6 0.0 copy-done
  160.6 11.3 %fusion = bf16[3328,2048]{1,0:T(8,128)(2,1)} fusion(bf16[3328,2048]{1,0:T(8,128)(2,1)} %param.12, f32[26,2048]{1,0:T(8,128)S(1)} %copy-done), kind=kLoop, calls=%fused_computation.1 | loop fusion | flops 20447232 | bytes 27475968 | tf_op jit(solution)/shard_map/convert_element_type | solution.py:10
  172.0 18.6 %all-gather.5.cloned.1.call-done = bf16[512,3328]{0,1:T(8,128)(2,1)} async-done(((bf16[512,832]{0,1:T(8,128)(2,1)}), bf16[512,3328]{0,1:T(8,128)(2,1)}) %all-gather.5.cloned.1.call-update) | async-done | bytes 3407888 | tf_op jit(solution)/shard_map/all_gather | solution.py:30
  190.6 12.3 %convolution_convert_fusion.2 = bf16[512,2048]{1,0:T(8,128)(2,1)} fusion(bf16[512,3328]{0,1:T(8,128)(2,1)} %all-gather.5.cloned.1.call-done, bf16[3328,2048]{1,0:T(8,128)(2,1)} %fusion), kind=kOutput, calls=%fused_computation.10 | convolution fusion | flops 6980370432 | bytes 19136512 | tf_op jit(solution)/shard_map/dot_general | solution.py:29
  202.9 0.0 reduce-scatter.8.cloned.1.call-update
  202.9 68.5 %reduce-scatter.8.cloned.1.call-done = bf16[512,256]{1,0:T(8,128)(2,1)} async-done(((bf16[512,2048]{1,0:T(8,128)(2,1)}), bf16[512,256]{1,0:T(8,128)(2,1)}) %reduce-scatter.8.cloned.1.call-update) | async-done | bytes 262160 | tf_op jit(solution)/shard_map/reduce_scatter | solution.py:34
Async XLA Ops:
  6.5 56.7 %all-gather.3.cloned.1.call-start = ((), (), s32[]{:S(2)}) async-start(), calls=%async_computation.3 | async-start | bytes 2359296 | tf_op jit(solution)/shard_map/all_gather | solution.py:17
  7.3 107.9 %reduce-scatter.4.cloned.1.call-start = ((), (), s32[]{:S(2)}) async-start(), calls=%async_computation.4 | async-start | bytes 4259840 | tf_op jit(solution)/shard_map/reduce_scatter | solution.py:21
  18.1 59.2 %copy-start.1 = (f32[16,3328]{1,0:T(8,128)S(1)}, f32[16,3328]{1,0:T(8,128)}, u32[]{:S(2)}) copy-start(f32[16,3328]{1,0:T(8,128)} %param.11) | copy-start | bytes 638980
  77.2 8.7 %copy-start.2 = (bf16[512,2048]{1,0:T(8,128)(2,1)S(1)}, bf16[512,2048]{1,0:T(8,128)(2,1)}, u32[]{:S(2)}) copy-start(bf16[512,2048]{1,0:T(8,128)(2,1)} %all-gather.3.cloned.1.call-done) | copy-start | bytes 6291460
  77.2 80.3 %reduce-scatter.6.cloned.1.call-start = ((), (), s32[]{:S(2)}) async-start(), calls=%async_computation.5 | async-start | bytes 4259840 | tf_op jit(solution)/shard_map/reduce_scatter | solution.py:24
  85.9 74.7 %copy-start = (f32[26,2048]{1,0:T(8,128)S(1)}, f32[26,2048]{1,0:T(8,128)}, u32[]{:S(2)}) copy-start(f32[26,2048]{1,0:T(8,128)} %param.13) | copy-start | bytes 638980
  95.1 95.5 %all-gather.5.cloned.1.call-start = ((), (), s32[]{:S(2)}) async-start(), calls=%async_computation.6 | async-start | bytes 4259840 | tf_op jit(solution)/shard_map/all_gather | solution.py:30
  160.4 111.1 %reduce-scatter.8.cloned.1.call-start = ((), (), s32[]{:S(2)}) async-start(), calls=%async_computation.7 | async-start | bytes 2359296 | tf_op jit(solution)/shard_map/reduce_scatter | solution.py:34
Sparse Core Ops, SparseCore 0:
  9.4 53.7 all-gather.2
  77.3 37.7 reduce-scatter.3
  117.8 39.6 reduce-scatter.5
  160.5 30.0 all-gather.4
  203.0 68.3 reduce-scatter.7
where the time goes:
time: 278 us
  waiting for transfers between devices  195 us (70%)
  matrix products  35.4 us (13%)
  other arithmetic  33.6 us (12%)
  between operations  13.2 us (5%)
    reduce_scatter x1, waiting for transfers between devices, on_device(): lax.psum_scatter(down_terms.astype(jnp.bfloat16), 'wide', scatter_dimensi...  68.5 us
    all_gather x1, waiting for transfers between devices, on_device(): segment = lax.all_gather(tokens, 'wide', axis=1, tiled=True)  45.1 us
    reduce_scatter x1, waiting for transfers between devices, on_device(): lax.psum_scatter(up_part.astype(jnp.bfloat16), 'nar', scatter_dimension=1...  42.4 us
    convert_element_type x3, other arithmetic, decode_weight(): return blocks.reshape(rows, cols).astype(jnp.bfloat16)  30.7 us
    reduce_scatter x1, waiting for transfers between devices, on_device(): lax.psum_scatter(gate_part.astype(jnp.bfloat16), 'nar', scatter_dimension...  20 us
    all_gather x1, waiting for transfers between devices, on_device(): lax.all_gather(hidden_share, 'nar', axis=1, tiled=True)  18.6 us
    dot_general x1, matrix products, on_device(): gate_part = jnp.dot(segment, gate_deq, preferred_element_type=jnp.float32)  14 us
    dot_general x1, matrix products, on_device(): jnp.dot(lax.all_gather(hidden_share, 'nar', axis=1, tiled=True), down_deq...  12.3 us
  transfers between devices with their start and end apart: 5, of which 5 were waited for; matrix products, arithmetic and copies ran while one was open for 14% of the time, Pallas kernels for 0%

commit v1 on v0

v1 whole, which is shorter than its diff:
```python
import functools

import jax
import jax.numpy as jnp
from jax import lax
from jax.experimental import pallas as pl
from jax.experimental.pallas import tpu as pltpu
from jax.sharding import PartitionSpec as P

GROUP = 128
MIB = 1 << 20


def n_bits(size):
    return size.bit_length() - 1


def reverse_bits(value, bits):
    out = value * 0
    for b in range(bits):
        out = out + ((value >> b) & 1) * (1 << (bits - 1 - b))
    return out


def flip(array, axis, size, mask):
    return lax.ppermute(array, axis, [(i, i ^ mask) for i in range(size)])


def decode(codes, scales):
    rows, cols = codes.shape
    blocks = codes.reshape(rows // GROUP, GROUP, cols) * scales.astype(jnp.bfloat16)[:, None, :]
    return blocks.reshape(rows, cols)


def in_hbm(array):
    return pltpu.with_memory_space_constraint(array, pltpu.HBM)


def in_vmem(array):
    return pltpu.with_memory_space_constraint(array, pltpu.VMEM)


def after(array, *others):
    return lax.optimization_barrier((array, *others))[0]


def cost(size=1024):
    return pl.CostEstimate(flops=size, bytes_accessed=size, transcendentals=0)


def decode_kernel(first, block, w_ref, sc_ref, out_ref, arrived):
    size = out_ref.shape[0]

    def fetch(k):
        return pltpu.make_async_copy(
            w_ref.at[pl.ds(first + k * block, block)], out_ref.at[pl.ds(k * block, block)], arrived.at[k]
        )

    count = size // block
    for k in range(count):
        fetch(k).start()
    for k in range(count):
        fetch(k).wait()
        for g in range(k * block // GROUP, (k + 1) * block // GROUP):
            rows = slice(g * GROUP, (g + 1) * GROUP)
            out_ref[rows] = out_ref[rows] * sc_ref[first // GROUP + g : first // GROUP + g + 1].astype(jnp.bfloat16)


def decode_part(codes, scales, part, parts):
    depth, units = codes.shape
    size = depth // parts
    block = 256 if size % 256 == 0 else GROUP
    vmem = pl.BlockSpec(memory_space=pltpu.VMEM)
    return pl.pallas_call(
        functools.partial(decode_kernel, part * size, block),
        in_specs=[pl.BlockSpec(memory_space=pl.ANY), vmem],
        out_specs=vmem,
        out_shape=pltpu.VMEM((size, units), jnp.bfloat16),
        scratch_shapes=[pltpu.SemaphoreType.DMA((size // block,))],
        compiler_params=pltpu.CompilerParams(vmem_limit_bytes=6 * MIB),
        cost_estimate=cost(),
        name="decode",
    )(in_hbm(codes), scales)


def gate_up_kernel(n_tok, n_gate, n_up, place_ref, *refs):
    cuts = (n_tok, n_tok + n_gate, n_tok + n_gate + n_up)
    tok_refs, gate_refs, up_refs = refs[: cuts[0]], refs[cuts[0] : cuts[1]], refs[cuts[1] : cuts[2]]
    keep_ref, send_ref, x_ref = refs[cuts[2] :]
    shards = [ref.at[i] for ref in tok_refs for i in range(ref.shape[0])]
    bits = n_bits(len(shards))
    for p, shard in enumerate(shards):
        width = shard.shape[1]
        spot = pl.multiple_of((place_ref[0] ^ reverse_bits(p, bits)) * width, width)
        x_ref[:, pl.ds(spot, width)] = shard[...]
    half, quarter = keep_ref.shape[0], keep_ref.shape[2]
    units = gate_refs[0].shape[1]
    tile = 256 if units % 256 == 0 else 128

    def column(j, carry):
        cols = pl.ds(pl.multiple_of(j * tile, tile), tile)
        for s, w_refs in enumerate((gate_refs, up_refs)):
            part = sum(
                jnp.dot(
                    x_ref[:, k * w_ref.shape[0] : (k + 1) * w_ref.shape[0]],
                    w_ref[:, cols],
                    preferred_element_type=jnp.float32,
                )
                for k, w_ref in enumerate(w_refs)
            ).astype(jnp.bfloat16)
            for b in range(half):
                keep_ref[b, s, :, cols] = part[b * quarter : (b + 1) * quarter]
                send_ref[b, s, :, cols] = part[(half + b) * quarter : (half + b + 1) * quarter]
        return carry

    lax.fori_loop(0, units // tile, column, 0)


def gate_up(place, shards, gate, up, n_nar):
    count, (rows, width) = sum(t.shape[0] for t in shards), shards[0].shape[1:]
    depth, units = sum(g.shape[0] for g in gate), gate[0].shape[1]
    quarter = rows // n_nar
    shape = (n_nar // 2, 2, quarter, units)
    if width % 128:
        order = reverse_bits(place ^ jnp.arange(count), n_bits(count))
        x = jnp.take(jnp.concatenate(shards), order, axis=0).transpose(1, 0, 2).reshape(rows, depth)
        both = [
            jnp.dot(x, jnp.concatenate(w), preferred_element_type=jnp.float32)
            .astype(jnp.bfloat16)
            .reshape(2, n_nar // 2, quarter, units)
            for w in (gate, up)
        ]
        both = jnp.stack(both, axis=2)
        return both[0], both[1]
    out = jax.ShapeDtypeStruct(shape, jnp.bfloat16)
    vmem = pl.BlockSpec(memory_space=pltpu.VMEM)
    return pl.pallas_call(
        functools.partial(gate_up_kernel, len(shards), len(gate), len(up)),
        in_specs=[pl.BlockSpec(memory_space=pltpu.SMEM)] + [vmem] * (len(shards) + len(gate) + len(up)),
        out_specs=[vmem, vmem],
        scratch_shapes=[pltpu.VMEM((rows, depth), jnp.bfloat16)],
        out_shape=[out, out],
        compiler_params=pltpu.CompilerParams(vmem_limit_bytes=6 * MIB),
        cost_estimate=cost(),
        name="gate_up",
    )(place.reshape(1), *shards, *[in_vmem(w) for w in (*gate, *up)])


def down_kernel(parts, pieces, place_ref, *refs):
    h_refs, w_refs, (keep_ref, send_ref, h_ref) = refs[:parts], refs[parts : parts + pieces], refs[parts + pieces :]
    top = 0
    for ref in h_refs:
        h_ref[top : top + ref.shape[0]] = ref[...]
        top += ref.shape[0]
    half, _, width = keep_ref.shape
    bits = n_bits(2 * half)
    size = w_refs[0].shape[0]
    for out_ref, first in ((send_ref, half), (keep_ref, 0)):

        def block(i, carry, out_ref=out_ref, first=first):
            spot = pl.multiple_of((place_ref[0] ^ reverse_bits(first + i, bits)) * width, width)
            part = sum(
                jnp.dot(
                    h_ref[:, k * size : (k + 1) * size], w_ref[:, pl.ds(spot, width)], preferred_element_type=jnp.float32
                )
                for k, w_ref in enumerate(w_refs)
            )
            out_ref[i] = part.astype(jnp.bfloat16)
            return carry

        lax.fori_loop(0, half, block, 0)


def down(place, hidden, weights, n_wide):
    rows = sum(h.shape[0] for h in hidden)
    units, features = sum(w.shape[0] for w in weights), weights[0].shape[1]
    width, bits, half = features // n_wide, n_bits(n_wide), n_wide // 2
    if width % 128:
        part = jnp.dot(jnp.concatenate(hidden), jnp.concatenate(weights), preferred_element_type=jnp.float32)
        part = part.astype(jnp.bfloat16).reshape(rows, n_wide, width).transpose(1, 0, 2)
        part = jnp.take(part, place ^ reverse_bits(jnp.arange(n_wide), bits), axis=0)
        return part[:half], part[half:]
    out = jax.ShapeDtypeStruct((half, rows, width), jnp.bfloat16)
    vmem = pl.BlockSpec(memory_space=pltpu.VMEM)
    return pl.pallas_call(
        functools.partial(down_kernel, len(hidden), len(weights)),
        in_specs=[pl.BlockSpec(memory_space=pltpu.SMEM)] + [vmem] * (len(hidden) + len(weights)),
        out_specs=[vmem, vmem],
        scratch_shapes=[pltpu.VMEM((rows, units), jnp.bfloat16)],
        out_shape=[out, out],
        compiler_params=pltpu.CompilerParams(vmem_limit_bytes=6 * MIB),
        cost_estimate=cost(),
        name="down",
    )(place.reshape(1), *hidden, *[in_vmem(w) for w in weights])


def add(a, b):
    return (a.astype(jnp.float32) + b.astype(jnp.float32)).astype(jnp.bfloat16)


def kernel_call(kernel, shapes, *operands, name, size=1024):
    vmem = pl.BlockSpec(memory_space=pltpu.VMEM)
    return pl.pallas_call(
        kernel,
        in_specs=[vmem] * len(operands),
        out_specs=[vmem] * len(shapes),
        out_shape=[jax.ShapeDtypeStruct(shape, jnp.bfloat16) for shape in shapes],
        compiler_params=pltpu.CompilerParams(vmem_limit_bytes=4 * MIB),
        cost_estimate=cost(size),
        name=name,
    )(*operands)


def tiles_of(width):
    return 256 if width % 256 == 0 else 128 if width % 128 == 0 else width


def add_halves_kernel(a_ref, *refs):
    piece_refs, (first_ref, second_ref) = refs[:-2], refs[-2:]
    half, width = first_ref.shape[0], a_ref.shape[-1]
    tile = tiles_of(width)

    def columns(j, carry):
        cols = pl.ds(pl.multiple_of(j * tile, tile), tile)
        for i in range(2 * half):
            for s in (0, 1):
                total = add(a_ref[i, s, :, cols], piece_refs[2 * i + s][:, cols])
                (first_ref if i < half else second_ref)[i % half, s, :, cols] = total
        return carry

    lax.fori_loop(0, width // tile, columns, 0)


def add_halves(a, pieces):
    if a.shape[-1] % 128 or a.shape[-2] % 16:
        total = add(a, jnp.stack(pieces).reshape(a.shape))
        return total[: a.shape[0] // 2], total[a.shape[0] // 2 :]
    shape = (a.shape[0] // 2, *a.shape[1:])
    return kernel_call(add_halves_kernel, [shape, shape], a, *pieces, name="add_halves")


def gated_kernel(a_ref, b_ref, out_ref):
    width = out_ref.shape[-1]
    tile = tiles_of(width)

    def columns(j, carry):
        cols = pl.ds(pl.multiple_of(j * tile, tile), tile)
        gate, up = (a_ref[0, s, :, cols].astype(jnp.float32) + b_ref[0, s, :, cols].astype(jnp.float32) for s in (0, 1))
        out_ref[:, cols] = (gate / (1 + jnp.exp(-gate)) * up).astype(jnp.bfloat16)
        return carry

    lax.fori_loop(0, width // tile, columns, 0)


def gated_sum(a, b):
    if a.shape[-1] % 128 or a.shape[-2] % 16:
        gate, up = (a[0, s].astype(jnp.float32) + b[0, s].astype(jnp.float32) for s in (0, 1))
        return (jax.nn.silu(gate) * up).astype(jnp.bfloat16)
    return kernel_call(gated_kernel, [a.shape[2:]], a, b, name="gated", size=4 * MIB)[0]


def deal_kernel(edges, place_ref, x_ref, *out_refs):
    count = x_ref.shape[0]
    for i in range(count):
        source = place_ref[0] ^ reverse_bits(i, n_bits(count))
        for out_ref, lo, hi in zip(out_refs, edges, edges[1:]):
            out_ref[i] = x_ref[source, lo:hi]


def deal(place, x, edges):
    count, _, width = x.shape
    sizes = [hi - lo for lo, hi in zip(edges, edges[1:])]
    if width % 128 or any(size % 16 for size in sizes):
        x = jnp.take(x, place ^ reverse_bits(jnp.arange(count), n_bits(count)), axis=0)
        return [x[:, lo:hi] for lo, hi in zip(edges, edges[1:])]
    vmem = pl.BlockSpec(memory_space=pltpu.VMEM)
    return pl.pallas_call(
        functools.partial(deal_kernel, edges),
        in_specs=[pl.BlockSpec(memory_space=pltpu.SMEM), vmem],
        out_specs=[vmem] * len(sizes),
        out_shape=[jax.ShapeDtypeStruct((count, size, width), x.dtype) for size in sizes],
        compiler_params=pltpu.CompilerParams(vmem_limit_bytes=4 * MIB),
        cost_estimate=cost(),
        name="deal",
    )(place.reshape(1), x)


def collect_kernel(edges, place_ref, *refs):
    part_refs, out_ref = refs[:-1], refs[-1]
    count = out_ref.shape[0]
    for i in range(count):
        target = place_ref[0] ^ reverse_bits(i, n_bits(count))
        for part_ref, lo, hi in zip(part_refs, edges, edges[1:]):
            out_ref[target, lo:hi] = part_ref[i]


def collect(place, parts, edges):
    count, _, width = parts[0].shape
    if width % 128 or any((hi - lo) % 16 for lo, hi in zip(edges, edges[1:])):
        order = reverse_bits(place ^ jnp.arange(count), n_bits(count))
        return jnp.take(jnp.concatenate(parts, axis=1), order, axis=0)
    vmem = pl.BlockSpec(memory_space=pltpu.VMEM)
    return pl.pallas_call(
        functools.partial(collect_kernel, edges),
        in_specs=[pl.BlockSpec(memory_space=pltpu.SMEM)] + [vmem] * len(parts),
        out_specs=vmem,
        out_shape=jax.ShapeDtypeStruct((count, edges[-1], width), parts[0].dtype),
        compiler_params=pltpu.CompilerParams(vmem_limit_bytes=4 * MIB),
        cost_estimate=cost(),
        name="collect",
    )(place.reshape(1), *parts)


def on_device(n_wide, n_nar, cuts, tokens, gw, gs, uw, us, dw, ds):
    wide, nar = lax.axis_index("wide"), lax.axis_index("nar")
    nar_bits, wide_bits = n_bits(n_nar), n_bits(n_wide)
    rows, width = tokens.shape
    fast = width % 128 == 0
    n = len(cuts)
    edges = [sum(cuts[:k]) // n_nar for k in range(n + 1)]
    dealt = deal(nar, after(tokens.reshape(n_nar, rows // n_nar, width), wide), edges)
    tok = [[t.reshape(1, -1, width)] for t in dealt]
    level = [wide_bits] * n

    def gather_tokens(k, to, *others):
        while level[k] > to:
            level[k] -= 1
            got = flip(tok[k][0], "wide", n_wide, 1 << level[k])
            if others:
                got = after(got, *others)
            tok[k] = [jnp.concatenate([tok[k][0], got])] if level[k] else [tok[k][0], got]

    def sum_core(k, *others):
        for b in range(nar_bits - 1):
            got = [flip(send[k][i, j], "nar", n_nar, 1 << b) for i in range(send[k].shape[0]) for j in (0, 1)]
            if others:
                got[0] = after(got[0], *others)
            keep[k], send[k] = add_halves(keep[k], got)

    far = 1 << (nar_bits - 1)

    def gated(k, *others):
        got = after(flip(send[k], "nar", n_nar, far), *others)
        hidden[k] = [gated_sum(keep[k], got)]
        hidden[k].append(flip(hidden[k][0], "nar", n_nar, far))

    def gather_hidden(k):
        for b in reversed(range(nar_bits - 1)):
            hidden[k] = hidden[k] + [flip(g, "nar", n_nar, 1 << b) for g in hidden[k]]

    keep, send, hidden = [None] * n, [None] * n, [None] * n
    parts, todo = [None] * n, [0] * n

    def scatter(k, to):
        while todo[k] > to:
            total = add(parts[k][0], flip(parts[k][1], "wide", n_wide, 1 << (wide_bits - todo[k])))
            todo[k] -= 1
            half = total.shape[0] // 2
            parts[k] = (total[:half], total[half:]) if todo[k] else (total,)

    def products(k, *others):
        keep[k], send[k] = gate_up(wide, [after(tok[k][0], *others), *tok[k][1:]], gate, up, n_nar)

    def finish(k, weights, *others):
        hidden[k][0] = after(hidden[k][0], *others)
        parts[k], todo[k] = down(wide, hidden[k], weights, n_wide), wide_bits

    if not fast or n != 4 or wide_bits < 2:
        gate, up, down_w = [decode(gw, gs)], [decode(uw, us)], [decode(dw, ds)]
        for k in range(n):
            gather_tokens(k, 0)
            products(k)
            sum_core(k)
            gated(k)
            gather_hidden(k)
            finish(k, down_w)
            scatter(k, 0)
    else:
        gate = [decode_part(after(gw, dealt[0]), gs, 0, 2)]
        for k in range(4):
            gather_tokens(k, wide_bits - 1, gate[0])
        gate.append(decode_part(after(gw, gate[0], tok[0][0]), gs, 1, 2))
        for k in (0, 1):
            gather_tokens(k, 1, gate[1])
        up = [decode_part(after(uw, tok[0][0], tok[1][0]), us, 0, 1)]
        for k in (2, 3):
            gather_tokens(k, 1, up[0])
        gather_tokens(0, 0, up[0])
        products(0)
        gather_tokens(1, 0, send[0])
        send[0] = after(send[0], tok[1][1], tok[2][0], tok[3][0])
        gather_tokens(2, 0)
        gather_tokens(3, 0)
        sum_core(0)
        down_w = []
        for k in range(3):
            products(k + 1, send[k], *(hidden[k - 1][:2] if k > 0 else []))
            if k < 2:
                down_w.append(decode_part(after(dw, send[k + 1]), ds, k, 2))
                tok[k + 2][1] = after(tok[k + 2][1], send[k + 1])
                send[k + 1] = after(send[k + 1], tok[k + 2][1], down_w[k])
            else:
                finish(0, down_w, send[3])
                send[3] = after(send[3], parts[0][1])
            gated(k, send[k + 1])
            sum_core(k + 1, hidden[k][0])
            gather_hidden(k)
        scatter(0, wide_bits - 1)
        finish(1, down_w, send[3], *parts[0])
        scatter(0, wide_bits - 2)
        scatter(1, wide_bits - 1)
        finish(2, down_w, *parts[0], *parts[1])
        gated(3, parts[2][1])
        scatter(0, max(wide_bits - 3, 0))
        scatter(1, wide_bits - 2)
        scatter(2, wide_bits - 1)
        gather_hidden(3)
        finish(3, down_w, *parts[0], *parts[1], *parts[2])
        for k in range(4):
            scatter(k, 0)
    outs = [part[0].reshape(n_nar, -1, width) for part in parts]
    return collect(nar, outs, edges).reshape(rows, width)


def solution(mesh):
    n_wide, n_nar = mesh.shape["wide"], mesh.shape["nar"]

    def local(tokens, *weights):
        rows = tokens.shape[0]
        cuts = (128,) * (rows // 128) if 128 // n_nar >= 16 else (rows,)
        return on_device(n_wide, n_nar, cuts, tokens, *weights)

    in_specs = (
        P("grp", ("nar", "wide")),
        P("nar", "wide"),
        P("nar", "wide"),
        P("nar", "wide"),
        P("nar", "wide"),
        P("wide", "nar"),
        P("wide", "nar"),
    )
    return jax.shard_map(
        local, mesh=mesh, in_specs=in_specs, out_specs=P("grp", ("nar", "wide")), check_vma=False
    )
```

time: 278 us -> 153 us (0.55)
  waiting for transfers between devices: 195 us -> 37.8 us
  Pallas kernels: 0 us -> 59.8 us
  starting transfers between devices: 0.35 us -> 51.7 us
  matrix products: 35.4 us -> 0 us
  other arithmetic: 33.6 us -> 0.63 us
  between operations: 13.2 us -> 0.6 us
    reduce_scatter x3 -> x0, waiting for transfers between devices: 131 us -> none  [the longest x1 68.5 us: on_device(): lax.psum_scatter(down_terms.astype(jnp.bfloat16), 'wide', scatter_dimensi...]
    all_gather x2 -> x0, waiting for transfers between devices: 63.7 us -> none  [the longest x1 45.1 us: on_device(): segment = lax.all_gather(tokens, 'wide', axis=1, tiled=True)]
    pallas_call x0 -> x23, Pallas kernels: none -> 59.8 us  [the longest x4 24.7 us: gate_up(): pl.pallas_call(functools.partial(gate_up_kernel, len(shards), len(gate),...]
    ppermute x0 -> x56, starting transfers between devices: none -> 51.7 us  [flip(): return lax.ppermute(array, axis, [(i, i ^ mask) for i in range(size)])]
    ppermute x0 -> x56, waiting for transfers between devices: none -> 37.8 us  [flip(): return lax.ppermute(array, axis, [(i, i ^ mask) for i in range(size)])]
    dot_general x3 -> x0, matrix products: 35.4 us -> none  [the longest x1 14 us: on_device(): gate_part = jnp.dot(segment, gate_deq, preferred_element_type=jnp.float32)]
    convert_element_type x4 -> x12, other arithmetic: 33.6 us -> 0.47 us  [add(): return (a.astype(jnp.float32) + b.astype(jnp.float32)).astype(jnp.bfloat16)]
  transfers between devices with their start and end apart: 5 -> 56, of which waited for: 5 -> 22; matrix products, arithmetic and copies ran while one was open for 14% -> 1% of each run, Pallas kernels for 0% -> 39%
where the time goes in v1:
time: 153 us
  Pallas kernels  59.8 us (39%)
  starting transfers between devices  51.7 us (34%)
  waiting for transfers between devices  37.8 us (25%)
  local copies, waits for them, and re-layouts  2.25 us (1%)
    ppermute x56, starting transfers between devices, flip(): return lax.ppermute(array, axis, [(i, i ^ mask) for i in range(size)])  51.7 us
    ppermute x56, waiting for transfers between devices, flip(): return lax.ppermute(array, axis, [(i, i ^ mask) for i in range(size)])  37.8 us
    pallas_call x4, Pallas kernels, gate_up(): pl.pallas_call(functools.partial(gate_up_kernel, len(shards), len(gate),...  24.7 us
    pallas_call x5, Pallas kernels, decode_part(): pl.pallas_call(functools.partial(decode_kernel, part * size, block), in_s...  17.8 us
    pallas_call x4, Pallas kernels, down(): pl.pallas_call(functools.partial(down_kernel, len(hidden), len(weights)),...  14 us
  transfers between devices with their start and end apart: 56, of which 22 were waited for; matrix products, arithmetic and copies ran while one was open for 1% of the time, Pallas kernels for 39%

profile of v1, /device:TPU:0, one launch (start us, length us, event | category | flops | bytes accessed | tf_op | source)
XLA Modules:
  0.0 152.7 jit_solution(18296568380782778082)
XLA Ops:
  0.0 1.0 copy-done.4
  1.0 4.1 %collective-permute-start = (bf16[1,128,256]{2,1,0:T(8,128)(2,1)S(1)}, bf16[1,128,256]{2,1,0:T(8,128)(2,1)S(1)}, u32[]{:S(2)}, u32[]{:S(2)}) collective-permute-start(bf16[1,128,256]{2,1,0:T(8,128)(2,1)S(1)} %bitcast.51), channel_id=1, source_target_pairs={{0,16},{4,20},{8,24},{12,28},{16,0},{20,4},{24,8},{28,12},{1,17},{... | collective-permute-start | bytes 196616 | tf_op jit(solution)/shard_map/ppermute | solution.py:26
  5.2 2.8 %collective-permute-start.8 = (bf16[1,128,256]{2,1,0:T(8,128)(2,1)S(1)}, bf16[1,128,256]{2,1,0:T(8,128)(2,1)S(1)}, u32[]{:S(2)}, u32[]{:S(2)}) collective-permute-start(bf16[1,128,256]{2,1,0:T(8,128)(2,1)S(1)} %bitcast.57), channel_id=1, source_target_pairs={{0,16},{4,20},{8,24},{12,28},{16,0},{20,4},{24,8},{28,12},{1,17},{... | collective-permute-start | bytes 196616 | tf_op jit(solution)/shard_map/ppermute | solution.py:26
  8.1 0.9 copy-done.2
  9.1 3.2 %decode.5.refs_2_ = bf16[1024,3328]{1,0:T(8,128)(2,1)S(1)} custom-call(bf16[2048,3328]{1,0:T(8,128)(2,1)} %w_ref.1, f32[16,3328]{1,0:T(8,128)S(1)} %copy-done.2), custom_call_target="tpu_custom_call" | custom-call | flops 1024 | bytes 1024 | tf_op jit(solution)/shard_map/decode/pallas_call | solution.py:74
  12.3 1.9 %collective-permute-start.1 = (bf16[2,128,256]{2,1,0:T(8,128)(2,1)S(1)}, bf16[2,128,256]{2,1,0:T(8,128)(2,1)S(1)}, u32[]{:S(2)}, u32[]{:S(2)}) collective-permute-start(bf16[2,128,256]{2,1,0:T(8,128)(2,1)S(1)} %pad_maximum_fusion.4), channel_id=1, source_target_pairs={{0,8},{4,12},{8,0},{12,4},{16,24},{20,28},{24,16},{28,20},{1,9},{5... | collective-permute-start | bytes 393224 | tf_op jit(solution)/shard_map/ppermute | solution.py:26
  15.1 1.3 collective-permute-done.8
  16.5 3.2 %decode.6.refs_3_ = bf16[1024,3328]{1,0:T(8,128)(2,1)S(1)} custom-call(bf16[2048,3328]{1,0:T(8,128)(2,1)} %w_ref.1, f32[16,3328]{1,0:T(8,128)S(1)} %copy-done.3), custom_call_target="tpu_custom_call" | custom-call | flops 1024 | bytes 1024 | tf_op jit(solution)/shard_map/decode/pallas_call | solution.py:74
  20.4 1.4 collective-permute-start.7
  21.8 1.1 collective-permute-done.4
  23.0 1.8 %collective-permute-start.2 = (bf16[4,128,256]{2,1,0:T(8,128)(2,1)S(1)}, bf16[4,128,256]{2,1,0:T(8,128)(2,1)S(1)}, u32[]{:S(2)}, u32[]{:S(2)}) collective-permute-start(bf16[4,128,256]{2,1,0:T(8,128)(2,1)S(1)} %get-tuple-element.149.refs_0_), channel_id=1, source_target_pairs={{0,4},{4,0},{8,12},{12,8},{16,20},{20,16},{24,28},{28,24},{1,5},{5... | collective-permute-start | bytes 786440 | tf_op jit(solution)/shard_map/ppermute | solution.py:26
  25.1 5.1 %decode.7.refs_4_ = bf16[2048,3328]{1,0:T(8,128)(2,1)S(1)} custom-call(bf16[2048,3328]{1,0:T(8,128)(2,1)} %w_ref.2, f32[16,3328]{1,0:T(8,128)S(1)} %copy-done.5), custom_call_target="tpu_custom_call" | custom-call | flops 1024 | bytes 1024 | tf_op jit(solution)/shard_map/decode/pallas_call | solution.py:74
  30.3 1.8 %collective-permute-start.15 = (bf16[4,128,256]{2,1,0:T(8,128)(2,1)S(1)}, bf16[4,128,256]{2,1,0:T(8,128)(2,1)S(1)}, u32[]{:S(2)}, u32[]{:S(2)}) collective-permute-start(bf16[4,128,256]{2,1,0:T(8,128)(2,1)S(1)} %pad_maximum_fusion.2.refs_0_), channel_id=1, source_target_pairs={{0,4},{4,0},{8,12},{12,8},{16,20},{20,16},{24,28},{28,24},{1,5},{5... | collective-permute-start | bytes 786440 | tf_op jit(solution)/shard_map/ppermute | solution.py:26
  32.2 6.3 %gate_up.4 = (bf16[2,2,32,3328]{3,2,1,0:T(8,128)(2,1)S(1)}, bf16[2,2,32,3328]{3,2,1,0:T(8,128)(2,1)S(1)}) custom-call(s32[1]{0:T(128)} %bitcast.1.place_ref, bf16[4,128,256]{2,1,0:T(8,128)(2,1)S(1)} %get-tuple-element.149.refs_0_, bf16[4,128,256]{2,1,0:T(8,128)(2,1)S(1)} %collective-permute-done.2.refs_1_, bf16[1024,3328]{1,0:T(8,128)(2,1)S(1)} %decode.5.refs_2_, ...), custom_call_target="tpu_custom_call" | custom-call | flops 1024 | bytes 1024 | tf_op jit(solution)/shard_map/gate_up/pallas_call | solution.py:137
  41.3 1.8 %collective-permute-start.14 = (bf16[1,2,32,3328]{3,2,1,0:T(8,128)(2,1)S(1)}, bf16[1,2,32,3328]{3,2,1,0:T(8,128)(2,1)S(1)}, u32[]{:S(2)}, u32[]{:S(2)}) collective-permute-start(bf16[1,2,32,3328]{3,2,1,0:T(8,128)(2,1)S(1)} %get-tuple-element.91), channel_id=1, source_target_pairs={{0,2},{1,3},{2,0},{3,1},{4,6},{5,7},{6,4},{7,5},{8,10},{9,11},{10,... | collective-permute-start | bytes 1277960 | tf_op jit(solution)/shard_map/ppermute | solution.py:26
  43.1 6.1 %gate_up.5 = (bf16[2,2,32,3328]{3,2,1,0:T(8,128)(2,1)S(1)}, bf16[2,2,32,3328]{3,2,1,0:T(8,128)(2,1)S(1)}) custom-call(s32[1]{0:T(128)} %bitcast.1.place_ref, bf16[4,128,256]{2,1,0:T(8,128)(2,1)S(1)} %get-tuple-element.92.refs_0_, bf16[4,128,256]{2,1,0:T(8,128)(2,1)S(1)} %collective-permute-done.5.refs_1_, bf16[1024,3328]{1,0:T(8,128)(2,1)S(1)} %decode.5.refs_2_, ...), custom_call_target="tpu_custom_call" | custom-call | flops 1024 | bytes 1024 | tf_op jit(solution)/shard_map/gate_up/pallas_call | solution.py:137
  49.2 3.1 %decode.8.refs_4_ = bf16[1664,2048]{1,0:T(8,128)(2,1)S(1)} custom-call(bf16[3328,2048]{1,0:T(8,128)(2,1)} %w_ref.4, f32[26,2048]{1,0:T(8,128)S(1)} %copy-done.1), custom_call_target="tpu_custom_call" | custom-call | flops 1024 | bytes 1024 | tf_op jit(solution)/shard_map/decode/pallas_call | solution.py:74
  52.5 1.6 %collective-permute-start.21 = (bf16[4,128,256]{2,1,0:T(8,128)(2,1)S(1)}, bf16[4,128,256]{2,1,0:T(8,128)(2,1)S(1)}, u32[]{:S(2)}, u32[]{:S(2)}) collective-permute-start(bf16[4,128,256]{2,1,0:T(8,128)(2,1)S(1)} %pad_maximum_fusion.3.refs_0_), channel_id=1, source_target_pairs={{0,4},{4,0},{8,12},{12,8},{16,20},{20,16},{24,28},{28,24},{1,5},{5... | collective-permute-start | bytes 786440 | tf_op jit(solution)/shard_map/ppermute | solution.py:26
  56.4 1.2 collective-permute-start.23
  57.6 5.7 %collective-permute-done.20.refs_1_ = bf16[32,3328]{1,0:T(8,128)(2,1)S(1)} collective-permute-done((bf16[32,3328]{1,0:T(8,128)(2,1)S(1)}, bf16[32,3328]{1,0:T(8,128)(2,1)S(1)}, u32[]{:S(2)}, u32[]{:S(2)}) %collective-permute-start.20) | collective-permute-done | bytes 213024 | tf_op jit(solution)/shard_map/ppermute | solution.py:26
  63.3 6.1 %gate_up.6 = (bf16[2,2,32,3328]{3,2,1,0:T(8,128)(2,1)S(1)}, bf16[2,2,32,3328]{3,2,1,0:T(8,128)(2,1)S(1)}) custom-call(s32[1]{0:T(128)} %bitcast.1.place_ref, bf16[4,128,256]{2,1,0:T(8,128)(2,1)S(1)} %pad_maximum_fusion.2.refs_0_, bf16[4,128,256]{2,1,0:T(8,128)(2,1)S(1)} %collective-permute-done.15.refs_1_, bf16[1024,3328]{1,0:T(8,128)(2,1)S(1)} %decode.5.refs_2_, ...), custom_call_target="tpu_custom_call" | custom-call | flops 1024 | bytes 1024 | tf_op jit(solution)/shard_map/gate_up/pallas_call | solution.py:137
  69.4 3.2 %decode.9.refs_5_ = bf16[1664,2048]{1,0:T(8,128)(2,1)S(1)} custom-call(bf16[3328,2048]{1,0:T(8,128)(2,1)} %w_ref.4, f32[26,2048]{1,0:T(8,128)S(1)} %copy-done.1), custom_call_target="tpu_custom_call" | custom-call | flops 1024 | bytes 1024 | tf_op jit(solution)/shard_map/decode/pallas_call | solution.py:74
  75.6 1.6 %collective-permute-start.34 = (bf16[1,2,32,3328]{3,2,1,0:T(8,128)(2,1)S(1)}, bf16[1,2,32,3328]{3,2,1,0:T(8,128)(2,1)S(1)}, u32[]{:S(2)}, u32[]{:S(2)}) collective-permute-start(bf16[1,2,32,3328]{3,2,1,0:T(8,128)(2,1)S(1)} %get-tuple-element.110), channel_id=1, source_target_pairs={{0,2},{1,3},{2,0},{3,1},{4,6},{5,7},{6,4},{7,5},{8,10},{9,11},{10,... | collective-permute-start | bytes 1277960 | tf_op jit(solution)/shard_map/ppermute | solution.py:26
  77.2 5.2 %collective-permute-done.27.refs_1_ = bf16[32,3328]{1,0:T(8,128)(2,1)S(1)} collective-permute-done((bf16[32,3328]{1,0:T(8,128)(2,1)S(1)}, bf16[32,3328]{1,0:T(8,128)(2,1)S(1)}, u32[]{:S(2)}, u32[]{:S(2)}) %collective-permute-start.27) | collective-permute-done | bytes 213024 | tf_op jit(solution)/shard_map/ppermute | solution.py:26
  82.4 6.1 %gate_up.7 = (bf16[2,2,32,3328]{3,2,1,0:T(8,128)(2,1)S(1)}, bf16[2,2,32,3328]{3,2,1,0:T(8,128)(2,1)S(1)}) custom-call(s32[1]{0:T(128)} %bitcast.1.place_ref, bf16[4,128,256]{2,1,0:T(8,128)(2,1)S(1)} %pad_maximum_fusion.3.refs_0_, bf16[4,128,256]{2,1,0:T(8,128)(2,1)S(1)} %collective-permute-done.21.refs_1_, bf16[1024,3328]{1,0:T(8,128)(2,1)S(1)} %decode.5.refs_2_, ...), custom_call_target="tpu_custom_call" | custom-call | flops 1024 | bytes 1024 | tf_op jit(solution)/shard_map/gate_up/pallas_call | solution.py:137
  88.6 3.5 %down.4 = (bf16[4,128,256]{2,1,0:T(8,128)(2,1)S(1)}, bf16[4,128,256]{2,1,0:T(8,128)(2,1)S(1)}) custom-call(s32[1]{0:T(128)} %bitcast.1.place_ref, bf16[32,3328]{1,0:T(8,128)(2,1)S(1)} %gated.4.refs_0_, bf16[32,3328]{1,0:T(8,128)(2,1)S(1)} %collective-permute-done.20.refs_1_, bf16[32,3328]{1,0:T(8,128)(2,1)S(1)} %collective-permute-done.28.refs_2_, ...), custom_call_target="tpu_custom_call" | custom-call | flops 1024 | bytes 1024 | tf_op jit(solution)/shard_map/down/pallas_call | solution.py:185
  94.4 4.3 %collective-permute-done.30 = bf16[4,128,256]{2,1,0:T(8,128)(2,1)S(1)} collective-permute-done((bf16[4,128,256]{2,1,0:T(8,128)(2,1)S(1)}, bf16[4,128,256]{2,1,0:T(8,128)(2,1)S(1)}, u32[]{:S(2)}, u32[]{:S(2)}) %collective-permute-start.30) | collective-permute-done | bytes 262176 | tf_op jit(solution)/shard_map/ppermute | solution.py:26
  100.2 3.5 %down.5 = (bf16[4,128,256]{2,1,0:T(8,128)(2,1)S(1)}, bf16[4,128,256]{2,1,0:T(8,128)(2,1)S(1)}) custom-call(s32[1]{0:T(128)} %bitcast.1.place_ref, bf16[32,3328]{1,0:T(8,128)(2,1)S(1)} %gated.5.refs_0_, bf16[32,3328]{1,0:T(8,128)(2,1)S(1)} %collective-permute-done.27.refs_1_, bf16[32,3328]{1,0:T(8,128)(2,1)S(1)} %collective-permute-done.38.refs_2_, ...), custom_call_target="tpu_custom_call" | custom-call | flops 1024 | bytes 1024 | tf_op jit(solution)/shard_map/down/pallas_call | solution.py:185
  104.3 1.2 collective-permute-start.43
  106.4 3.2 %collective-permute-start.32 = (bf16[1,128,256]{2,1,0:T(8,128)(2,1)S(1)}, bf16[1,128,256]{2,1,0:T(8,128)(2,1)S(1)}, u32[]{:S(2)}, u32[]{:S(2)}) collective-permute-start(bf16[1,128,256]{2,1,0:T(8,128)(2,1)S(1)} %slice.131), channel_id=1, source_target_pairs={{0,16},{4,20},{8,24},{12,28},{16,0},{20,4},{24,8},{28,12},{1,17},{... | collective-permute-start | bytes 196616 | tf_op jit(solution)/shard_map/ppermute | solution.py:26
  109.6 2.9 %collective-permute-done.43.refs_1_ = bf16[32,3328]{1,0:T(8,128)(2,1)S(1)} collective-permute-done((bf16[32,3328]{1,0:T(8,128)(2,1)S(1)}, bf16[32,3328]{1,0:T(8,128)(2,1)S(1)}, u32[]{:S(2)}, u32[]{:S(2)}) %collective-permute-start.43) | collective-permute-done | bytes 213024 | tf_op jit(solution)/shard_map/ppermute | solution.py:26
  112.5 1.5 collective-permute-start.41
  114.0 3.5 %down.6 = (bf16[4,128,256]{2,1,0:T(8,128)(2,1)S(1)}, bf16[4,128,256]{2,1,0:T(8,128)(2,1)S(1)}) custom-call(s32[1]{0:T(128)} %bitcast.1.place_ref, bf16[32,3328]{1,0:T(8,128)(2,1)S(1)} %gated.6.refs_0_, bf16[32,3328]{1,0:T(8,128)(2,1)S(1)} %collective-permute-done.43.refs_1_, bf16[32,3328]{1,0:T(8,128)(2,1)S(1)} %collective-permute-done.44.refs_2_, ...), custom_call_target="tpu_custom_call" | custom-call | flops 1024 | bytes 1024 | tf_op jit(solution)/shard_map/down/pallas_call | solution.py:185
  117.5 1.5 %collective-permute-start.46 = (bf16[4,128,256]{2,1,0:T(8,128)(2,1)S(1)}, bf16[4,128,256]{2,1,0:T(8,128)(2,1)S(1)}, u32[]{:S(2)}, u32[]{:S(2)}) collective-permute-start(bf16[4,128,256]{2,1,0:T(8,128)(2,1)S(1)} %get-tuple-element.127), channel_id=1, source_target_pairs={{0,4},{4,0},{8,12},{12,8},{16,20},{20,16},{24,28},{28,24},{1,5},{5... | collective-permute-start | bytes 786440 | tf_op jit(solution)/shard_map/ppermute | solution.py:26
  119.1 1.3 collective-permute-done.49.b_ref
  120.8 1.3 collective-permute-start.50
  122.2 3.3 %collective-permute-start.42 = (bf16[1,128,256]{2,1,0:T(8,128)(2,1)S(1)}, bf16[1,128,256]{2,1,0:T(8,128)(2,1)S(1)}, u32[]{:S(2)}, u32[]{:S(2)}) collective-permute-start(bf16[1,128,256]{2,1,0:T(8,128)(2,1)S(1)} %slice.135), channel_id=1, source_target_pairs={{0,16},{4,20},{8,24},{12,28},{16,0},{20,4},{24,8},{28,12},{1,17},{... | collective-permute-start | bytes 196616 | tf_op jit(solution)/shard_map/ppermute | solution.py:26
  125.5 1.5 %collective-permute-done.50.refs_1_ = bf16[32,3328]{1,0:T(8,128)(2,1)S(1)} collective-permute-done((bf16[32,3328]{1,0:T(8,128)(2,1)S(1)}, bf16[32,3328]{1,0:T(8,128)(2,1)S(1)}, u32[]{:S(2)}, u32[]{:S(2)}) %collective-permute-start.50) | collective-permute-done | bytes 213024 | tf_op jit(solution)/shard_map/ppermute | solution.py:26
  127.1 1.4 collective-permute-done.52.refs_3_
  128.5 3.5 %down.7 = (bf16[4,128,256]{2,1,0:T(8,128)(2,1)S(1)}, bf16[4,128,256]{2,1,0:T(8,128)(2,1)S(1)}) custom-call(s32[1]{0:T(128)} %bitcast.1.place_ref, bf16[32,3328]{1,0:T(8,128)(2,1)S(1)} %gated.7.refs_0_, bf16[32,3328]{1,0:T(8,128)(2,1)S(1)} %collective-permute-done.50.refs_1_, bf16[32,3328]{1,0:T(8,128)(2,1)S(1)} %collective-permute-done.51.refs_2_, ...), custom_call_target="tpu_custom_call" | custom-call | flops 1024 | bytes 1024 | tf_op jit(solution)/shard_map/down/pallas_call | solution.py:185
  132.0 1.5 %collective-permute-start.53 = (bf16[4,128,256]{2,1,0:T(8,128)(2,1)S(1)}, bf16[4,128,256]{2,1,0:T(8,128)(2,1)S(1)}, u32[]{:S(2)}, u32[]{:S(2)}) collective-permute-start(bf16[4,128,256]{2,1,0:T(8,128)(2,1)S(1)} %get-tuple-element.132), channel_id=1, source_target_pairs={{0,4},{4,0},{8,12},{12,8},{16,20},{20,16},{24,28},{28,24},{1,5},{5... | collective-permute-start | bytes 786440 | tf_op jit(solution)/shard_map/ppermute | solution.py:26
  133.6 1.7 %collective-permute-start.47 = (bf16[2,128,256]{2,1,0:T(8,128)(2,1)S(1)}, bf16[2,128,256]{2,1,0:T(8,128)(2,1)S(1)}, u32[]{:S(2)}, u32[]{:S(2)}) collective-permute-start(bf16[2,128,256]{2,1,0:T(8,128)(2,1)S(1)} %slice.137), channel_id=1, source_target_pairs={{0,8},{4,12},{8,0},{12,4},{16,24},{20,28},{24,16},{28,20},{1,9},{5... | collective-permute-start | bytes 393224 | tf_op jit(solution)/shard_map/ppermute | solution.py:26
  135.3 5.1 %collective-permute-done.53 = bf16[4,128,256]{2,1,0:T(8,128)(2,1)S(1)} collective-permute-done((bf16[4,128,256]{2,1,0:T(8,128)(2,1)S(1)}, bf16[4,128,256]{2,1,0:T(8,128)(2,1)S(1)}, u32[]{:S(2)}, u32[]{:S(2)}) %collective-permute-start.53) | collective-permute-done | bytes 262176 | tf_op jit(solution)/shard_map/ppermute | solution.py:26
  140.5 1.7 %collective-permute-start.54 = (bf16[2,128,256]{2,1,0:T(8,128)(2,1)S(1)}, bf16[2,128,256]{2,1,0:T(8,128)(2,1)S(1)}, u32[]{:S(2)}, u32[]{:S(2)}) collective-permute-start(bf16[2,128,256]{2,1,0:T(8,128)(2,1)S(1)} %slice.141), channel_id=1, source_target_pairs={{0,8},{4,12},{8,0},{12,4},{16,24},{20,28},{24,16},{28,20},{1,9},{5... | collective-permute-start | bytes 393224 | tf_op jit(solution)/shard_map/ppermute | solution.py:26
  142.3 2.1 %collective-permute-start.48 = (bf16[1,128,256]{2,1,0:T(8,128)(2,1)S(1)}, bf16[1,128,256]{2,1,0:T(8,128)(2,1)S(1)}, u32[]{:S(2)}, u32[]{:S(2)}) collective-permute-start(bf16[1,128,256]{2,1,0:T(8,128)(2,1)S(1)} %slice.139), channel_id=1, source_target_pairs={{0,16},{4,20},{8,24},{12,28},{16,0},{20,4},{24,8},{28,12},{1,17},{... | collective-permute-start | bytes 196616 | tf_op jit(solution)/shard_map/ppermute | solution.py:26
  144.4 1.8 %collective-permute-done.54 = bf16[2,128,256]{2,1,0:T(8,128)(2,1)S(1)} collective-permute-done((bf16[2,128,256]{2,1,0:T(8,128)(2,1)S(1)}, bf16[2,128,256]{2,1,0:T(8,128)(2,1)S(1)}, u32[]{:S(2)}, u32[]{:S(2)}) %collective-permute-start.54) | collective-permute-done | bytes 131104 | tf_op jit(solution)/shard_map/ppermute | solution.py:26
  146.3 3.4 %collective-permute-start.55 = (bf16[1,128,256]{2,1,0:T(8,128)(2,1)S(1)}, bf16[1,128,256]{2,1,0:T(8,128)(2,1)S(1)}, u32[]{:S(2)}, u32[]{:S(2)}) collective-permute-start(bf16[1,128,256]{2,1,0:T(8,128)(2,1)S(1)} %slice.143), channel_id=1, source_target_pairs={{0,16},{4,20},{8,24},{12,28},{16,0},{20,4},{24,8},{28,12},{1,17},{... | collective-permute-start | bytes 196616 | tf_op jit(solution)/shard_map/ppermute | solution.py:26
  149.7 2.2 %collective-permute-done.55 = bf16[1,128,256]{2,1,0:T(8,128)(2,1)S(1)} collective-permute-done((bf16[1,128,256]{2,1,0:T(8,128)(2,1)S(1)}, bf16[1,128,256]{2,1,0:T(8,128)(2,1)S(1)}, u32[]{:S(2)}, u32[]{:S(2)}) %collective-permute-start.55) | collective-permute-done | bytes 65568 | tf_op jit(solution)/shard_map/ppermute | solution.py:26
  (135 shorter events, 17.3 us)
Async XLA Ops:
  1.0 11.2 %collective-permute-start = (bf16[1,128,256]{2,1,0:T(8,128)(2,1)S(1)}, bf16[1,128,256]{2,1,0:T(8,128)(2,1)S(1)}, u32[]{:S(2)}, u32[]{:S(2)}) collective-permute-start(bf16[1,128,256]{2,1,0:T(8,128)(2,1)S(1)} %bitcast.51), channel_id=1, source_target_pairs={{0,16},{4,20},{8,24},{12,28},{16,0},{20,4},{24,8},{28,12},{1,17},{... | collective-permute-start | bytes 196616 | tf_op jit(solution)/shard_map/ppermute | solution.py:26
  5.1 9.9 %collective-permute-start.3 = (bf16[1,128,256]{2,1,0:T(8,128)(2,1)S(1)}, bf16[1,128,256]{2,1,0:T(8,128)(2,1)S(1)}, u32[]{:S(2)}, u32[]{:S(2)}) collective-permute-start(bf16[1,128,256]{2,1,0:T(8,128)(2,1)S(1)} %bitcast.54), channel_id=1, source_target_pairs={{0,16},{4,20},{8,24},{12,28},{16,0},{20,4},{24,8},{28,12},{1,17},{... | collective-permute-start | bytes 196616 | tf_op jit(solution)/shard_map/ppermute | solution.py:26
  5.2 11.3 %collective-permute-start.8 = (bf16[1,128,256]{2,1,0:T(8,128)(2,1)S(1)}, bf16[1,128,256]{2,1,0:T(8,128)(2,1)S(1)}, u32[]{:S(2)}, u32[]{:S(2)}) collective-permute-start(bf16[1,128,256]{2,1,0:T(8,128)(2,1)S(1)} %bitcast.57), channel_id=1, source_target_pairs={{0,16},{4,20},{8,24},{12,28},{16,0},{20,4},{24,8},{28,12},{1,17},{... | collective-permute-start | bytes 196616 | tf_op jit(solution)/shard_map/ppermute | solution.py:26
  8.0 12.3 %collective-permute-start.6 = (bf16[1,128,256]{2,1,0:T(8,128)(2,1)S(1)}, bf16[1,128,256]{2,1,0:T(8,128)(2,1)S(1)}, u32[]{:S(2)}, u32[]{:S(2)}) collective-permute-start(bf16[1,128,256]{2,1,0:T(8,128)(2,1)S(1)} %bitcast.60), channel_id=1, source_target_pairs={{0,16},{4,20},{8,24},{12,28},{16,0},{20,4},{24,8},{28,12},{1,17},{... | collective-permute-start | bytes 196616 | tf_op jit(solution)/shard_map/ppermute | solution.py:26
  12.3 9.6 %collective-permute-start.1 = (bf16[2,128,256]{2,1,0:T(8,128)(2,1)S(1)}, bf16[2,128,256]{2,1,0:T(8,128)(2,1)S(1)}, u32[]{:S(2)}, u32[]{:S(2)}) collective-permute-start(bf16[2,128,256]{2,1,0:T(8,128)(2,1)S(1)} %pad_maximum_fusion.4), channel_id=1, source_target_pairs={{0,8},{4,12},{8,0},{12,4},{16,24},{20,28},{24,16},{28,20},{1,9},{5... | collective-permute-start | bytes 393224 | tf_op jit(solution)/shard_map/ppermute | solution.py:26
  15.0 7.9 %collective-permute-start.4 = (bf16[2,128,256]{2,1,0:T(8,128)(2,1)S(1)}, bf16[2,128,256]{2,1,0:T(8,128)(2,1)S(1)}, u32[]{:S(2)}, u32[]{:S(2)}) collective-permute-start(bf16[2,128,256]{2,1,0:T(8,128)(2,1)S(1)} %pad_maximum_fusion.5), channel_id=1, source_target_pairs={{0,8},{4,12},{8,0},{12,4},{16,24},{20,28},{24,16},{28,20},{1,9},{5... | collective-permute-start | bytes 393224 | tf_op jit(solution)/shard_map/ppermute | solution.py:26
  19.7 10.5 %collective-permute-start.9 = (bf16[2,128,256]{2,1,0:T(8,128)(2,1)S(1)}, bf16[2,128,256]{2,1,0:T(8,128)(2,1)S(1)}, u32[]{:S(2)}, u32[]{:S(2)}) collective-permute-start(bf16[2,128,256]{2,1,0:T(8,128)(2,1)S(1)} %pad_maximum_fusion.7), channel_id=1, source_target_pairs={{0,8},{4,12},{8,0},{12,4},{16,24},{20,28},{24,16},{28,20},{1,9},{5... | collective-permute-start | bytes 393224 | tf_op jit(solution)/shard_map/ppermute | solution.py:26
  20.4 9.8 %collective-permute-start.7 = (bf16[2,128,256]{2,1,0:T(8,128)(2,1)S(1)}, bf16[2,128,256]{2,1,0:T(8,128)(2,1)S(1)}, u32[]{:S(2)}, u32[]{:S(2)}) collective-permute-start(bf16[2,128,256]{2,1,0:T(8,128)(2,1)S(1)} %pad_maximum_fusion.6), channel_id=1, source_target_pairs={{0,8},{4,12},{8,0},{12,4},{16,24},{20,28},{24,16},{28,20},{1,9},{5... | collective-permute-start | bytes 393224 | tf_op jit(solution)/shard_map/ppermute | solution.py:26
  23.0 9.2 %collective-permute-start.2 = (bf16[4,128,256]{2,1,0:T(8,128)(2,1)S(1)}, bf16[4,128,256]{2,1,0:T(8,128)(2,1)S(1)}, u32[]{:S(2)}, u32[]{:S(2)}) collective-permute-start(bf16[4,128,256]{2,1,0:T(8,128)(2,1)S(1)} %get-tuple-element.149.refs_0_), channel_id=1, source_target_pairs={{0,4},{4,0},{8,12},{12,8},{16,20},{20,16},{24,28},{28,24},{1,5},{5... | collective-permute-start | bytes 786440 | tf_op jit(solution)/shard_map/ppermute | solution.py:26
  24.8 13.8 %collective-permute-start.5 = (bf16[4,128,256]{2,1,0:T(8,128)(2,1)S(1)}, bf16[4,128,256]{2,1,0:T(8,128)(2,1)S(1)}, u32[]{:S(2)}, u32[]{:S(2)}) collective-permute-start(bf16[4,128,256]{2,1,0:T(8,128)(2,1)S(1)} %get-tuple-element.92.refs_0_), channel_id=1, source_target_pairs={{0,4},{4,0},{8,12},{12,8},{16,20},{20,16},{24,28},{28,24},{1,5},{5... | collective-permute-start | bytes 786440 | tf_op jit(solution)/shard_map/ppermute | solution.py:26
  30.3 18.9 %collective-permute-start.15 = (bf16[4,128,256]{2,1,0:T(8,128)(2,1)S(1)}, bf16[4,128,256]{2,1,0:T(8,128)(2,1)S(1)}, u32[]{:S(2)}, u32[]{:S(2)}) collective-permute-start(bf16[4,128,256]{2,1,0:T(8,128)(2,1)S(1)} %pad_maximum_fusion.2.refs_0_), channel_id=1, source_target_pairs={{0,4},{4,0},{8,12},{12,8},{16,20},{20,16},{24,28},{28,24},{1,5},{5... | collective-permute-start | bytes 786440 | tf_op jit(solution)/shard_map/ppermute | solution.py:26
  38.7 1.8 %collective-permute-start.11 = (bf16[32,3328]{1,0:T(8,128)(2,1)S(1)}, bf16[32,3328]{1,0:T(8,128)(2,1)S(1)}, u32[]{:S(2)}, u32[]{:S(2)}) collective-permute-start(bf16[32,3328]{1,0:T(8,128)(2,1)S(1)} %get-tuple-element.147), channel_id=1, source_target_pairs={{0,1},{1,0},{2,3},{3,2},{4,5},{5,4},{6,7},{7,6},{8,9},{9,8},{10,11... | collective-permute-start | bytes 638984 | tf_op jit(solution)/shard_map/ppermute | solution.py:26
  39.2 1.8 %collective-permute-start.13 = (bf16[32,3328]{1,0:T(8,128)(2,1)S(1)}, bf16[32,3328]{1,0:T(8,128)(2,1)S(1)}, u32[]{:S(2)}, u32[]{:S(2)}) collective-permute-start(bf16[32,3328]{1,0:T(8,128)(2,1)S(1)} %get-tuple-element.145), channel_id=1, source_target_pairs={{0,1},{1,0},{2,3},{3,2},{4,5},{5,4},{6,7},{7,6},{8,9},{9,8},{10,11... | collective-permute-start | bytes 638984 | tf_op jit(solution)/shard_map/ppermute | solution.py:26
  41.3 13.3 %collective-permute-start.14 = (bf16[1,2,32,3328]{3,2,1,0:T(8,128)(2,1)S(1)}, bf16[1,2,32,3328]{3,2,1,0:T(8,128)(2,1)S(1)}, u32[]{:S(2)}, u32[]{:S(2)}) collective-permute-start(bf16[1,2,32,3328]{3,2,1,0:T(8,128)(2,1)S(1)} %get-tuple-element.91), channel_id=1, source_target_pairs={{0,2},{1,3},{2,0},{3,1},{4,6},{5,7},{6,4},{7,5},{8,10},{9,11},{10,... | collective-permute-start | bytes 1277960 | tf_op jit(solution)/shard_map/ppermute | solution.py:26
  52.4 2.7 %collective-permute-start.16 = (bf16[32,3328]{1,0:T(8,128)(2,1)S(1)}, bf16[32,3328]{1,0:T(8,128)(2,1)S(1)}, u32[]{:S(2)}, u32[]{:S(2)}) collective-permute-start(bf16[32,3328]{1,0:T(8,128)(2,1)S(1)} %get-tuple-element.144), channel_id=1, source_target_pairs={{0,1},{1,0},{2,3},{3,2},{4,5},{5,4},{6,7},{7,6},{8,9},{9,8},{10,11... | collective-permute-start | bytes 638984 | tf_op jit(solution)/shard_map/ppermute | solution.py:26
  52.5 20.2 %collective-permute-start.21 = (bf16[4,128,256]{2,1,0:T(8,128)(2,1)S(1)}, bf16[4,128,256]{2,1,0:T(8,128)(2,1)S(1)}, u32[]{:S(2)}, u32[]{:S(2)}) collective-permute-start(bf16[4,128,256]{2,1,0:T(8,128)(2,1)S(1)} %pad_maximum_fusion.3.refs_0_), channel_id=1, source_target_pairs={{0,4},{4,0},{8,12},{12,8},{16,20},{20,16},{24,28},{28,24},{1,5},{5... | collective-permute-start | bytes 786440 | tf_op jit(solution)/shard_map/ppermute | solution.py:26
  54.1 1.7 %collective-permute-start.17 = (bf16[32,3328]{1,0:T(8,128)(2,1)S(1)}, bf16[32,3328]{1,0:T(8,128)(2,1)S(1)}, u32[]{:S(2)}, u32[]{:S(2)}) collective-permute-start(bf16[32,3328]{1,0:T(8,128)(2,1)S(1)} %get-tuple-element.143), channel_id=1, source_target_pairs={{0,1},{1,0},{2,3},{3,2},{4,5},{5,4},{6,7},{7,6},{8,9},{9,8},{10,11... | collective-permute-start | bytes 638984 | tf_op jit(solution)/shard_map/ppermute | solution.py:26
  55.1 8.1 %collective-permute-start.20 = (bf16[32,3328]{1,0:T(8,128)(2,1)S(1)}, bf16[32,3328]{1,0:T(8,128)(2,1)S(1)}, u32[]{:S(2)}, u32[]{:S(2)}) collective-permute-start(bf16[32,3328]{1,0:T(8,128)(2,1)S(1)} %gated.4.refs_0_), channel_id=1, source_target_pairs={{0,2},{1,3},{2,0},{3,1},{4,6},{5,7},{6,4},{7,5},{8,10},{9,11},{10,... | collective-permute-start | bytes 638984 | tf_op jit(solution)/shard_map/ppermute | solution.py:26
  56.4 17.4 %collective-permute-start.23 = (bf16[1,2,32,3328]{3,2,1,0:T(8,128)(2,1)S(1)}, bf16[1,2,32,3328]{3,2,1,0:T(8,128)(2,1)S(1)}, u32[]{:S(2)}, u32[]{:S(2)}) collective-permute-start(bf16[1,2,32,3328]{3,2,1,0:T(8,128)(2,1)S(1)} %get-tuple-element.100), channel_id=1, source_target_pairs={{0,2},{1,3},{2,0},{3,1},{4,6},{5,7},{6,4},{7,5},{8,10},{9,11},{10,... | collective-permute-start | bytes 1277960 | tf_op jit(solution)/shard_map/ppermute | solution.py:26
  72.7 2.1 %collective-permute-start.22 = (bf16[32,3328]{1,0:T(8,128)(2,1)S(1)}, bf16[32,3328]{1,0:T(8,128)(2,1)S(1)}, u32[]{:S(2)}, u32[]{:S(2)}) collective-permute-start(bf16[32,3328]{1,0:T(8,128)(2,1)S(1)} %get-tuple-element.140), channel_id=1, source_target_pairs={{0,1},{1,0},{2,3},{3,2},{4,5},{5,4},{6,7},{7,6},{8,9},{9,8},{10,11... | collective-permute-start | bytes 638984 | tf_op jit(solution)/shard_map/ppermute | solution.py:26
  72.8 2.0 %collective-permute-start.24 = (bf16[32,3328]{1,0:T(8,128)(2,1)S(1)}, bf16[32,3328]{1,0:T(8,128)(2,1)S(1)}, u32[]{:S(2)}, u32[]{:S(2)}) collective-permute-start(bf16[32,3328]{1,0:T(8,128)(2,1)S(1)} %get-tuple-element.139), channel_id=1, source_target_pairs={{0,1},{1,0},{2,3},{3,2},{4,5},{5,4},{6,7},{7,6},{8,9},{9,8},{10,11... | collective-permute-start | bytes 638984 | tf_op jit(solution)/shard_map/ppermute | solution.py:26
  73.3 2.0 %collective-permute-start.25 = (bf16[32,3328]{1,0:T(8,128)(2,1)S(1)}, bf16[32,3328]{1,0:T(8,128)(2,1)S(1)}, u32[]{:S(2)}, u32[]{:S(2)}) collective-permute-start(bf16[32,3328]{1,0:T(8,128)(2,1)S(1)} %get-tuple-element.138), channel_id=1, source_target_pairs={{0,1},{1,0},{2,3},{3,2},{4,5},{5,4},{6,7},{7,6},{8,9},{9,8},{10,11... | collective-permute-start | bytes 638984 | tf_op jit(solution)/shard_map/ppermute | solution.py:26
  73.4 1.9 %collective-permute-start.26 = (bf16[32,3328]{1,0:T(8,128)(2,1)S(1)}, bf16[32,3328]{1,0:T(8,128)(2,1)S(1)}, u32[]{:S(2)}, u32[]{:S(2)}) collective-permute-start(bf16[32,3328]{1,0:T(8,128)(2,1)S(1)} %get-tuple-element.137), channel_id=1, source_target_pairs={{0,1},{1,0},{2,3},{3,2},{4,5},{5,4},{6,7},{7,6},{8,9},{9,8},{10,11... | collective-permute-start | bytes 638984 | tf_op jit(solution)/shard_map/ppermute | solution.py:26
  74.2 8.2 %collective-permute-start.27 = (bf16[32,3328]{1,0:T(8,128)(2,1)S(1)}, bf16[32,3328]{1,0:T(8,128)(2,1)S(1)}, u32[]{:S(2)}, u32[]{:S(2)}) collective-permute-start(bf16[32,3328]{1,0:T(8,128)(2,1)S(1)} %gated.5.refs_0_), channel_id=1, source_target_pairs={{0,2},{1,3},{2,0},{3,1},{4,6},{5,7},{6,4},{7,5},{8,10},{9,11},{10,... | collective-permute-start | bytes 638984 | tf_op jit(solution)/shard_map/ppermute | solution.py:26
  74.8 13.7 %collective-permute-start.28 = (bf16[32,3328]{1,0:T(8,128)(2,1)S(1)}, bf16[32,3328]{1,0:T(8,128)(2,1)S(1)}, u32[]{:S(2)}, u32[]{:S(2)}) collective-permute-start(bf16[32,3328]{1,0:T(8,128)(2,1)S(1)} %gated.4.refs_0_), channel_id=1, source_target_pairs={{0,1},{1,0},{2,3},{3,2},{4,5},{5,4},{6,7},{7,6},{8,9},{9,8},{10,11... | collective-permute-start | bytes 638984 | tf_op jit(solution)/shard_map/ppermute | solution.py:26
  74.8 13.7 %collective-permute-start.29 = (bf16[32,3328]{1,0:T(8,128)(2,1)S(1)}, bf16[32,3328]{1,0:T(8,128)(2,1)S(1)}, u32[]{:S(2)}, u32[]{:S(2)}) collective-permute-start(bf16[32,3328]{1,0:T(8,128)(2,1)S(1)} %collective-permute-done.20.refs_1_), channel_id=1, source_target_pairs={{0,1},{1,0},{2,3},{3,2},{4,5},{5,4},{6,7},{7,6},{8,9},{9,8},{10,11... | collective-permute-start | bytes 638984 | tf_op jit(solution)/shard_map/ppermute | solution.py:26
  75.6 17.8 %collective-permute-start.34 = (bf16[1,2,32,3328]{3,2,1,0:T(8,128)(2,1)S(1)}, bf16[1,2,32,3328]{3,2,1,0:T(8,128)(2,1)S(1)}, u32[]{:S(2)}, u32[]{:S(2)}) collective-permute-start(bf16[1,2,32,3328]{3,2,1,0:T(8,128)(2,1)S(1)} %get-tuple-element.110), channel_id=1, source_target_pairs={{0,2},{1,3},{2,0},{3,1},{4,6},{5,7},{6,4},{7,5},{8,10},{9,11},{10,... | collective-permute-start | bytes 1277960 | tf_op jit(solution)/shard_map/ppermute | solution.py:26
  92.1 6.6 %collective-permute-start.30 = (bf16[4,128,256]{2,1,0:T(8,128)(2,1)S(1)}, bf16[4,128,256]{2,1,0:T(8,128)(2,1)S(1)}, u32[]{:S(2)}, u32[]{:S(2)}) collective-permute-start(bf16[4,128,256]{2,1,0:T(8,128)(2,1)S(1)} %get-tuple-element.115), channel_id=1, source_target_pairs={{0,4},{4,0},{8,12},{12,8},{16,20},{20,16},{24,28},{28,24},{1,5},{5... | collective-permute-start | bytes 786440 | tf_op jit(solution)/shard_map/ppermute | solution.py:26
  92.8 6.8 %collective-permute-start.38 = (bf16[32,3328]{1,0:T(8,128)(2,1)S(1)}, bf16[32,3328]{1,0:T(8,128)(2,1)S(1)}, u32[]{:S(2)}, u32[]{:S(2)}) collective-permute-start(bf16[32,3328]{1,0:T(8,128)(2,1)S(1)} %gated.5.refs_0_), channel_id=1, source_target_pairs={{0,1},{1,0},{2,3},{3,2},{4,5},{5,4},{6,7},{7,6},{8,9},{9,8},{10,11... | collective-permute-start | bytes 638984 | tf_op jit(solution)/shard_map/ppermute | solution.py:26
  93.3 5.5 %collective-permute-start.35 = (bf16[32,3328]{1,0:T(8,128)(2,1)S(1)}, bf16[32,3328]{1,0:T(8,128)(2,1)S(1)}, u32[]{:S(2)}, u32[]{:S(2)}) collective-permute-start(bf16[32,3328]{1,0:T(8,128)(2,1)S(1)} %get-tuple-element.135), channel_id=1, source_target_pairs={{0,1},{1,0},{2,3},{3,2},{4,5},{5,4},{6,7},{7,6},{8,9},{9,8},{10,11... | collective-permute-start | bytes 638984 | tf_op jit(solution)/shard_map/ppermute | solution.py:26
  93.4 5.9 %collective-permute-start.36 = (bf16[32,3328]{1,0:T(8,128)(2,1)S(1)}, bf16[32,3328]{1,0:T(8,128)(2,1)S(1)}, u32[]{:S(2)}, u32[]{:S(2)}) collective-permute-start(bf16[32,3328]{1,0:T(8,128)(2,1)S(1)} %get-tuple-element.134), channel_id=1, source_target_pairs={{0,1},{1,0},{2,3},{3,2},{4,5},{5,4},{6,7},{7,6},{8,9},{9,8},{10,11... | collective-permute-start | bytes 638984 | tf_op jit(solution)/shard_map/ppermute | solution.py:26
  94.3 5.0 %collective-permute-start.37 = (bf16[32,3328]{1,0:T(8,128)(2,1)S(1)}, bf16[32,3328]{1,0:T(8,128)(2,1)S(1)}, u32[]{:S(2)}, u32[]{:S(2)}) collective-permute-start(bf16[32,3328]{1,0:T(8,128)(2,1)S(1)} %get-tuple-element.133), channel_id=1, source_target_pairs={{0,1},{1,0},{2,3},{3,2},{4,5},{5,4},{6,7},{7,6},{8,9},{9,8},{10,11... | collective-permute-start | bytes 638984 | tf_op jit(solution)/shard_map/ppermute | solution.py:26
  98.8 7.5 %collective-permute-start.31 = (bf16[2,128,256]{2,1,0:T(8,128)(2,1)S(1)}, bf16[2,128,256]{2,1,0:T(8,128)(2,1)S(1)}, u32[]{:S(2)}, u32[]{:S(2)}) collective-permute-start(bf16[2,128,256]{2,1,0:T(8,128)(2,1)S(1)} %slice.129), channel_id=1, source_target_pairs={{0,8},{4,12},{8,0},{12,4},{16,24},{20,28},{24,16},{28,20},{1,9},{5... | collective-permute-start | bytes 393224 | tf_op jit(solution)/shard_map/ppermute | solution.py:26
  103.7 8.8 %collective-permute-start.40 = (bf16[4,128,256]{2,1,0:T(8,128)(2,1)S(1)}, bf16[4,128,256]{2,1,0:T(8,128)(2,1)S(1)}, u32[]{:S(2)}, u32[]{:S(2)}) collective-permute-start(bf16[4,128,256]{2,1,0:T(8,128)(2,1)S(1)} %get-tuple-element.124), channel_id=1, source_target_pairs={{0,4},{4,0},{8,12},{12,8},{16,20},{20,16},{24,28},{28,24},{1,5},{5... | collective-permute-start | bytes 786440 | tf_op jit(solution)/shard_map/ppermute | solution.py:26
  104.3 8.1 %collective-permute-start.43 = (bf16[32,3328]{1,0:T(8,128)(2,1)S(1)}, bf16[32,3328]{1,0:T(8,128)(2,1)S(1)}, u32[]{:S(2)}, u32[]{:S(2)}) collective-permute-start(bf16[32,3328]{1,0:T(8,128)(2,1)S(1)} %gated.6.refs_0_), channel_id=1, source_target_pairs={{0,2},{1,3},{2,0},{3,1},{4,6},{5,7},{6,4},{7,5},{8,10},{9,11},{10,... | collective-permute-start | bytes 638984 | tf_op jit(solution)/shard_map/ppermute | solution.py:26
  105.5 8.5 %collective-permute-start.44 = (bf16[32,3328]{1,0:T(8,128)(2,1)S(1)}, bf16[32,3328]{1,0:T(8,128)(2,1)S(1)}, u32[]{:S(2)}, u32[]{:S(2)}) collective-permute-start(bf16[32,3328]{1,0:T(8,128)(2,1)S(1)} %gated.6.refs_0_), channel_id=1, source_target_pairs={{0,1},{1,0},{2,3},{3,2},{4,5},{5,4},{6,7},{7,6},{8,9},{9,8},{10,11... | collective-permute-start | bytes 638984 | tf_op jit(solution)/shard_map/ppermute | solution.py:26
  105.5 14.9 %collective-permute-start.49 = (bf16[1,2,32,3328]{3,2,1,0:T(8,128)(2,1)S(1)}, bf16[1,2,32,3328]{3,2,1,0:T(8,128)(2,1)S(1)}, u32[]{:S(2)}, u32[]{:S(2)}) collective-permute-start(bf16[1,2,32,3328]{3,2,1,0:T(8,128)(2,1)S(1)} %get-tuple-element.121), channel_id=1, source_target_pairs={{0,2},{1,3},{2,0},{3,1},{4,6},{5,7},{6,4},{7,5},{8,10},{9,11},{10,... | collective-permute-start | bytes 1277960 | tf_op jit(solution)/shard_map/ppermute | solution.py:26
  106.4 12.7 %collective-permute-start.32 = (bf16[1,128,256]{2,1,0:T(8,128)(2,1)S(1)}, bf16[1,128,256]{2,1,0:T(8,128)(2,1)S(1)}, u32[]{:S(2)}, u32[]{:S(2)}) collective-permute-start(bf16[1,128,256]{2,1,0:T(8,128)(2,1)S(1)} %slice.131), channel_id=1, source_target_pairs={{0,16},{4,20},{8,24},{12,28},{16,0},{20,4},{24,8},{28,12},{1,17},{... | collective-permute-start | bytes 196616 | tf_op jit(solution)/shard_map/ppermute | solution.py:26
  112.5 9.6 %collective-permute-start.41 = (bf16[2,128,256]{2,1,0:T(8,128)(2,1)S(1)}, bf16[2,128,256]{2,1,0:T(8,128)(2,1)S(1)}, u32[]{:S(2)}, u32[]{:S(2)}) collective-permute-start(bf16[2,128,256]{2,1,0:T(8,128)(2,1)S(1)} %slice.133), channel_id=1, source_target_pairs={{0,8},{4,12},{8,0},{12,4},{16,24},{20,28},{24,16},{28,20},{1,9},{5... | collective-permute-start | bytes 393224 | tf_op jit(solution)/shard_map/ppermute | solution.py:26
  117.5 9.5 %collective-permute-start.46 = (bf16[4,128,256]{2,1,0:T(8,128)(2,1)S(1)}, bf16[4,128,256]{2,1,0:T(8,128)(2,1)S(1)}, u32[]{:S(2)}, u32[]{:S(2)}) collective-permute-start(bf16[4,128,256]{2,1,0:T(8,128)(2,1)S(1)} %get-tuple-element.127), channel_id=1, source_target_pairs={{0,4},{4,0},{8,12},{12,8},{16,20},{20,16},{24,28},{28,24},{1,5},{5... | collective-permute-start | bytes 786440 | tf_op jit(solution)/shard_map/ppermute | solution.py:26
  120.8 6.2 %collective-permute-start.50 = (bf16[32,3328]{1,0:T(8,128)(2,1)S(1)}, bf16[32,3328]{1,0:T(8,128)(2,1)S(1)}, u32[]{:S(2)}, u32[]{:S(2)}) collective-permute-start(bf16[32,3328]{1,0:T(8,128)(2,1)S(1)} %gated.7.refs_0_), channel_id=1, source_target_pairs={{0,2},{1,3},{2,0},{3,1},{4,6},{5,7},{6,4},{7,5},{8,10},{9,11},{10,... | collective-permute-start | bytes 638984 | tf_op jit(solution)/shard_map/ppermute | solution.py:26
  122.1 5.0 %collective-permute-start.51 = (bf16[32,3328]{1,0:T(8,128)(2,1)S(1)}, bf16[32,3328]{1,0:T(8,128)(2,1)S(1)}, u32[]{:S(2)}, u32[]{:S(2)}) collective-permute-start(bf16[32,3328]{1,0:T(8,128)(2,1)S(1)} %gated.7.refs_0_), channel_id=1, source_target_pairs={{0,1},{1,0},{2,3},{3,2},{4,5},{5,4},{6,7},{7,6},{8,9},{9,8},{10,11... | collective-permute-start | bytes 638984 | tf_op jit(solution)/shard_map/ppermute | solution.py:26
  122.2 11.4 %collective-permute-start.42 = (bf16[1,128,256]{2,1,0:T(8,128)(2,1)S(1)}, bf16[1,128,256]{2,1,0:T(8,128)(2,1)S(1)}, u32[]{:S(2)}, u32[]{:S(2)}) collective-permute-start(bf16[1,128,256]{2,1,0:T(8,128)(2,1)S(1)} %slice.135), channel_id=1, source_target_pairs={{0,16},{4,20},{8,24},{12,28},{16,0},{20,4},{24,8},{28,12},{1,17},{... | collective-permute-start | bytes 196616 | tf_op jit(solution)/shard_map/ppermute | solution.py:26
  132.0 8.4 %collective-permute-start.53 = (bf16[4,128,256]{2,1,0:T(8,128)(2,1)S(1)}, bf16[4,128,256]{2,1,0:T(8,128)(2,1)S(1)}, u32[]{:S(2)}, u32[]{:S(2)}) collective-permute-start(bf16[4,128,256]{2,1,0:T(8,128)(2,1)S(1)} %get-tuple-element.132), channel_id=1, source_target_pairs={{0,4},{4,0},{8,12},{12,8},{16,20},{20,16},{24,28},{28,24},{1,5},{5... | collective-permute-start | bytes 786440 | tf_op jit(solution)/shard_map/ppermute | solution.py:26
  133.6 8.6 %collective-permute-start.47 = (bf16[2,128,256]{2,1,0:T(8,128)(2,1)S(1)}, bf16[2,128,256]{2,1,0:T(8,128)(2,1)S(1)}, u32[]{:S(2)}, u32[]{:S(2)}) collective-permute-start(bf16[2,128,256]{2,1,0:T(8,128)(2,1)S(1)} %slice.137), channel_id=1, source_target_pairs={{0,8},{4,12},{8,0},{12,4},{16,24},{20,28},{24,16},{28,20},{1,9},{5... | collective-permute-start | bytes 393224 | tf_op jit(solution)/shard_map/ppermute | solution.py:26
  140.5 5.7 %collective-permute-start.54 = (bf16[2,128,256]{2,1,0:T(8,128)(2,1)S(1)}, bf16[2,128,256]{2,1,0:T(8,128)(2,1)S(1)}, u32[]{:S(2)}, u32[]{:S(2)}) collective-permute-start(bf16[2,128,256]{2,1,0:T(8,128)(2,1)S(1)} %slice.141), channel_id=1, source_target_pairs={{0,8},{4,12},{8,0},{12,4},{16,24},{20,28},{24,16},{28,20},{1,9},{5... | collective-permute-start | bytes 393224 | tf_op jit(solution)/shard_map/ppermute | solution.py:26
  142.3 7.4 %collective-permute-start.48 = (bf16[1,128,256]{2,1,0:T(8,128)(2,1)S(1)}, bf16[1,128,256]{2,1,0:T(8,128)(2,1)S(1)}, u32[]{:S(2)}, u32[]{:S(2)}) collective-permute-start(bf16[1,128,256]{2,1,0:T(8,128)(2,1)S(1)} %slice.139), channel_id=1, source_target_pairs={{0,16},{4,20},{8,24},{12,28},{16,0},{20,4},{24,8},{28,12},{1,17},{... | collective-permute-start | bytes 196616 | tf_op jit(solution)/shard_map/ppermute | solution.py:26
  146.3 5.7 %collective-permute-start.55 = (bf16[1,128,256]{2,1,0:T(8,128)(2,1)S(1)}, bf16[1,128,256]{2,1,0:T(8,128)(2,1)S(1)}, u32[]{:S(2)}, u32[]{:S(2)}) collective-permute-start(bf16[1,128,256]{2,1,0:T(8,128)(2,1)S(1)} %slice.143), channel_id=1, source_target_pairs={{0,16},{4,20},{8,24},{12,28},{16,0},{20,4},{24,8},{28,12},{1,17},{... | collective-permute-start | bytes 196616 | tf_op jit(solution)/shard_map/ppermute | solution.py:26
  (16 other events, 121.1 us)

commit v2 on v1

--- a/solution.py
+++ b/solution.py
@@ -20,6 +20,10 @@
     for b in range(bits):
         out = out + ((value >> b) & 1) * (1 << (bits - 1 - b))
     return out
+
+
+def spread(value, order):
+    return sum(((value >> (len(order) - 1 - s)) & 1) << b for s, b in enumerate(order))
 
 
 def flip(array, axis, size, mask):
@@ -146,19 +150,18 @@
     )(place.reshape(1), *shards, *[in_vmem(w) for w in (*gate, *up)])
 
 
-def down_kernel(parts, pieces, place_ref, *refs):
+def down_kernel(parts, pieces, order, place_ref, *refs):
     h_refs, w_refs, (keep_ref, send_ref, h_ref) = refs[:parts], refs[parts : parts + pieces], refs[parts + pieces :]
     top = 0
     for ref in h_refs:
         h_ref[top : top + ref.shape[0]] = ref[...]
         top += ref.shape[0]
     half, _, width = keep_ref.shape
-    bits = n_bits(2 * half)
     size = w_refs[0].shape[0]
     for out_ref, first in ((send_ref, half), (keep_ref, 0)):
 
         def block(i, carry, out_ref=out_ref, first=first):
-            spot = pl.multiple_of((place_ref[0] ^ reverse_bits(first + i, bits)) * width, width)
+            spot = pl.multiple_of((place_ref[0] ^ spread(first + i, order)) * width, width)
             part = sum(
                 jnp.dot(
                     h_ref[:, k * size : (k + 1) * size], w_ref[:, pl.ds(spot, width)], preferred_element_type=jnp.float32
@@ -171,19 +174,19 @@
         lax.fori_loop(0, half, block, 0)
 
 
-def down(place, hidden, weights, n_wide):
+def down(place, hidden, weights, n_wide, order):
     rows = sum(h.shape[0] for h in hidden)
     units, features = sum(w.shape[0] for w in weights), weights[0].shape[1]
-    width, bits, half = features // n_wide, n_bits(n_wide), n_wide // 2
+    width, half = features // n_wide, n_wide // 2
     if width % 128:
         part = jnp.dot(jnp.concatenate(hidden), jnp.concatenate(weights), preferred_element_type=jnp.float32)
         part = part.astype(jnp.bfloat16).reshape(rows, n_wide, width).transpose(1, 0, 2)
-        part = jnp.take(part, place ^ reverse_bits(jnp.arange(n_wide), bits), axis=0)
+        part = jnp.take(part, place ^ spread(jnp.arange(n_wide), order), axis=0)
         return part[:half], part[half:]
     out = jax.ShapeDtypeStruct((half, rows, width), jnp.bfloat16)
     vmem = pl.BlockSpec(memory_space=pltpu.VMEM)
     return pl.pallas_call(
-        functools.partial(down_kernel, len(hidden), len(weights)),
+        functools.partial(down_kernel, len(hidden), len(weights), order),
         in_specs=[pl.BlockSpec(memory_space=pltpu.SMEM)] + [vmem] * (len(hidden) + len(weights)),
         out_specs=[vmem, vmem],
         scratch_shapes=[pltpu.VMEM((rows, units), jnp.bfloat16)],
@@ -217,15 +220,18 @@
 
 def add_halves_kernel(a_ref, *refs):
     piece_refs, (first_ref, second_ref) = refs[:-2], refs[-2:]
-    half, width = first_ref.shape[0], a_ref.shape[-1]
+    half, rows, width = first_ref.shape[0], a_ref.shape[-2], a_ref.shape[-1]
     tile = tiles_of(width)
 
     def columns(j, carry):
         cols = pl.ds(pl.multiple_of(j * tile, tile), tile)
-        for i in range(2 * half):
-            for s in (0, 1):
-                total = add(a_ref[i, s, :, cols], piece_refs[2 * i + s][:, cols])
-                (first_ref if i < half else second_ref)[i % half, s, :, cols] = total
+        top = 0
+        for ref in piece_refs:
+            size = ref.shape[0]
+            i, s, row = top // (2 * rows), top // rows % 2, top % rows
+            total = add(a_ref[i, s, row : row + size, cols], ref[:, cols])
+            (first_ref if i < half else second_ref)[i % half, s, row : row + size, cols] = total
+            top += size
         return carry
 
     lax.fori_loop(0, width // tile, columns, 0)
@@ -256,7 +262,7 @@
     if a.shape[-1] % 128 or a.shape[-2] % 16:
         gate, up = (a[0, s].astype(jnp.float32) + b[0, s].astype(jnp.float32) for s in (0, 1))
         return (jax.nn.silu(gate) * up).astype(jnp.bfloat16)
-    return kernel_call(gated_kernel, [a.shape[2:]], a, b, name="gated", size=4 * MIB)[0]
+    return kernel_call(gated_kernel, [a.shape[2:]], a, b, name="gated", size=8 * MIB)[0]
 
 
 def deal_kernel(edges, place_ref, x_ref, *out_refs):
@@ -288,17 +294,18 @@
 def collect_kernel(edges, place_ref, *refs):
     part_refs, out_ref = refs[:-1], refs[-1]
     count = out_ref.shape[0]
+    pieces = [ref.at[m] for ref in part_refs for m in range(ref.shape[0])]
     for i in range(count):
         target = place_ref[0] ^ reverse_bits(i, n_bits(count))
-        for part_ref, lo, hi in zip(part_refs, edges, edges[1:]):
-            out_ref[target, lo:hi] = part_ref[i]
+        for piece, lo, hi in zip(pieces, edges, edges[1:]):
+            out_ref[target, lo:hi] = piece[i]
 
 
 def collect(place, parts, edges):
-    count, _, width = parts[0].shape
+    _, count, _, width = parts[0].shape
     if width % 128 or any((hi - lo) % 16 for lo, hi in zip(edges, edges[1:])):
         order = reverse_bits(place ^ jnp.arange(count), n_bits(count))
-        return jnp.take(jnp.concatenate(parts, axis=1), order, axis=0)
+        return jnp.take(jnp.concatenate([piece for part in parts for piece in part], axis=1), order, axis=0)
     vmem = pl.BlockSpec(memory_space=pltpu.VMEM)
     return pl.pallas_call(
         functools.partial(collect_kernel, edges),
@@ -330,11 +337,11 @@
                 got = after(got, *others)
             tok[k] = [jnp.concatenate([tok[k][0], got])] if level[k] else [tok[k][0], got]
 
-    def sum_core(k, *others):
+    def sum_core(k, pieces=8):
         for b in range(nar_bits - 1):
-            got = [flip(send[k][i, j], "nar", n_nar, 1 << b) for i in range(send[k].shape[0]) for j in (0, 1)]
-            if others:
-                got[0] = after(got[0], *others)
+            flat = send[k].reshape(-1, send[k].shape[-1])
+            size = min(max(flat.shape[0] // pieces, 16), send[k].shape[-2])
+            got = [flip(flat[i : i + size], "nar", n_nar, 1 << b) for i in range(0, flat.shape[0], size)]
             keep[k], send[k] = add_halves(keep[k], got)
 
     far = 1 << (nar_bits - 1)
@@ -344,26 +351,39 @@
         hidden[k] = [gated_sum(keep[k], got)]
         hidden[k].append(flip(hidden[k][0], "nar", n_nar, far))
 
-    def gather_hidden(k):
+    def gather_hidden(k, pieces=1):
         for b in reversed(range(nar_bits - 1)):
-            hidden[k] = hidden[k] + [flip(g, "nar", n_nar, 1 << b) for g in hidden[k]]
+            cut = [piece for g in hidden[k] for piece in jnp.split(g, pieces)]
+            hidden[k] = hidden[k] + [flip(g, "nar", n_nar, 1 << b) for g in cut]
 
     keep, send, hidden = [None] * n, [None] * n, [None] * n
     parts, todo = [None] * n, [0] * n
-
-    def scatter(k, to):
+    orders = [tuple(range(wide_bits)) if k != 2 or wide_bits < 2 else (1, 0, *range(2, wide_bits)) for k in range(n)]
+
+    def scatter(k, to, *others, split=False):
         while todo[k] > to:
-            total = add(parts[k][0], flip(parts[k][1], "wide", n_wide, 1 << (wide_bits - todo[k])))
+            mask = 1 << orders[k][wide_bits - todo[k]]
             todo[k] -= 1
-            half = total.shape[0] // 2
-            parts[k] = (total[:half], total[half:]) if todo[k] else (total,)
+            mine, other = parts[k]
+            half = mine.shape[0] // 2
+            if todo[k] and split:
+                got = [flip(other[:half], "wide", n_wide, mask), flip(other[half:], "wide", n_wide, mask)]
+                got = [after(g, *others) if others else g for g in got]
+                parts[k] = (add(mine[:half], got[0]), add(mine[half:], got[1]))
+            else:
+                got = flip(other, "wide", n_wide, mask)
+                total = add(mine, after(got, *others) if others else got)
+                parts[k] = (total[:half], total[half:]) if todo[k] else (total,)
 
     def products(k, *others):
         keep[k], send[k] = gate_up(wide, [after(tok[k][0], *others), *tok[k][1:]], gate, up, n_nar)
 
     def finish(k, weights, *others):
-        hidden[k][0] = after(hidden[k][0], *others)
-        parts[k], todo[k] = down(wide, hidden[k], weights, n_wide), wide_bits
+        chunks = k if isinstance(k, list) else [k]
+        rows_of = [g for j in chunks for g in hidden[j]]
+        rows_of[0] = after(rows_of[0], *others)
+        k = chunks[0]
+        parts[k], todo[k] = down(wide, rows_of, weights, n_wide, orders[k]), wide_bits
 
     if not fast or n != 4 or wide_bits < 2:
         gate, up, down_w = [decode(gw, gs)], [decode(uw, us)], [decode(dw, ds)]
@@ -377,9 +397,11 @@
             scatter(k, 0)
     else:
         gate = [decode_part(after(gw, dealt[0]), gs, 0, 2)]
-        for k in range(4):
+        for k in (0, 1):
             gather_tokens(k, wide_bits - 1, gate[0])
         gate.append(decode_part(after(gw, gate[0], tok[0][0]), gs, 1, 2))
+        for k in (2, 3):
+            gather_tokens(k, wide_bits - 1, gate[1])
         for k in (0, 1):
             gather_tokens(k, 1, gate[1])
         up = [decode_part(after(uw, tok[0][0], tok[1][0]), us, 0, 1)]
@@ -389,36 +411,38 @@
         products(0)
         gather_tokens(1, 0, send[0])
         send[0] = after(send[0], tok[1][1], tok[2][0], tok[3][0])
+        tok[2], tok[3] = [after(tok[2][0], send[0])], [after(tok[3][0], send[0])]
         gather_tokens(2, 0)
         gather_tokens(3, 0)
-        sum_core(0)
+        sum_core(0, 4)
         down_w = []
         for k in range(3):
-            products(k + 1, send[k], *(hidden[k - 1][:2] if k > 0 else []))
+            products(k + 1, send[0] if k == 0 else hidden[k - 1][0])
             if k < 2:
-                down_w.append(decode_part(after(dw, send[k + 1]), ds, k, 2))
                 tok[k + 2][1] = after(tok[k + 2][1], send[k + 1])
-                send[k + 1] = after(send[k + 1], tok[k + 2][1], down_w[k])
-            else:
-                finish(0, down_w, send[3])
-                send[3] = after(send[3], parts[0][1])
-            gated(k, send[k + 1])
-            sum_core(k + 1, hidden[k][0])
-            gather_hidden(k)
-        scatter(0, wide_bits - 1)
-        finish(1, down_w, send[3], *parts[0])
-        scatter(0, wide_bits - 2)
-        scatter(1, wide_bits - 1)
-        finish(2, down_w, *parts[0], *parts[1])
-        gated(3, parts[2][1])
-        scatter(0, max(wide_bits - 3, 0))
-        scatter(1, wide_bits - 2)
-        scatter(2, wide_bits - 1)
-        gather_hidden(3)
-        finish(3, down_w, *parts[0], *parts[1], *parts[2])
-        for k in range(4):
+                send[k + 1] = after(send[k + 1], tok[k + 2][1])
+            sum_core(k + 1)
+            others = [send[k + 1]]
+            if k > 0:
+                down_w.append(decode_part(after(dw, send[k + 1]), ds, k - 1, 2))
+                others += [down_w[-1], hidden[k - 1][1]]
+            gated(k, *others)
+        for j in (0, 1):
+            hidden[j] = [after(g, hidden[2][0]) for g in hidden[j]]
+            gather_hidden(j, 1)
+        finish([0, 1], down_w, hidden[2][0])
+        gated(3, parts[0][1])
+        gather_hidden(2, 2)
+        finish(2, down_w, hidden[3][0])
+        scatter(0, wide_bits - 1, parts[2][1], split=True)
+        gather_hidden(3, 1)
+        finish(3, down_w, *parts[0])
+        scatter(0, wide_bits - 2, parts[3][1])
+        scatter(2, wide_bits - 1, parts[3][1])
+        for k in (0, 2, 3):
             scatter(k, 0)
-    outs = [part[0].reshape(n_nar, -1, width) for part in parts]
+        parts = [parts[0], parts[2], parts[3]]
+    outs = [part[0].reshape(-1, n_nar, cuts[0] // n_nar, width) for part in parts]
     return collect(nar, outs, edges).reshape(rows, width)
 
 

time: 153 us -> 142 us (0.928)
  starting transfers between devices: 51.7 us -> 47.1 us
  waiting for transfers between devices: 37.8 us -> 33.6 us
  Pallas kernels: 59.8 us -> 57.9 us
    ppermute x56 -> x68, starting transfers between devices: 51.7 us -> 47.1 us  [flip(): return lax.ppermute(array, axis, [(i, i ^ mask) for i in range(size)])]
    ppermute x56 -> x68, waiting for transfers between devices: 37.8 us -> 33.6 us  [flip(): return lax.ppermute(array, axis, [(i, i ^ mask) for i in range(size)])]
    pallas_call x4 -> x3, Pallas kernels: 14 us -> 12.3 us  [down(): pl.pallas_call(functools.partial(down_kernel, len(hidden), len(weights),...]
  transfers between devices with their start and end apart: 56 -> 68, of which waited for: 22 -> 33; matrix products, arithmetic and copies ran while one was open for 1% -> 1% of each run, Pallas kernels for 39% -> 40%
where the time goes in v2:
time: 142 us
  Pallas kernels  57.9 us (41%)
  starting transfers between devices  47.1 us (33%)
  waiting for transfers between devices  33.6 us (24%)
  local copies, waits for them, and re-layouts  2.28 us (2%)
    ppermute x68, starting transfers between devices, flip(): return lax.ppermute(array, axis, [(i, i ^ mask) for i in range(size)])  47.1 us
    ppermute x68, waiting for transfers between devices, flip(): return lax.ppermute(array, axis, [(i, i ^ mask) for i in range(size)])  33.6 us
    pallas_call x4, Pallas kernels, gate_up(): pl.pallas_call(functools.partial(gate_up_kernel, len(shards), len(gate),...  24.6 us
    pallas_call x5, Pallas kernels, decode_part(): pl.pallas_call(functools.partial(decode_kernel, part * size, block), in_s...  17.7 us
    pallas_call x3, Pallas kernels, down(): pl.pallas_call(functools.partial(down_kernel, len(hidden), len(weights),...  12.3 us
  transfers between devices with their start and end apart: 68, of which 33 were waited for; matrix products, arithmetic and copies ran while one was open for 1% of the time, Pallas kernels for 40%

profile of v2, /device:TPU:0, one launch (start us, length us, event | category | flops | bytes accessed | tf_op | source)
XLA Modules:
  0.0 142.1 jit_solution(8576302446692754866)
XLA Ops:
  0.0 1.0 copy-done.3
  1.0 4.1 %collective-permute-start = (bf16[1,128,256]{2,1,0:T(8,128)(2,1)S(1)}, bf16[1,128,256]{2,1,0:T(8,128)(2,1)S(1)}, u32[]{:S(2)}, u32[]{:S(2)}) collective-permute-start(bf16[1,128,256]{2,1,0:T(8,128)(2,1)S(1)} %bitcast.23), channel_id=1, source_target_pairs={{0,16},{4,20},{8,24},{12,28},{16,0},{20,4},{24,8},{28,12},{1,17},{... | collective-permute-start | bytes 196616 | tf_op jit(solution)/shard_map/ppermute | solution.py:30
  5.2 2.8 %collective-permute-start.3 = (bf16[1,128,256]{2,1,0:T(8,128)(2,1)S(1)}, bf16[1,128,256]{2,1,0:T(8,128)(2,1)S(1)}, u32[]{:S(2)}, u32[]{:S(2)}) collective-permute-start(bf16[1,128,256]{2,1,0:T(8,128)(2,1)S(1)} %bitcast.26), channel_id=1, source_target_pairs={{0,16},{4,20},{8,24},{12,28},{16,0},{20,4},{24,8},{28,12},{1,17},{... | collective-permute-start | bytes 196616 | tf_op jit(solution)/shard_map/ppermute | solution.py:30
  8.1 0.9 copy-done.1
  9.1 3.2 %decode.5.refs_2_ = bf16[1024,3328]{1,0:T(8,128)(2,1)S(1)} custom-call(bf16[2048,3328]{1,0:T(8,128)(2,1)} %w_ref.1, f32[16,3328]{1,0:T(8,128)S(1)} %copy-done.1), custom_call_target="tpu_custom_call" | custom-call | flops 1024 | bytes 1024 | tf_op jit(solution)/shard_map/decode/pallas_call | solution.py:78
  12.3 1.9 %collective-permute-start.1 = (bf16[2,128,256]{2,1,0:T(8,128)(2,1)S(1)}, bf16[2,128,256]{2,1,0:T(8,128)(2,1)S(1)}, u32[]{:S(2)}, u32[]{:S(2)}) collective-permute-start(bf16[2,128,256]{2,1,0:T(8,128)(2,1)S(1)} %pad_maximum_fusion.4), channel_id=1, source_target_pairs={{0,8},{4,12},{8,0},{12,4},{16,24},{20,28},{24,16},{28,20},{1,9},{5... | collective-permute-start | bytes 393224 | tf_op jit(solution)/shard_map/ppermute | solution.py:30
  14.2 2.3 %collective-permute-done.3 = bf16[1,128,256]{2,1,0:T(8,128)(2,1)S(1)} collective-permute-done((bf16[1,128,256]{2,1,0:T(8,128)(2,1)S(1)}, bf16[1,128,256]{2,1,0:T(8,128)(2,1)S(1)}, u32[]{:S(2)}, u32[]{:S(2)}) %collective-permute-start.3) | collective-permute-done | bytes 65568 | tf_op jit(solution)/shard_map/ppermute | solution.py:30
  16.6 3.2 %decode.6.refs_3_ = bf16[1024,3328]{1,0:T(8,128)(2,1)S(1)} custom-call(bf16[2048,3328]{1,0:T(8,128)(2,1)} %w_ref.1, f32[16,3328]{1,0:T(8,128)S(1)} %copy-done.2), custom_call_target="tpu_custom_call" | custom-call | flops 1024 | bytes 1024 | tf_op jit(solution)/shard_map/decode/pallas_call | solution.py:78
  19.8 2.1 %collective-permute-start.9 = (bf16[2,128,256]{2,1,0:T(8,128)(2,1)S(1)}, bf16[2,128,256]{2,1,0:T(8,128)(2,1)S(1)}, u32[]{:S(2)}, u32[]{:S(2)}) collective-permute-start(bf16[2,128,256]{2,1,0:T(8,128)(2,1)S(1)} %pad_maximum_fusion.7), channel_id=1, source_target_pairs={{0,8},{4,12},{8,0},{12,4},{16,24},{20,28},{24,16},{28,20},{1,9},{5... | collective-permute-start | bytes 393224 | tf_op jit(solution)/shard_map/ppermute | solution.py:30
  21.9 1.0 collective-permute-done.4
  23.0 1.8 %collective-permute-start.2 = (bf16[4,128,256]{2,1,0:T(8,128)(2,1)S(1)}, bf16[4,128,256]{2,1,0:T(8,128)(2,1)S(1)}, u32[]{:S(2)}, u32[]{:S(2)}) collective-permute-start(bf16[4,128,256]{2,1,0:T(8,128)(2,1)S(1)} %get-tuple-element.175.refs_0_), channel_id=1, source_target_pairs={{0,4},{4,0},{8,12},{12,8},{16,20},{20,16},{24,28},{28,24},{1,5},{5... | collective-permute-start | bytes 786440 | tf_op jit(solution)/shard_map/ppermute | solution.py:30
  25.1 5.1 %decode.7.refs_4_ = bf16[2048,3328]{1,0:T(8,128)(2,1)S(1)} custom-call(bf16[2048,3328]{1,0:T(8,128)(2,1)} %w_ref.2, f32[16,3328]{1,0:T(8,128)S(1)} %copy-done.4), custom_call_target="tpu_custom_call" | custom-call | flops 1024 | bytes 1024 | tf_op jit(solution)/shard_map/decode/pallas_call | solution.py:78
  30.3 1.9 %collective-permute-done.2.refs_1_ = bf16[4,128,256]{2,1,0:T(8,128)(2,1)S(1)} collective-permute-done((bf16[4,128,256]{2,1,0:T(8,128)(2,1)S(1)}, bf16[4,128,256]{2,1,0:T(8,128)(2,1)S(1)}, u32[]{:S(2)}, u32[]{:S(2)}) %collective-permute-start.2) | collective-permute-done | bytes 262176 | tf_op jit(solution)/shard_map/ppermute | solution.py:30
  32.2 6.3 %gate_up.4 = (bf16[2,2,32,3328]{3,2,1,0:T(8,128)(2,1)S(1)}, bf16[2,2,32,3328]{3,2,1,0:T(8,128)(2,1)S(1)}) custom-call(s32[1]{0:T(128)} %bitcast.1.place_ref, bf16[4,128,256]{2,1,0:T(8,128)(2,1)S(1)} %get-tuple-element.175.refs_0_, bf16[4,128,256]{2,1,0:T(8,128)(2,1)S(1)} %collective-permute-done.2.refs_1_, bf16[1024,3328]{1,0:T(8,128)(2,1)S(1)} %decode.5.refs_2_, ...), custom_call_target="tpu_custom_call" | custom-call | flops 1024 | bytes 1024 | tf_op jit(solution)/shard_map/gate_up/pallas_call | solution.py:141
  38.5 1.8 %collective-permute-start.15 = (bf16[4,128,256]{2,1,0:T(8,128)(2,1)S(1)}, bf16[4,128,256]{2,1,0:T(8,128)(2,1)S(1)}, u32[]{:S(2)}, u32[]{:S(2)}) collective-permute-start(bf16[4,128,256]{2,1,0:T(8,128)(2,1)S(1)} %pad_maximum_fusion.2.refs_0_), channel_id=1, source_target_pairs={{0,4},{4,0},{8,12},{12,8},{16,20},{20,16},{24,28},{28,24},{1,5},{5... | collective-permute-start | bytes 786440 | tf_op jit(solution)/shard_map/ppermute | solution.py:30
  43.1 1.6 %collective-permute-start.14 = (bf16[1,2,32,3328]{3,2,1,0:T(8,128)(2,1)S(1)}, bf16[1,2,32,3328]{3,2,1,0:T(8,128)(2,1)S(1)}, u32[]{:S(2)}, u32[]{:S(2)}) collective-permute-start(bf16[1,2,32,3328]{3,2,1,0:T(8,128)(2,1)S(1)} %get-tuple-element.94), channel_id=1, source_target_pairs={{0,2},{1,3},{2,0},{3,1},{4,6},{5,7},{6,4},{7,5},{8,10},{9,11},{10,... | collective-permute-start | bytes 1277960 | tf_op jit(solution)/shard_map/ppermute | solution.py:30
  44.6 6.1 %gate_up.5 = (bf16[2,2,32,3328]{3,2,1,0:T(8,128)(2,1)S(1)}, bf16[2,2,32,3328]{3,2,1,0:T(8,128)(2,1)S(1)}) custom-call(s32[1]{0:T(128)} %bitcast.1.place_ref, bf16[4,128,256]{2,1,0:T(8,128)(2,1)S(1)} %get-tuple-element.95.refs_0_, bf16[4,128,256]{2,1,0:T(8,128)(2,1)S(1)} %collective-permute-done.5.refs_1_, bf16[1024,3328]{1,0:T(8,128)(2,1)S(1)} %decode.5.refs_2_, ...), custom_call_target="tpu_custom_call" | custom-call | flops 1024 | bytes 1024 | tf_op jit(solution)/shard_map/gate_up/pallas_call | solution.py:141
  56.3 6.1 %gate_up.6 = (bf16[2,2,32,3328]{3,2,1,0:T(8,128)(2,1)S(1)}, bf16[2,2,32,3328]{3,2,1,0:T(8,128)(2,1)S(1)}) custom-call(s32[1]{0:T(128)} %bitcast.1.place_ref, bf16[4,128,256]{2,1,0:T(8,128)(2,1)S(1)} %pad_maximum_fusion.2.refs_0_, bf16[4,128,256]{2,1,0:T(8,128)(2,1)S(1)} %collective-permute-done.15.refs_1_, bf16[1024,3328]{1,0:T(8,128)(2,1)S(1)} %decode.5.refs_2_, ...), custom_call_target="tpu_custom_call" | custom-call | flops 1024 | bytes 1024 | tf_op jit(solution)/shard_map/gate_up/pallas_call | solution.py:141
  64.0 1.6 %collective-permute-start.35 = (bf16[32,3328]{1,0:T(8,128)(2,1)S(1)}, bf16[32,3328]{1,0:T(8,128)(2,1)S(1)}, u32[]{:S(2)}, u32[]{:S(2)}) collective-permute-start(bf16[32,3328]{1,0:T(8,128)(2,1)S(1)} %gated.4.refs_0_), channel_id=1, source_target_pairs={{0,2},{1,3},{2,0},{3,1},{4,6},{5,7},{6,4},{7,5},{8,10},{9,11},{10,... | collective-permute-start | bytes 638984 | tf_op jit(solution)/shard_map/ppermute | solution.py:30
  66.2 0.7 collective-permute-done.27.refs_2_
  68.4 3.1 %decode.8.refs_8_.refs_6_.refs_4_ = bf16[1664,2048]{1,0:T(8,128)(2,1)S(1)} custom-call(bf16[3328,2048]{1,0:T(8,128)(2,1)} %w_ref.4, f32[26,2048]{1,0:T(8,128)S(1)} %copy-done), custom_call_target="tpu_custom_call" | custom-call | flops 1024 | bytes 1024 | tf_op jit(solution)/shard_map/decode/pallas_call | solution.py:78
  71.5 0.8 collective-permute-done.35.refs_1_
  72.7 6.1 %gate_up.7 = (bf16[2,2,32,3328]{3,2,1,0:T(8,128)(2,1)S(1)}, bf16[2,2,32,3328]{3,2,1,0:T(8,128)(2,1)S(1)}) custom-call(s32[1]{0:T(128)} %bitcast.1.place_ref, bf16[4,128,256]{2,1,0:T(8,128)(2,1)S(1)} %pad_maximum_fusion.3.refs_0_, bf16[4,128,256]{2,1,0:T(8,128)(2,1)S(1)} %collective-permute-done.24.refs_1_, bf16[1024,3328]{1,0:T(8,128)(2,1)S(1)} %decode.5.refs_2_, ...), custom_call_target="tpu_custom_call" | custom-call | flops 1024 | bytes 1024 | tf_op jit(solution)/shard_map/gate_up/pallas_call | solution.py:141
  80.4 1.3 collective-permute-start.44
  82.4 0.7 collective-permute-done.38.refs_2_
  83.9 0.8 collective-permute-start.50
  84.6 3.1 %decode.9.refs_9_.refs_7_.refs_5_ = bf16[1664,2048]{1,0:T(8,128)(2,1)S(1)} custom-call(bf16[3328,2048]{1,0:T(8,128)(2,1)} %w_ref.4, f32[26,2048]{1,0:T(8,128)S(1)} %copy-done), custom_call_target="tpu_custom_call" | custom-call | flops 1024 | bytes 1024 | tf_op jit(solution)/shard_map/decode/pallas_call | solution.py:78
  87.7 0.8 collective-permute-done.44.refs_5_
  90.4 1.3 collective-permute-start.51
  92.3 5.3 %down.3 = (bf16[4,256,256]{2,1,0:T(8,128)(2,1)S(1)}, bf16[4,256,256]{2,1,0:T(8,128)(2,1)S(1)}) custom-call(s32[1]{0:T(128)} %bitcast.1.place_ref, bf16[32,3328]{1,0:T(8,128)(2,1)S(1)} %gated.4.refs_0_, bf16[32,3328]{1,0:T(8,128)(2,1)S(1)} %collective-permute-done.35.refs_1_, bf16[32,3328]{1,0:T(8,128)(2,1)S(1)} %collective-permute-done.45.refs_2_, ...), custom_call_target="tpu_custom_call" | custom-call | flops 1024 | bytes 1024 | tf_op jit(solution)/shard_map/down/pallas_call | solution.py:188
  98.0 1.4 collective-permute-start.58
  99.5 1.6 %collective-permute-start.49 = (bf16[2,256,256]{2,1,0:T(8,128)(2,1)S(1)}, bf16[2,256,256]{2,1,0:T(8,128)(2,1)S(1)}, u32[]{:S(2)}, u32[]{:S(2)}) collective-permute-start(bf16[2,256,256]{2,1,0:T(8,128)(2,1)S(1)} %get-tuple-element.169), channel_id=1, source_target_pairs={{0,4},{4,0},{8,12},{12,8},{16,20},{20,16},{24,28},{28,24},{1,5},{5... | collective-permute-start | bytes 786440 | tf_op jit(solution)/shard_map/ppermute | solution.py:30
  101.0 1.2 collective-permute-done.51.refs_1_
  102.2 1.3 collective-permute-start.56
  104.2 0.8 collective-permute-done.55.refs_5_
  105.1 3.5 %down.4 = (bf16[4,128,256]{2,1,0:T(8,128)(2,1)S(1)}, bf16[4,128,256]{2,1,0:T(8,128)(2,1)S(1)}) custom-call(s32[1]{0:T(128)} %bitcast.1.place_ref, bf16[32,3328]{1,0:T(8,128)(2,1)S(1)} %gated.6.refs_0_, bf16[32,3328]{1,0:T(8,128)(2,1)S(1)} %collective-permute-done.51.refs_1_, bf16[16,3328]{1,0:T(8,128)(2,1)S(1)} %collective-permute-done.52.refs_2_, ...), custom_call_target="tpu_custom_call" | custom-call | flops 1024 | bytes 1024 | tf_op jit(solution)/shard_map/down/pallas_call | solution.py:188
  108.6 0.9 collective-permute-start.62
  109.7 2.8 %collective-permute-done.56 = bf16[2,256,256]{2,1,0:T(8,128)(2,1)S(1)} collective-permute-done((bf16[2,256,256]{2,1,0:T(8,128)(2,1)S(1)}, bf16[2,256,256]{2,1,0:T(8,128)(2,1)S(1)}, u32[]{:S(2)}, u32[]{:S(2)}) %collective-permute-start.56) | collective-permute-done | bytes 262176 | tf_op jit(solution)/shard_map/ppermute | solution.py:30
  112.6 0.8 collective-permute-start.57
  113.5 3.5 %down.5 = (bf16[4,128,256]{2,1,0:T(8,128)(2,1)S(1)}, bf16[4,128,256]{2,1,0:T(8,128)(2,1)S(1)}) custom-call(s32[1]{0:T(128)} %bitcast.1.place_ref, bf16[32,3328]{1,0:T(8,128)(2,1)S(1)} %gated.7.refs_0_, bf16[32,3328]{1,0:T(8,128)(2,1)S(1)} %collective-permute-done.58.refs_1_, bf16[32,3328]{1,0:T(8,128)(2,1)S(1)} %collective-permute-done.59.refs_2_, ...), custom_call_target="tpu_custom_call" | custom-call | flops 1024 | bytes 1024 | tf_op jit(solution)/shard_map/down/pallas_call | solution.py:188
  117.0 1.5 %collective-permute-start.65 = (bf16[4,128,256]{2,1,0:T(8,128)(2,1)S(1)}, bf16[4,128,256]{2,1,0:T(8,128)(2,1)S(1)}, u32[]{:S(2)}, u32[]{:S(2)}) collective-permute-start(bf16[4,128,256]{2,1,0:T(8,128)(2,1)S(1)} %get-tuple-element.134), channel_id=1, source_target_pairs={{0,4},{4,0},{8,12},{12,8},{16,20},{20,16},{24,28},{28,24},{1,5},{5... | collective-permute-start | bytes 786440 | tf_op jit(solution)/shard_map/ppermute | solution.py:30
  119.2 3.7 %collective-permute-done.57 = bf16[2,256,256]{2,1,0:T(8,128)(2,1)S(1)} collective-permute-done((bf16[2,256,256]{2,1,0:T(8,128)(2,1)S(1)}, bf16[2,256,256]{2,1,0:T(8,128)(2,1)S(1)}, u32[]{:S(2)}, u32[]{:S(2)}) %collective-permute-start.57) | collective-permute-done | bytes 262176 | tf_op jit(solution)/shard_map/ppermute | solution.py:30
  123.0 2.4 %collective-permute-start.61 = (bf16[1,256,256]{2,1,0:T(8,128)(2,1)S(1)}, bf16[1,256,256]{2,1,0:T(8,128)(2,1)S(1)}, u32[]{:S(2)}, u32[]{:S(2)}) collective-permute-start(bf16[1,256,256]{2,1,0:T(8,128)(2,1)S(1)} %slice.197), channel_id=1, source_target_pairs={{0,16},{4,20},{8,24},{12,28},{16,0},{20,4},{24,8},{28,12},{1,17},{... | collective-permute-start | bytes 393224 | tf_op jit(solution)/shard_map/ppermute | solution.py:30
  126.0 3.0 %collective-permute-start.64 = (bf16[1,128,256]{2,1,0:T(8,128)(2,1)S(1)}, bf16[1,128,256]{2,1,0:T(8,128)(2,1)S(1)}, u32[]{:S(2)}, u32[]{:S(2)}) collective-permute-start(bf16[1,128,256]{2,1,0:T(8,128)(2,1)S(1)} %slice.201), channel_id=1, source_target_pairs={{0,16},{4,20},{8,24},{12,28},{16,0},{20,4},{24,8},{28,12},{1,17},{... | collective-permute-start | bytes 196616 | tf_op jit(solution)/shard_map/ppermute | solution.py:30
  129.0 0.8 collective-permute-start.66
  129.8 4.8 %collective-permute-done.64 = bf16[1,128,256]{2,1,0:T(8,128)(2,1)S(1)} collective-permute-done((bf16[1,128,256]{2,1,0:T(8,128)(2,1)S(1)}, bf16[1,128,256]{2,1,0:T(8,128)(2,1)S(1)}, u32[]{:S(2)}, u32[]{:S(2)}) %collective-permute-start.64) | collective-permute-done | bytes 65568 | tf_op jit(solution)/shard_map/ppermute | solution.py:30
  134.6 1.3 collective-permute-done.66
  136.6 4.8 %collective-permute-done.67 = bf16[1,128,256]{2,1,0:T(8,128)(2,1)S(1)} collective-permute-done((bf16[1,128,256]{2,1,0:T(8,128)(2,1)S(1)}, bf16[1,128,256]{2,1,0:T(8,128)(2,1)S(1)}, u32[]{:S(2)}, u32[]{:S(2)}) %collective-permute-start.67) | collective-permute-done | bytes 65568 | tf_op jit(solution)/shard_map/ppermute | solution.py:30
  (148 shorter events, 22.8 us)
Async XLA Ops:
  1.0 11.2 %collective-permute-start = (bf16[1,128,256]{2,1,0:T(8,128)(2,1)S(1)}, bf16[1,128,256]{2,1,0:T(8,128)(2,1)S(1)}, u32[]{:S(2)}, u32[]{:S(2)}) collective-permute-start(bf16[1,128,256]{2,1,0:T(8,128)(2,1)S(1)} %bitcast.23), channel_id=1, source_target_pairs={{0,16},{4,20},{8,24},{12,28},{16,0},{20,4},{24,8},{28,12},{1,17},{... | collective-permute-start | bytes 196616 | tf_op jit(solution)/shard_map/ppermute | solution.py:30
  5.1 14.6 %collective-permute-start.6 = (bf16[1,128,256]{2,1,0:T(8,128)(2,1)S(1)}, bf16[1,128,256]{2,1,0:T(8,128)(2,1)S(1)}, u32[]{:S(2)}, u32[]{:S(2)}) collective-permute-start(bf16[1,128,256]{2,1,0:T(8,128)(2,1)S(1)} %bitcast.29), channel_id=1, source_target_pairs={{0,16},{4,20},{8,24},{12,28},{16,0},{20,4},{24,8},{28,12},{1,17},{... | collective-permute-start | bytes 196616 | tf_op jit(solution)/shard_map/ppermute | solution.py:30
  5.2 11.3 %collective-permute-start.3 = (bf16[1,128,256]{2,1,0:T(8,128)(2,1)S(1)}, bf16[1,128,256]{2,1,0:T(8,128)(2,1)S(1)}, u32[]{:S(2)}, u32[]{:S(2)}) collective-permute-start(bf16[1,128,256]{2,1,0:T(8,128)(2,1)S(1)} %bitcast.26), channel_id=1, source_target_pairs={{0,16},{4,20},{8,24},{12,28},{16,0},{20,4},{24,8},{28,12},{1,17},{... | collective-permute-start | bytes 196616 | tf_op jit(solution)/shard_map/ppermute | solution.py:30
  8.0 11.7 %collective-permute-start.8 = (bf16[1,128,256]{2,1,0:T(8,128)(2,1)S(1)}, bf16[1,128,256]{2,1,0:T(8,128)(2,1)S(1)}, u32[]{:S(2)}, u32[]{:S(2)}) collective-permute-start(bf16[1,128,256]{2,1,0:T(8,128)(2,1)S(1)} %bitcast.32), channel_id=1, source_target_pairs={{0,16},{4,20},{8,24},{12,28},{16,0},{20,4},{24,8},{28,12},{1,17},{... | collective-permute-start | bytes 196616 | tf_op jit(solution)/shard_map/ppermute | solution.py:30
  12.3 10.6 %collective-permute-start.1 = (bf16[2,128,256]{2,1,0:T(8,128)(2,1)S(1)}, bf16[2,128,256]{2,1,0:T(8,128)(2,1)S(1)}, u32[]{:S(2)}, u32[]{:S(2)}) collective-permute-start(bf16[2,128,256]{2,1,0:T(8,128)(2,1)S(1)} %pad_maximum_fusion.4), channel_id=1, source_target_pairs={{0,8},{4,12},{8,0},{12,4},{16,24},{20,28},{24,16},{28,20},{1,9},{5... | collective-permute-start | bytes 393224 | tf_op jit(solution)/shard_map/ppermute | solution.py:30
  16.5 6.4 %collective-permute-start.4 = (bf16[2,128,256]{2,1,0:T(8,128)(2,1)S(1)}, bf16[2,128,256]{2,1,0:T(8,128)(2,1)S(1)}, u32[]{:S(2)}, u32[]{:S(2)}) collective-permute-start(bf16[2,128,256]{2,1,0:T(8,128)(2,1)S(1)} %pad_maximum_fusion.5), channel_id=1, source_target_pairs={{0,8},{4,12},{8,0},{12,4},{16,24},{20,28},{24,16},{28,20},{1,9},{5... | collective-permute-start | bytes 393224 | tf_op jit(solution)/shard_map/ppermute | solution.py:30
  19.8 10.4 %collective-permute-start.9 = (bf16[2,128,256]{2,1,0:T(8,128)(2,1)S(1)}, bf16[2,128,256]{2,1,0:T(8,128)(2,1)S(1)}, u32[]{:S(2)}, u32[]{:S(2)}) collective-permute-start(bf16[2,128,256]{2,1,0:T(8,128)(2,1)S(1)} %pad_maximum_fusion.7), channel_id=1, source_target_pairs={{0,8},{4,12},{8,0},{12,4},{16,24},{20,28},{24,16},{28,20},{1,9},{5... | collective-permute-start | bytes 393224 | tf_op jit(solution)/shard_map/ppermute | solution.py:30
  21.9 8.4 %collective-permute-start.7 = (bf16[2,128,256]{2,1,0:T(8,128)(2,1)S(1)}, bf16[2,128,256]{2,1,0:T(8,128)(2,1)S(1)}, u32[]{:S(2)}, u32[]{:S(2)}) collective-permute-start(bf16[2,128,256]{2,1,0:T(8,128)(2,1)S(1)} %pad_maximum_fusion.6), channel_id=1, source_target_pairs={{0,8},{4,12},{8,0},{12,4},{16,24},{20,28},{24,16},{28,20},{1,9},{5... | collective-permute-start | bytes 393224 | tf_op jit(solution)/shard_map/ppermute | solution.py:30
  23.0 9.2 %collective-permute-start.2 = (bf16[4,128,256]{2,1,0:T(8,128)(2,1)S(1)}, bf16[4,128,256]{2,1,0:T(8,128)(2,1)S(1)}, u32[]{:S(2)}, u32[]{:S(2)}) collective-permute-start(bf16[4,128,256]{2,1,0:T(8,128)(2,1)S(1)} %get-tuple-element.175.refs_0_), channel_id=1, source_target_pairs={{0,4},{4,0},{8,12},{12,8},{16,20},{20,16},{24,28},{28,24},{1,5},{5... | collective-permute-start | bytes 786440 | tf_op jit(solution)/shard_map/ppermute | solution.py:30
  24.8 13.8 %collective-permute-start.5 = (bf16[4,128,256]{2,1,0:T(8,128)(2,1)S(1)}, bf16[4,128,256]{2,1,0:T(8,128)(2,1)S(1)}, u32[]{:S(2)}, u32[]{:S(2)}) collective-permute-start(bf16[4,128,256]{2,1,0:T(8,128)(2,1)S(1)} %get-tuple-element.95.refs_0_), channel_id=1, source_target_pairs={{0,4},{4,0},{8,12},{12,8},{16,20},{20,16},{24,28},{28,24},{1,5},{5... | collective-permute-start | bytes 786440 | tf_op jit(solution)/shard_map/ppermute | solution.py:30
  38.5 12.2 %collective-permute-start.15 = (bf16[4,128,256]{2,1,0:T(8,128)(2,1)S(1)}, bf16[4,128,256]{2,1,0:T(8,128)(2,1)S(1)}, u32[]{:S(2)}, u32[]{:S(2)}) collective-permute-start(bf16[4,128,256]{2,1,0:T(8,128)(2,1)S(1)} %pad_maximum_fusion.2.refs_0_), channel_id=1, source_target_pairs={{0,4},{4,0},{8,12},{12,8},{16,20},{20,16},{24,28},{28,24},{1,5},{5... | collective-permute-start | bytes 786440 | tf_op jit(solution)/shard_map/ppermute | solution.py:30
  40.4 1.5 %collective-permute-start.13 = (bf16[32,3328]{1,0:T(8,128)(2,1)S(1)}, bf16[32,3328]{1,0:T(8,128)(2,1)S(1)}, u32[]{:S(2)}, u32[]{:S(2)}) collective-permute-start(bf16[32,3328]{1,0:T(8,128)(2,1)S(1)} %get-tuple-element.163), channel_id=1, source_target_pairs={{0,1},{1,0},{2,3},{3,2},{4,5},{5,4},{6,7},{7,6},{8,9},{9,8},{10,11... | collective-permute-start | bytes 638984 | tf_op jit(solution)/shard_map/ppermute | solution.py:30
  40.4 1.8 %collective-permute-start.12 = (bf16[32,3328]{1,0:T(8,128)(2,1)S(1)}, bf16[32,3328]{1,0:T(8,128)(2,1)S(1)}, u32[]{:S(2)}, u32[]{:S(2)}) collective-permute-start(bf16[32,3328]{1,0:T(8,128)(2,1)S(1)} %get-tuple-element.164), channel_id=1, source_target_pairs={{0,1},{1,0},{2,3},{3,2},{4,5},{5,4},{6,7},{7,6},{8,9},{9,8},{10,11... | collective-permute-start | bytes 638984 | tf_op jit(solution)/shard_map/ppermute | solution.py:30
  40.9 1.6 %collective-permute-start.11 = (bf16[32,3328]{1,0:T(8,128)(2,1)S(1)}, bf16[32,3328]{1,0:T(8,128)(2,1)S(1)}, u32[]{:S(2)}, u32[]{:S(2)}) collective-permute-start(bf16[32,3328]{1,0:T(8,128)(2,1)S(1)} %get-tuple-element.165), channel_id=1, source_target_pairs={{0,1},{1,0},{2,3},{3,2},{4,5},{5,4},{6,7},{7,6},{8,9},{9,8},{10,11... | collective-permute-start | bytes 638984 | tf_op jit(solution)/shard_map/ppermute | solution.py:30
  41.0 1.8 %collective-permute-start.10 = (bf16[32,3328]{1,0:T(8,128)(2,1)S(1)}, bf16[32,3328]{1,0:T(8,128)(2,1)S(1)}, u32[]{:S(2)}, u32[]{:S(2)}) collective-permute-start(bf16[32,3328]{1,0:T(8,128)(2,1)S(1)} %get-tuple-element.166), channel_id=1, source_target_pairs={{0,1},{1,0},{2,3},{3,2},{4,5},{5,4},{6,7},{7,6},{8,9},{9,8},{10,11... | collective-permute-start | bytes 638984 | tf_op jit(solution)/shard_map/ppermute | solution.py:30
  43.1 12.8 %collective-permute-start.14 = (bf16[1,2,32,3328]{3,2,1,0:T(8,128)(2,1)S(1)}, bf16[1,2,32,3328]{3,2,1,0:T(8,128)(2,1)S(1)}, u32[]{:S(2)}, u32[]{:S(2)}) collective-permute-start(bf16[1,2,32,3328]{3,2,1,0:T(8,128)(2,1)S(1)} %get-tuple-element.94), channel_id=1, source_target_pairs={{0,2},{1,3},{2,0},{3,1},{4,6},{5,7},{6,4},{7,5},{8,10},{9,11},{10,... | collective-permute-start | bytes 1277960 | tf_op jit(solution)/shard_map/ppermute | solution.py:30
  50.9 1.5 %collective-permute-start.22 = (bf16[16,3328]{1,0:T(8,128)(2,1)S(1)}, bf16[16,3328]{1,0:T(8,128)(2,1)S(1)}, u32[]{:S(2)}, u32[]{:S(2)}) collective-permute-start(bf16[16,3328]{1,0:T(8,128)(2,1)S(1)} %get-tuple-element.156), channel_id=1, source_target_pairs={{0,1},{1,0},{2,3},{3,2},{4,5},{5,4},{6,7},{7,6},{8,9},{9,8},{10,11... | collective-permute-start | bytes 319496 | tf_op jit(solution)/shard_map/ppermute | solution.py:30
  51.4 11.0 %collective-permute-start.24 = (bf16[4,128,256]{2,1,0:T(8,128)(2,1)S(1)}, bf16[4,128,256]{2,1,0:T(8,128)(2,1)S(1)}, u32[]{:S(2)}, u32[]{:S(2)}) collective-permute-start(bf16[4,128,256]{2,1,0:T(8,128)(2,1)S(1)} %pad_maximum_fusion.3.refs_0_), channel_id=1, source_target_pairs={{0,4},{4,0},{8,12},{12,8},{16,20},{20,16},{24,28},{28,24},{1,5},{5... | collective-permute-start | bytes 786440 | tf_op jit(solution)/shard_map/ppermute | solution.py:30
  55.3 16.2 %collective-permute-start.34 = (bf16[1,2,32,3328]{3,2,1,0:T(8,128)(2,1)S(1)}, bf16[1,2,32,3328]{3,2,1,0:T(8,128)(2,1)S(1)}, u32[]{:S(2)}, u32[]{:S(2)}) collective-permute-start(bf16[1,2,32,3328]{3,2,1,0:T(8,128)(2,1)S(1)} %get-tuple-element.101), channel_id=1, source_target_pairs={{0,2},{1,3},{2,0},{3,1},{4,6},{5,7},{6,4},{7,5},{8,10},{9,11},{10,... | collective-permute-start | bytes 1277960 | tf_op jit(solution)/shard_map/ppermute | solution.py:30
  63.1 2.5 %collective-permute-start.30 = (bf16[16,3328]{1,0:T(8,128)(2,1)S(1)}, bf16[16,3328]{1,0:T(8,128)(2,1)S(1)}, u32[]{:S(2)}, u32[]{:S(2)}) collective-permute-start(bf16[16,3328]{1,0:T(8,128)(2,1)S(1)} %get-tuple-element.149), channel_id=1, source_target_pairs={{0,1},{1,0},{2,3},{3,2},{4,5},{5,4},{6,7},{7,6},{8,9},{9,8},{10,11... | collective-permute-start | bytes 319496 | tf_op jit(solution)/shard_map/ppermute | solution.py:30
  63.1 2.5 %collective-permute-start.29 = (bf16[16,3328]{1,0:T(8,128)(2,1)S(1)}, bf16[16,3328]{1,0:T(8,128)(2,1)S(1)}, u32[]{:S(2)}, u32[]{:S(2)}) collective-permute-start(bf16[16,3328]{1,0:T(8,128)(2,1)S(1)} %get-tuple-element.150), channel_id=1, source_target_pairs={{0,1},{1,0},{2,3},{3,2},{4,5},{5,4},{6,7},{7,6},{8,9},{9,8},{10,11... | collective-permute-start | bytes 319496 | tf_op jit(solution)/shard_map/ppermute | solution.py:30
  63.9 2.2 %collective-permute-start.28 = (bf16[16,3328]{1,0:T(8,128)(2,1)S(1)}, bf16[16,3328]{1,0:T(8,128)(2,1)S(1)}, u32[]{:S(2)}, u32[]{:S(2)}) collective-permute-start(bf16[16,3328]{1,0:T(8,128)(2,1)S(1)} %get-tuple-element.151), channel_id=1, source_target_pairs={{0,1},{1,0},{2,3},{3,2},{4,5},{5,4},{6,7},{7,6},{8,9},{9,8},{10,11... | collective-permute-start | bytes 319496 | tf_op jit(solution)/shard_map/ppermute | solution.py:30
  64.0 8.3 %collective-permute-start.35 = (bf16[32,3328]{1,0:T(8,128)(2,1)S(1)}, bf16[32,3328]{1,0:T(8,128)(2,1)S(1)}, u32[]{:S(2)}, u32[]{:S(2)}) collective-permute-start(bf16[32,3328]{1,0:T(8,128)(2,1)S(1)} %gated.4.refs_0_), channel_id=1, source_target_pairs={{0,2},{1,3},{2,0},{3,1},{4,6},{5,7},{6,4},{7,5},{8,10},{9,11},{10,... | collective-permute-start | bytes 638984 | tf_op jit(solution)/shard_map/ppermute | solution.py:30
  67.7 20.9 %collective-permute-start.33 = (bf16[1,2,32,3328]{3,2,1,0:T(8,128)(2,1)S(1)}, bf16[1,2,32,3328]{3,2,1,0:T(8,128)(2,1)S(1)}, u32[]{:S(2)}, u32[]{:S(2)}) collective-permute-start(bf16[1,2,32,3328]{3,2,1,0:T(8,128)(2,1)S(1)} %get-tuple-element.110), channel_id=1, source_target_pairs={{0,2},{1,3},{2,0},{3,1},{4,6},{5,7},{6,4},{7,5},{8,10},{9,11},{10,... | collective-permute-start | bytes 1277960 | tf_op jit(solution)/shard_map/ppermute | solution.py:30
  79.5 2.3 %collective-permute-start.41 = (bf16[16,3328]{1,0:T(8,128)(2,1)S(1)}, bf16[16,3328]{1,0:T(8,128)(2,1)S(1)}, u32[]{:S(2)}, u32[]{:S(2)}) collective-permute-start(bf16[16,3328]{1,0:T(8,128)(2,1)S(1)} %get-tuple-element.141), channel_id=1, source_target_pairs={{0,1},{1,0},{2,3},{3,2},{4,5},{5,4},{6,7},{7,6},{8,9},{9,8},{10,11... | collective-permute-start | bytes 319496 | tf_op jit(solution)/shard_map/ppermute | solution.py:30
  79.6 2.3 %collective-permute-start.40 = (bf16[16,3328]{1,0:T(8,128)(2,1)S(1)}, bf16[16,3328]{1,0:T(8,128)(2,1)S(1)}, u32[]{:S(2)}, u32[]{:S(2)}) collective-permute-start(bf16[16,3328]{1,0:T(8,128)(2,1)S(1)} %get-tuple-element.142), channel_id=1, source_target_pairs={{0,1},{1,0},{2,3},{3,2},{4,5},{5,4},{6,7},{7,6},{8,9},{9,8},{10,11... | collective-permute-start | bytes 319496 | tf_op jit(solution)/shard_map/ppermute | solution.py:30
  80.3 2.0 %collective-permute-start.39 = (bf16[16,3328]{1,0:T(8,128)(2,1)S(1)}, bf16[16,3328]{1,0:T(8,128)(2,1)S(1)}, u32[]{:S(2)}, u32[]{:S(2)}) collective-permute-start(bf16[16,3328]{1,0:T(8,128)(2,1)S(1)} %get-tuple-element.143), channel_id=1, source_target_pairs={{0,1},{1,0},{2,3},{3,2},{4,5},{5,4},{6,7},{7,6},{8,9},{9,8},{10,11... | collective-permute-start | bytes 319496 | tf_op jit(solution)/shard_map/ppermute | solution.py:30
  80.4 8.1 %collective-permute-start.44 = (bf16[32,3328]{1,0:T(8,128)(2,1)S(1)}, bf16[32,3328]{1,0:T(8,128)(2,1)S(1)}, u32[]{:S(2)}, u32[]{:S(2)}) collective-permute-start(bf16[32,3328]{1,0:T(8,128)(2,1)S(1)} %gated.5.refs_4_), channel_id=1, source_target_pairs={{0,2},{1,3},{2,0},{3,1},{4,6},{5,7},{6,4},{7,5},{8,10},{9,11},{10,... | collective-permute-start | bytes 638984 | tf_op jit(solution)/shard_map/ppermute | solution.py:30
  83.9 13.8 %collective-permute-start.50 = (bf16[1,2,32,3328]{3,2,1,0:T(8,128)(2,1)S(1)}, bf16[1,2,32,3328]{3,2,1,0:T(8,128)(2,1)S(1)}, u32[]{:S(2)}, u32[]{:S(2)}) collective-permute-start(bf16[1,2,32,3328]{3,2,1,0:T(8,128)(2,1)S(1)} %get-tuple-element.117), channel_id=1, source_target_pairs={{0,2},{1,3},{2,0},{3,1},{4,6},{5,7},{6,4},{7,5},{8,10},{9,11},{10,... | collective-permute-start | bytes 1277960 | tf_op jit(solution)/shard_map/ppermute | solution.py:30
  89.0 2.8 %collective-permute-start.46 = (bf16[32,3328]{1,0:T(8,128)(2,1)S(1)}, bf16[32,3328]{1,0:T(8,128)(2,1)S(1)}, u32[]{:S(2)}, u32[]{:S(2)}) collective-permute-start(bf16[32,3328]{1,0:T(8,128)(2,1)S(1)} %collective-permute-done.35.refs_1_), channel_id=1, source_target_pairs={{0,1},{1,0},{2,3},{3,2},{4,5},{5,4},{6,7},{7,6},{8,9},{9,8},{10,11... | collective-permute-start | bytes 638984 | tf_op jit(solution)/shard_map/ppermute | solution.py:30
  89.5 2.3 %collective-permute-start.47 = (bf16[32,3328]{1,0:T(8,128)(2,1)S(1)}, bf16[32,3328]{1,0:T(8,128)(2,1)S(1)}, u32[]{:S(2)}, u32[]{:S(2)}) collective-permute-start(bf16[32,3328]{1,0:T(8,128)(2,1)S(1)} %gated.5.refs_4_), channel_id=1, source_target_pairs={{0,1},{1,0},{2,3},{3,2},{4,5},{5,4},{6,7},{7,6},{8,9},{9,8},{10,11... | collective-permute-start | bytes 638984 | tf_op jit(solution)/shard_map/ppermute | solution.py:30
  89.6 2.7 %collective-permute-start.48 = (bf16[32,3328]{1,0:T(8,128)(2,1)S(1)}, bf16[32,3328]{1,0:T(8,128)(2,1)S(1)}, u32[]{:S(2)}, u32[]{:S(2)}) collective-permute-start(bf16[32,3328]{1,0:T(8,128)(2,1)S(1)} %collective-permute-done.44.refs_5_), channel_id=1, source_target_pairs={{0,1},{1,0},{2,3},{3,2},{4,5},{5,4},{6,7},{7,6},{8,9},{9,8},{10,11... | collective-permute-start | bytes 638984 | tf_op jit(solution)/shard_map/ppermute | solution.py:30
  90.4 11.8 %collective-permute-start.51 = (bf16[32,3328]{1,0:T(8,128)(2,1)S(1)}, bf16[32,3328]{1,0:T(8,128)(2,1)S(1)}, u32[]{:S(2)}, u32[]{:S(2)}) collective-permute-start(bf16[32,3328]{1,0:T(8,128)(2,1)S(1)} %gated.6.refs_0_), channel_id=1, source_target_pairs={{0,2},{1,3},{2,0},{3,1},{4,6},{5,7},{6,4},{7,5},{8,10},{9,11},{10,... | collective-permute-start | bytes 638984 | tf_op jit(solution)/shard_map/ppermute | solution.py:30
  91.8 11.8 %collective-permute-start.53 = (bf16[16,3328]{1,0:T(8,128)(2,1)S(1)}, bf16[16,3328]{1,0:T(8,128)(2,1)S(1)}, u32[]{:S(2)}, u32[]{:S(2)}) collective-permute-start(bf16[16,3328]{1,0:T(8,128)(2,1)S(1)} %get-tuple-element.173), channel_id=1, source_target_pairs={{0,1},{1,0},{2,3},{3,2},{4,5},{5,4},{6,7},{7,6},{8,9},{9,8},{10,11... | collective-permute-start | bytes 319496 | tf_op jit(solution)/shard_map/ppermute | solution.py:30
  91.8 11.9 %collective-permute-start.52 = (bf16[16,3328]{1,0:T(8,128)(2,1)S(1)}, bf16[16,3328]{1,0:T(8,128)(2,1)S(1)}, u32[]{:S(2)}, u32[]{:S(2)}) collective-permute-start(bf16[16,3328]{1,0:T(8,128)(2,1)S(1)} %get-tuple-element.174), channel_id=1, source_target_pairs={{0,1},{1,0},{2,3},{3,2},{4,5},{5,4},{6,7},{7,6},{8,9},{9,8},{10,11... | collective-permute-start | bytes 319496 | tf_op jit(solution)/shard_map/ppermute | solution.py:30
  98.0 11.5 %collective-permute-start.58 = (bf16[32,3328]{1,0:T(8,128)(2,1)S(1)}, bf16[32,3328]{1,0:T(8,128)(2,1)S(1)}, u32[]{:S(2)}, u32[]{:S(2)}) collective-permute-start(bf16[32,3328]{1,0:T(8,128)(2,1)S(1)} %gated.7.refs_0_), channel_id=1, source_target_pairs={{0,2},{1,3},{2,0},{3,1},{4,6},{5,7},{6,4},{7,5},{8,10},{9,11},{10,... | collective-permute-start | bytes 638984 | tf_op jit(solution)/shard_map/ppermute | solution.py:30
  99.5 10.2 %collective-permute-start.49 = (bf16[2,256,256]{2,1,0:T(8,128)(2,1)S(1)}, bf16[2,256,256]{2,1,0:T(8,128)(2,1)S(1)}, u32[]{:S(2)}, u32[]{:S(2)}) collective-permute-start(bf16[2,256,256]{2,1,0:T(8,128)(2,1)S(1)} %get-tuple-element.169), channel_id=1, source_target_pairs={{0,4},{4,0},{8,12},{12,8},{16,20},{20,16},{24,28},{28,24},{1,5},{5... | collective-permute-start | bytes 786440 | tf_op jit(solution)/shard_map/ppermute | solution.py:30
  102.2 10.2 %collective-permute-start.56 = (bf16[2,256,256]{2,1,0:T(8,128)(2,1)S(1)}, bf16[2,256,256]{2,1,0:T(8,128)(2,1)S(1)}, u32[]{:S(2)}, u32[]{:S(2)}) collective-permute-start(bf16[2,256,256]{2,1,0:T(8,128)(2,1)S(1)} %get-tuple-element.170), channel_id=1, source_target_pairs={{0,4},{4,0},{8,12},{12,8},{16,20},{20,16},{24,28},{28,24},{1,5},{5... | collective-permute-start | bytes 786440 | tf_op jit(solution)/shard_map/ppermute | solution.py:30
  105.0 8.5 %collective-permute-start.59 = (bf16[32,3328]{1,0:T(8,128)(2,1)S(1)}, bf16[32,3328]{1,0:T(8,128)(2,1)S(1)}, u32[]{:S(2)}, u32[]{:S(2)}) collective-permute-start(bf16[32,3328]{1,0:T(8,128)(2,1)S(1)} %gated.7.refs_0_), channel_id=1, source_target_pairs={{0,1},{1,0},{2,3},{3,2},{4,5},{5,4},{6,7},{7,6},{8,9},{9,8},{10,11... | collective-permute-start | bytes 638984 | tf_op jit(solution)/shard_map/ppermute | solution.py:30
  108.6 9.8 %collective-permute-start.62 = (bf16[4,128,256]{2,1,0:T(8,128)(2,1)S(1)}, bf16[4,128,256]{2,1,0:T(8,128)(2,1)S(1)}, u32[]{:S(2)}, u32[]{:S(2)}) collective-permute-start(bf16[4,128,256]{2,1,0:T(8,128)(2,1)S(1)} %get-tuple-element.130), channel_id=1, source_target_pairs={{0,8},{4,12},{8,0},{12,4},{16,24},{20,28},{24,16},{28,20},{1,9},{5... | collective-permute-start | bytes 786440 | tf_op jit(solution)/shard_map/ppermute | solution.py:30
  109.6 3.9 %collective-permute-start.60 = (bf16[32,3328]{1,0:T(8,128)(2,1)S(1)}, bf16[32,3328]{1,0:T(8,128)(2,1)S(1)}, u32[]{:S(2)}, u32[]{:S(2)}) collective-permute-start(bf16[32,3328]{1,0:T(8,128)(2,1)S(1)} %collective-permute-done.58.refs_1_), channel_id=1, source_target_pairs={{0,1},{1,0},{2,3},{3,2},{4,5},{5,4},{6,7},{7,6},{8,9},{9,8},{10,11... | collective-permute-start | bytes 638984 | tf_op jit(solution)/shard_map/ppermute | solution.py:30
  112.6 10.3 %collective-permute-start.57 = (bf16[2,256,256]{2,1,0:T(8,128)(2,1)S(1)}, bf16[2,256,256]{2,1,0:T(8,128)(2,1)S(1)}, u32[]{:S(2)}, u32[]{:S(2)}) collective-permute-start(bf16[2,256,256]{2,1,0:T(8,128)(2,1)S(1)} %get-tuple-element.168), channel_id=1, source_target_pairs={{0,8},{4,12},{8,0},{12,4},{16,24},{20,28},{24,16},{28,20},{1,9},{5... | collective-permute-start | bytes 786440 | tf_op jit(solution)/shard_map/ppermute | solution.py:30
  117.0 12.0 %collective-permute-start.65 = (bf16[4,128,256]{2,1,0:T(8,128)(2,1)S(1)}, bf16[4,128,256]{2,1,0:T(8,128)(2,1)S(1)}, u32[]{:S(2)}, u32[]{:S(2)}) collective-permute-start(bf16[4,128,256]{2,1,0:T(8,128)(2,1)S(1)} %get-tuple-element.134), channel_id=1, source_target_pairs={{0,4},{4,0},{8,12},{12,8},{16,20},{20,16},{24,28},{28,24},{1,5},{5... | collective-permute-start | bytes 786440 | tf_op jit(solution)/shard_map/ppermute | solution.py:30
  118.6 7.3 %collective-permute-start.63 = (bf16[2,128,256]{2,1,0:T(8,128)(2,1)S(1)}, bf16[2,128,256]{2,1,0:T(8,128)(2,1)S(1)}, u32[]{:S(2)}, u32[]{:S(2)}) collective-permute-start(bf16[2,128,256]{2,1,0:T(8,128)(2,1)S(1)} %slice.199), channel_id=1, source_target_pairs={{0,4},{4,0},{8,12},{12,8},{16,20},{20,16},{24,28},{28,24},{1,5},{5... | collective-permute-start | bytes 393224 | tf_op jit(solution)/shard_map/ppermute | solution.py:30
  123.0 13.6 %collective-permute-start.61 = (bf16[1,256,256]{2,1,0:T(8,128)(2,1)S(1)}, bf16[1,256,256]{2,1,0:T(8,128)(2,1)S(1)}, u32[]{:S(2)}, u32[]{:S(2)}) collective-permute-start(bf16[1,256,256]{2,1,0:T(8,128)(2,1)S(1)} %slice.197), channel_id=1, source_target_pairs={{0,16},{4,20},{8,24},{12,28},{16,0},{20,4},{24,8},{28,12},{1,17},{... | collective-permute-start | bytes 393224 | tf_op jit(solution)/shard_map/ppermute | solution.py:30
  126.0 8.7 %collective-permute-start.64 = (bf16[1,128,256]{2,1,0:T(8,128)(2,1)S(1)}, bf16[1,128,256]{2,1,0:T(8,128)(2,1)S(1)}, u32[]{:S(2)}, u32[]{:S(2)}) collective-permute-start(bf16[1,128,256]{2,1,0:T(8,128)(2,1)S(1)} %slice.201), channel_id=1, source_target_pairs={{0,16},{4,20},{8,24},{12,28},{16,0},{20,4},{24,8},{28,12},{1,17},{... | collective-permute-start | bytes 196616 | tf_op jit(solution)/shard_map/ppermute | solution.py:30
  129.0 6.9 %collective-permute-start.66 = (bf16[2,128,256]{2,1,0:T(8,128)(2,1)S(1)}, bf16[2,128,256]{2,1,0:T(8,128)(2,1)S(1)}, u32[]{:S(2)}, u32[]{:S(2)}) collective-permute-start(bf16[2,128,256]{2,1,0:T(8,128)(2,1)S(1)} %slice.203), channel_id=1, source_target_pairs={{0,8},{4,12},{8,0},{12,4},{16,24},{20,28},{24,16},{28,20},{1,9},{5... | collective-permute-start | bytes 393224 | tf_op jit(solution)/shard_map/ppermute | solution.py:30
  136.0 5.4 %collective-permute-start.67 = (bf16[1,128,256]{2,1,0:T(8,128)(2,1)S(1)}, bf16[1,128,256]{2,1,0:T(8,128)(2,1)S(1)}, u32[]{:S(2)}, u32[]{:S(2)}) collective-permute-start(bf16[1,128,256]{2,1,0:T(8,128)(2,1)S(1)} %slice.205), channel_id=1, source_target_pairs={{0,16},{4,20},{8,24},{12,28},{16,0},{20,4},{24,8},{28,12},{1,17},{... | collective-permute-start | bytes 196616 | tf_op jit(solution)/shard_map/ppermute | solution.py:30
  (25 other events, 70.7 us)

commit v3 on v2

--- a/solution.py
+++ b/solution.py
@@ -52,8 +52,9 @@
     return pl.CostEstimate(flops=size, bytes_accessed=size, transcendentals=0)
 
 
-def decode_kernel(first, block, w_ref, sc_ref, out_ref, arrived):
+def decode_kernel(first, block, w_ref, sc_ref, out_ref, scale_ref, arrived, scaled):
     size = out_ref.shape[0]
+    scales = pltpu.make_async_copy(sc_ref, scale_ref, scaled)
 
     def fetch(k):
         return pltpu.make_async_copy(
@@ -61,30 +62,37 @@
         )
 
     count = size // block
+    scales.start()
     for k in range(count):
         fetch(k).start()
+    scales.wait()
     for k in range(count):
         fetch(k).wait()
         for g in range(k * block // GROUP, (k + 1) * block // GROUP):
             rows = slice(g * GROUP, (g + 1) * GROUP)
-            out_ref[rows] = out_ref[rows] * sc_ref[first // GROUP + g : first // GROUP + g + 1].astype(jnp.bfloat16)
+            scale = scale_ref[first // GROUP + g : first // GROUP + g + 1]
+            out_ref[rows] = out_ref[rows] * scale.astype(jnp.bfloat16)
 
 
 def decode_part(codes, scales, part, parts):
     depth, units = codes.shape
     size = depth // parts
     block = 256 if size % 256 == 0 else GROUP
-    vmem = pl.BlockSpec(memory_space=pltpu.VMEM)
+    hbm = pl.BlockSpec(memory_space=pl.ANY)
     return pl.pallas_call(
         functools.partial(decode_kernel, part * size, block),
-        in_specs=[pl.BlockSpec(memory_space=pl.ANY), vmem],
-        out_specs=vmem,
+        in_specs=[hbm, hbm],
+        out_specs=pl.BlockSpec(memory_space=pltpu.VMEM),
         out_shape=pltpu.VMEM((size, units), jnp.bfloat16),
-        scratch_shapes=[pltpu.SemaphoreType.DMA((size // block,))],
+        scratch_shapes=[
+            pltpu.VMEM(scales.shape, jnp.float32),
+            pltpu.SemaphoreType.DMA((size // block,)),
+            pltpu.SemaphoreType.DMA,
+        ],
         compiler_params=pltpu.CompilerParams(vmem_limit_bytes=6 * MIB),
         cost_estimate=cost(),
         name="decode",
-    )(in_hbm(codes), scales)
+    )(in_hbm(codes), in_hbm(scales))
 
 
 def gate_up_kernel(n_tok, n_gate, n_up, place_ref, *refs):
@@ -401,14 +409,16 @@
             gather_tokens(k, wide_bits - 1, gate[0])
         gate.append(decode_part(after(gw, gate[0], tok[0][0]), gs, 1, 2))
         for k in (2, 3):
-            gather_tokens(k, wide_bits - 1, gate[1])
+            tok[k] = [after(tok[k][0], tok[0][0])]
         for k in (0, 1):
             gather_tokens(k, 1, gate[1])
         up = [decode_part(after(uw, tok[0][0], tok[1][0]), us, 0, 1)]
         for k in (2, 3):
-            gather_tokens(k, 1, up[0])
+            gather_tokens(k, wide_bits - 1, up[0])
         gather_tokens(0, 0, up[0])
         products(0)
+        for k in (2, 3):
+            gather_tokens(k, 1, send[0])
         gather_tokens(1, 0, send[0])
         send[0] = after(send[0], tok[1][1], tok[2][0], tok[3][0])
         tok[2], tok[3] = [after(tok[2][0], send[0])], [after(tok[3][0], send[0])]
@@ -439,7 +449,10 @@
         finish(3, down_w, *parts[0])
         scatter(0, wide_bits - 2, parts[3][1])
         scatter(2, wide_bits - 1, parts[3][1])
-        for k in (0, 2, 3):
+        scatter(3, wide_bits - 1)
+        for k in (0, 2):
+            parts[k] = tuple(after(p, parts[3][1]) for p in parts[k])
+        for k in (3, 0, 2):
             scatter(k, 0)
         parts = [parts[0], parts[2], parts[3]]
     outs = [part[0].reshape(-1, n_nar, cuts[0] // n_nar, width) for part in parts]
@@ -451,7 +464,7 @@
 
     def local(tokens, *weights):
         rows = tokens.shape[0]
-        cuts = (128,) * (rows // 128) if 128 // n_nar >= 16 else (rows,)
+        cuts = (128,) * (rows // 128) if rows % 128 == 0 and 128 // n_nar >= 16 else (rows,)
         return on_device(n_wide, n_nar, cuts, tokens, *weights)
 
     in_specs = (

time: 142 us -> 139 us (0.979)
  waiting for transfers between devices: 33.6 us -> 25.4 us
  starting transfers between devices: 47.1 us -> 51.1 us
  Pallas kernels: 57.9 us -> 59.4 us
    ppermute x68, waiting for transfers between devices: 33.6 us -> 25.4 us  [flip(): return lax.ppermute(array, axis, [(i, i ^ mask) for i in range(size)])]
    ppermute x68, starting transfers between devices: 47.1 us -> 51.1 us  [flip(): return lax.ppermute(array, axis, [(i, i ^ mask) for i in range(size)])]
    pallas_call x5, Pallas kernels: 17.7 us -> 19.2 us  [decode_part(): pl.pallas_call(functools.partial(decode_kernel, part * size, block), in_s...]
  transfers between devices with their start and end apart: 68 -> 68, of which waited for: 33 -> 35; matrix products, arithmetic and copies ran while one was open for 1% -> 1% of each run, Pallas kernels for 40% -> 42%
where the time goes in v3:
time: 139 us; the launch traced here: 138 us
  Pallas kernels  59.4 us (43%)
  starting transfers between devices  51.1 us (37%)
  waiting for transfers between devices  25.4 us (18%)
    ppermute x68, starting transfers between devices, flip(): return lax.ppermute(array, axis, [(i, i ^ mask) for i in range(size)])  51.1 us
    ppermute x68, waiting for transfers between devices, flip(): return lax.ppermute(array, axis, [(i, i ^ mask) for i in range(size)])  25.4 us
    pallas_call x4, Pallas kernels, gate_up(): pl.pallas_call(functools.partial(gate_up_kernel, len(shards), len(gate),...  24.6 us
    pallas_call x5, Pallas kernels, decode_part(): pl.pallas_call(functools.partial(decode_kernel, part * size, block), in_s...  19.2 us
    pallas_call x3, Pallas kernels, down(): pl.pallas_call(functools.partial(down_kernel, len(hidden), len(weights),...  12.3 us
  transfers between devices with their start and end apart: 68, of which 35 were waited for; matrix products, arithmetic and copies ran while one was open for 1% of the time, Pallas kernels for 42%

profile of v3, /device:TPU:0, one launch (start us, length us, event | category | flops | bytes accessed | tf_op | source)
XLA Modules:
  0.0 138.4 jit_solution(6317645665234720066)
XLA Ops:
  0.0 0.9 copy-done
  1.0 4.1 %collective-permute-start = (bf16[1,128,256]{2,1,0:T(8,128)(2,1)S(1)}, bf16[1,128,256]{2,1,0:T(8,128)(2,1)S(1)}, u32[]{:S(2)}, u32[]{:S(2)}) collective-permute-start(bf16[1,128,256]{2,1,0:T(8,128)(2,1)S(1)} %bitcast.23), channel_id=1, source_target_pairs={{0,16},{4,20},{8,24},{12,28},{16,0},{20,4},{24,8},{28,12},{1,17},{... | collective-permute-start | bytes 196616 | tf_op jit(solution)/shard_map/ppermute | solution.py:30
  5.2 3.2 %decode.5.refs_2_ = bf16[1024,3328]{1,0:T(8,128)(2,1)S(1)} custom-call(bf16[2048,3328]{1,0:T(8,128)(2,1)} %w_ref.1, f32[16,3328]{1,0:T(8,128)} %sc_ref.6), custom_call_target="tpu_custom_call" | custom-call | flops 1024 | bytes 1024 | tf_op jit(solution)/shard_map/decode/pallas_call | solution.py:82
  8.7 2.1 %collective-permute-start.1 = (bf16[2,128,256]{2,1,0:T(8,128)(2,1)S(1)}, bf16[2,128,256]{2,1,0:T(8,128)(2,1)S(1)}, u32[]{:S(2)}, u32[]{:S(2)}) collective-permute-start(bf16[2,128,256]{2,1,0:T(8,128)(2,1)S(1)} %pad_maximum_fusion.2), channel_id=1, source_target_pairs={{0,8},{4,12},{8,0},{12,4},{16,24},{20,28},{24,16},{28,20},{1,9},{5... | collective-permute-start | bytes 393224 | tf_op jit(solution)/shard_map/ppermute | solution.py:30
  11.5 2.7 %collective-permute-start.6 = (bf16[1,128,256]{2,1,0:T(8,128)(2,1)S(1)}, bf16[1,128,256]{2,1,0:T(8,128)(2,1)S(1)}, u32[]{:S(2)}, u32[]{:S(2)}) collective-permute-start(bf16[1,128,256]{2,1,0:T(8,128)(2,1)S(1)} %bitcast.29), channel_id=1, source_target_pairs={{0,16},{4,20},{8,24},{12,28},{16,0},{20,4},{24,8},{28,12},{1,17},{... | collective-permute-start | bytes 196616 | tf_op jit(solution)/shard_map/ppermute | solution.py:30
  14.3 1.3 collective-permute-start.4
  15.6 3.2 %decode.6.refs_3_ = bf16[1024,3328]{1,0:T(8,128)(2,1)S(1)} custom-call(bf16[2048,3328]{1,0:T(8,128)(2,1)} %w_ref.1, f32[16,3328]{1,0:T(8,128)} %sc_ref.6), custom_call_target="tpu_custom_call" | custom-call | flops 1024 | bytes 1024 | tf_op jit(solution)/shard_map/decode/pallas_call | solution.py:82
  18.8 2.1 %collective-permute-done.4 = bf16[2,128,256]{2,1,0:T(8,128)(2,1)S(1)} collective-permute-done((bf16[2,128,256]{2,1,0:T(8,128)(2,1)S(1)}, bf16[2,128,256]{2,1,0:T(8,128)(2,1)S(1)}, u32[]{:S(2)}, u32[]{:S(2)}) %collective-permute-start.4) | collective-permute-done | bytes 131104 | tf_op jit(solution)/shard_map/ppermute | solution.py:30
  21.0 1.8 %collective-permute-start.2 = (bf16[4,128,256]{2,1,0:T(8,128)(2,1)S(1)}, bf16[4,128,256]{2,1,0:T(8,128)(2,1)S(1)}, u32[]{:S(2)}, u32[]{:S(2)}) collective-permute-start(bf16[4,128,256]{2,1,0:T(8,128)(2,1)S(1)} %get-tuple-element.191.refs_0_), channel_id=1, source_target_pairs={{0,4},{4,0},{8,12},{12,8},{16,20},{20,16},{24,28},{28,24},{1,5},{5... | collective-permute-start | bytes 786440 | tf_op jit(solution)/shard_map/ppermute | solution.py:30
  23.1 5.6 %decode.7.refs_4_ = bf16[2048,3328]{1,0:T(8,128)(2,1)S(1)} custom-call(bf16[2048,3328]{1,0:T(8,128)(2,1)} %w_ref.2, f32[16,3328]{1,0:T(8,128)} %sc_ref.7), custom_call_target="tpu_custom_call" | custom-call | flops 1024 | bytes 1024 | tf_op jit(solution)/shard_map/decode/pallas_call | solution.py:82
  28.7 1.1 collective-permute-start.7
  29.8 1.0 collective-permute-start.9
  30.8 6.3 %gate_up.4 = (bf16[2,2,32,3328]{3,2,1,0:T(8,128)(2,1)S(1)}, bf16[2,2,32,3328]{3,2,1,0:T(8,128)(2,1)S(1)}) custom-call(s32[1]{0:T(128)} %bitcast.1.place_ref, bf16[4,128,256]{2,1,0:T(8,128)(2,1)S(1)} %get-tuple-element.191.refs_0_, bf16[4,128,256]{2,1,0:T(8,128)(2,1)S(1)} %collective-permute-done.2.refs_1_, bf16[1024,3328]{1,0:T(8,128)(2,1)S(1)} %decode.5.refs_2_, ...), custom_call_target="tpu_custom_call" | custom-call | flops 1024 | bytes 1024 | tf_op jit(solution)/shard_map/gate_up/pallas_call | solution.py:149
  37.2 1.8 %collective-permute-start.15 = (bf16[4,128,256]{2,1,0:T(8,128)(2,1)S(1)}, bf16[4,128,256]{2,1,0:T(8,128)(2,1)S(1)}, u32[]{:S(2)}, u32[]{:S(2)}) collective-permute-start(bf16[4,128,256]{2,1,0:T(8,128)(2,1)S(1)} %constant_dynamic-update-slice_fusion.refs_0_), channel_id=1, source_target_pairs={{0,4},{4,0},{8,12},{12,8},{16,20},{20,16},{24,28},{28,24},{1,5},{5... | collective-permute-start | bytes 786440 | tf_op jit(solution)/shard_map/ppermute | solution.py:30
  41.8 1.6 %collective-permute-start.14 = (bf16[1,2,32,3328]{3,2,1,0:T(8,128)(2,1)S(1)}, bf16[1,2,32,3328]{3,2,1,0:T(8,128)(2,1)S(1)}, u32[]{:S(2)}, u32[]{:S(2)}) collective-permute-start(bf16[1,2,32,3328]{3,2,1,0:T(8,128)(2,1)S(1)} %get-tuple-element.102), channel_id=1, source_target_pairs={{0,2},{1,3},{2,0},{3,1},{4,6},{5,7},{6,4},{7,5},{8,10},{9,11},{10,... | collective-permute-start | bytes 1277960 | tf_op jit(solution)/shard_map/ppermute | solution.py:30
  43.3 6.1 %gate_up.5 = (bf16[2,2,32,3328]{3,2,1,0:T(8,128)(2,1)S(1)}, bf16[2,2,32,3328]{3,2,1,0:T(8,128)(2,1)S(1)}) custom-call(s32[1]{0:T(128)} %bitcast.1.place_ref, bf16[4,128,256]{2,1,0:T(8,128)(2,1)S(1)} %get-tuple-element.103.refs_0_, bf16[4,128,256]{2,1,0:T(8,128)(2,1)S(1)} %collective-permute-done.5.refs_1_, bf16[1024,3328]{1,0:T(8,128)(2,1)S(1)} %decode.5.refs_2_, ...), custom_call_target="tpu_custom_call" | custom-call | flops 1024 | bytes 1024 | tf_op jit(solution)/shard_map/gate_up/pallas_call | solution.py:149
  55.0 6.1 %gate_up.6 = (bf16[2,2,32,3328]{3,2,1,0:T(8,128)(2,1)S(1)}, bf16[2,2,32,3328]{3,2,1,0:T(8,128)(2,1)S(1)}) custom-call(s32[1]{0:T(128)} %bitcast.1.place_ref, bf16[4,128,256]{2,1,0:T(8,128)(2,1)S(1)} %constant_dynamic-update-slice_fusion.refs_0_, bf16[4,128,256]{2,1,0:T(8,128)(2,1)S(1)} %collective-permute-done.15.refs_1_, ...), custom_call_target="tpu_custom_call" | custom-call | flops 1024 | bytes 1024 | tf_op jit(solution)/shard_map/gate_up/pallas_call | solution.py:149
  62.7 1.6 %collective-permute-start.35 = (bf16[32,3328]{1,0:T(8,128)(2,1)S(1)}, bf16[32,3328]{1,0:T(8,128)(2,1)S(1)}, u32[]{:S(2)}, u32[]{:S(2)}) collective-permute-start(bf16[32,3328]{1,0:T(8,128)(2,1)S(1)} %gated.4.refs_0_), channel_id=1, source_target_pairs={{0,2},{1,3},{2,0},{3,1},{4,6},{5,7},{6,4},{7,5},{8,10},{9,11},{10,... | collective-permute-start | bytes 638984 | tf_op jit(solution)/shard_map/ppermute | solution.py:30
  64.8 0.7 collective-permute-done.27.refs_2_
  66.3 0.7 collective-permute-start.33
  67.0 3.6 %decode.8.refs_8_.refs_6_.refs_4_ = bf16[1664,2048]{1,0:T(8,128)(2,1)S(1)} custom-call(bf16[3328,2048]{1,0:T(8,128)(2,1)} %w_ref.4, f32[26,2048]{1,0:T(8,128)} %sc_ref.9), custom_call_target="tpu_custom_call" | custom-call | flops 1024 | bytes 1024 | tf_op jit(solution)/shard_map/decode/pallas_call | solution.py:82
  71.4 6.1 %gate_up.7 = (bf16[2,2,32,3328]{3,2,1,0:T(8,128)(2,1)S(1)}, bf16[2,2,32,3328]{3,2,1,0:T(8,128)(2,1)S(1)}) custom-call(s32[1]{0:T(128)} %bitcast.1.place_ref, bf16[4,128,256]{2,1,0:T(8,128)(2,1)S(1)} %constant_dynamic-update-slice_fusion.3.refs_0_, bf16[4,128,256]{2,1,0:T(8,128)(2,1)S(1)} %collective-permute-done.24.refs_1_, ...), custom_call_target="tpu_custom_call" | custom-call | flops 1024 | bytes 1024 | tf_op jit(solution)/shard_map/gate_up/pallas_call | solution.py:149
  79.1 1.3 collective-permute-start.44
  81.0 0.7 collective-permute-done.38.refs_2_
  82.6 0.8 collective-permute-start.50
  83.3 3.6 %decode.9.refs_9_.refs_7_.refs_5_ = bf16[1664,2048]{1,0:T(8,128)(2,1)S(1)} custom-call(bf16[3328,2048]{1,0:T(8,128)(2,1)} %w_ref.4, f32[26,2048]{1,0:T(8,128)} %sc_ref.9), custom_call_target="tpu_custom_call" | custom-call | flops 1024 | bytes 1024 | tf_op jit(solution)/shard_map/decode/pallas_call | solution.py:82
  89.1 1.3 collective-permute-start.51
  91.0 5.3 %down.3 = (bf16[4,256,256]{2,1,0:T(8,128)(2,1)S(1)}, bf16[4,256,256]{2,1,0:T(8,128)(2,1)S(1)}) custom-call(s32[1]{0:T(128)} %bitcast.1.place_ref, bf16[32,3328]{1,0:T(8,128)(2,1)S(1)} %gated.4.refs_0_, bf16[32,3328]{1,0:T(8,128)(2,1)S(1)} %collective-permute-done.35.refs_1_, bf16[32,3328]{1,0:T(8,128)(2,1)S(1)} %collective-permute-done.45.refs_2_, ...), custom_call_target="tpu_custom_call" | custom-call | flops 1024 | bytes 1024 | tf_op jit(solution)/shard_map/down/pallas_call | solution.py:196
  96.7 1.4 collective-permute-start.58
  98.1 1.6 %collective-permute-start.49 = (bf16[2,256,256]{2,1,0:T(8,128)(2,1)S(1)}, bf16[2,256,256]{2,1,0:T(8,128)(2,1)S(1)}, u32[]{:S(2)}, u32[]{:S(2)}) collective-permute-start(bf16[2,256,256]{2,1,0:T(8,128)(2,1)S(1)} %get-tuple-element.181), channel_id=1, source_target_pairs={{0,4},{4,0},{8,12},{12,8},{16,20},{20,16},{24,28},{28,24},{1,5},{5... | collective-permute-start | bytes 786440 | tf_op jit(solution)/shard_map/ppermute | solution.py:30
  99.7 1.2 collective-permute-done.51.refs_1_
  100.9 1.3 collective-permute-start.56
  102.9 0.8 collective-permute-done.55.refs_5_
  103.8 3.5 %down.4 = (bf16[4,128,256]{2,1,0:T(8,128)(2,1)S(1)}, bf16[4,128,256]{2,1,0:T(8,128)(2,1)S(1)}) custom-call(s32[1]{0:T(128)} %bitcast.1.place_ref, bf16[32,3328]{1,0:T(8,128)(2,1)S(1)} %gated.6.refs_0_, bf16[32,3328]{1,0:T(8,128)(2,1)S(1)} %collective-permute-done.51.refs_1_, bf16[16,3328]{1,0:T(8,128)(2,1)S(1)} %collective-permute-done.52.refs_2_, ...), custom_call_target="tpu_custom_call" | custom-call | flops 1024 | bytes 1024 | tf_op jit(solution)/shard_map/down/pallas_call | solution.py:196
  107.3 0.9 collective-permute-start.63
  108.7 2.4 %collective-permute-done.56 = bf16[2,256,256]{2,1,0:T(8,128)(2,1)S(1)} collective-permute-done((bf16[2,256,256]{2,1,0:T(8,128)(2,1)S(1)}, bf16[2,256,256]{2,1,0:T(8,128)(2,1)S(1)}, u32[]{:S(2)}, u32[]{:S(2)}) %collective-permute-start.56) | collective-permute-done | bytes 262176 | tf_op jit(solution)/shard_map/ppermute | solution.py:30
  111.3 0.8 collective-permute-start.57
  112.2 3.5 %down.5 = (bf16[4,128,256]{2,1,0:T(8,128)(2,1)S(1)}, bf16[4,128,256]{2,1,0:T(8,128)(2,1)S(1)}) custom-call(s32[1]{0:T(128)} %bitcast.1.place_ref, bf16[32,3328]{1,0:T(8,128)(2,1)S(1)} %gated.7.refs_0_, bf16[32,3328]{1,0:T(8,128)(2,1)S(1)} %collective-permute-done.58.refs_1_, bf16[32,3328]{1,0:T(8,128)(2,1)S(1)} %collective-permute-done.59.refs_2_, ...), custom_call_target="tpu_custom_call" | custom-call | flops 1024 | bytes 1024 | tf_op jit(solution)/shard_map/down/pallas_call | solution.py:196
  115.7 1.4 %collective-permute-start.61 = (bf16[4,128,256]{2,1,0:T(8,128)(2,1)S(1)}, bf16[4,128,256]{2,1,0:T(8,128)(2,1)S(1)}, u32[]{:S(2)}, u32[]{:S(2)}) collective-permute-start(bf16[4,128,256]{2,1,0:T(8,128)(2,1)S(1)} %get-tuple-element.142), channel_id=1, source_target_pairs={{0,4},{4,0},{8,12},{12,8},{16,20},{20,16},{24,28},{28,24},{1,5},{5... | collective-permute-start | bytes 786440 | tf_op jit(solution)/shard_map/ppermute | solution.py:30
  117.2 4.3 %collective-permute-done.57 = bf16[2,256,256]{2,1,0:T(8,128)(2,1)S(1)} collective-permute-done((bf16[2,256,256]{2,1,0:T(8,128)(2,1)S(1)}, bf16[2,256,256]{2,1,0:T(8,128)(2,1)S(1)}, u32[]{:S(2)}, u32[]{:S(2)}) %collective-permute-start.57) | collective-permute-done | bytes 262176 | tf_op jit(solution)/shard_map/ppermute | solution.py:30
  122.2 1.4 %collective-permute-start.64 = (bf16[2,128,256]{2,1,0:T(8,128)(2,1)S(1)}, bf16[2,128,256]{2,1,0:T(8,128)(2,1)S(1)}, u32[]{:S(2)}, u32[]{:S(2)}) collective-permute-start(bf16[2,128,256]{2,1,0:T(8,128)(2,1)S(1)} %get-tuple-element.150), channel_id=1, source_target_pairs={{0,4},{4,0},{8,12},{12,8},{16,20},{20,16},{24,28},{28,24},{1,5},{5... | collective-permute-start | bytes 393224 | tf_op jit(solution)/shard_map/ppermute | solution.py:30
  123.7 1.3 collective-permute-start.66
  125.0 2.1 %collective-permute-start.62 = (bf16[1,256,256]{2,1,0:T(8,128)(2,1)S(1)}, bf16[1,256,256]{2,1,0:T(8,128)(2,1)S(1)}, u32[]{:S(2)}, u32[]{:S(2)}) collective-permute-start(bf16[1,256,256]{2,1,0:T(8,128)(2,1)S(1)} %get-tuple-element.146), channel_id=1, source_target_pairs={{0,16},{4,20},{8,24},{12,28},{16,0},{20,4},{24,8},{28,12},{1,17},{... | collective-permute-start | bytes 393224 | tf_op jit(solution)/shard_map/ppermute | solution.py:30
  127.3 3.3 %collective-permute-start.65 = (bf16[1,128,256]{2,1,0:T(8,128)(2,1)S(1)}, bf16[1,128,256]{2,1,0:T(8,128)(2,1)S(1)}, u32[]{:S(2)}, u32[]{:S(2)}) collective-permute-start(bf16[1,128,256]{2,1,0:T(8,128)(2,1)S(1)} %slice.202), channel_id=1, source_target_pairs={{0,16},{4,20},{8,24},{12,28},{16,0},{20,4},{24,8},{28,12},{1,17},{... | collective-permute-start | bytes 196616 | tf_op jit(solution)/shard_map/ppermute | solution.py:30
  130.6 1.8 %collective-permute-start.67 = (bf16[1,128,256]{2,1,0:T(8,128)(2,1)S(1)}, bf16[1,128,256]{2,1,0:T(8,128)(2,1)S(1)}, u32[]{:S(2)}, u32[]{:S(2)}) collective-permute-start(bf16[1,128,256]{2,1,0:T(8,128)(2,1)S(1)} %slice.205), channel_id=1, source_target_pairs={{0,16},{4,20},{8,24},{12,28},{16,0},{20,4},{24,8},{28,12},{1,17},{... | collective-permute-start | bytes 196616 | tf_op jit(solution)/shard_map/ppermute | solution.py:30
  132.4 3.8 %collective-permute-done.62 = bf16[1,256,256]{2,1,0:T(8,128)(2,1)S(1)} collective-permute-done((bf16[1,256,256]{2,1,0:T(8,128)(2,1)S(1)}, bf16[1,256,256]{2,1,0:T(8,128)(2,1)S(1)}, u32[]{:S(2)}, u32[]{:S(2)}) %collective-permute-start.62) | collective-permute-done | bytes 131104 | tf_op jit(solution)/shard_map/ppermute | solution.py:30
  137.0 0.7 collective-permute-done.67
  137.7 0.7 collect.1
  (144 shorter events, 22.8 us)
Async XLA Ops:
  1.0 7.8 %collective-permute-start = (bf16[1,128,256]{2,1,0:T(8,128)(2,1)S(1)}, bf16[1,128,256]{2,1,0:T(8,128)(2,1)S(1)}, u32[]{:S(2)}, u32[]{:S(2)}) collective-permute-start(bf16[1,128,256]{2,1,0:T(8,128)(2,1)S(1)} %bitcast.23), channel_id=1, source_target_pairs={{0,16},{4,20},{8,24},{12,28},{16,0},{20,4},{24,8},{28,12},{1,17},{... | collective-permute-start | bytes 196616 | tf_op jit(solution)/shard_map/ppermute | solution.py:30
  5.1 6.5 %collective-permute-start.3 = (bf16[1,128,256]{2,1,0:T(8,128)(2,1)S(1)}, bf16[1,128,256]{2,1,0:T(8,128)(2,1)S(1)}, u32[]{:S(2)}, u32[]{:S(2)}) collective-permute-start(bf16[1,128,256]{2,1,0:T(8,128)(2,1)S(1)} %bitcast.26), channel_id=1, source_target_pairs={{0,16},{4,20},{8,24},{12,28},{16,0},{20,4},{24,8},{28,12},{1,17},{... | collective-permute-start | bytes 196616 | tf_op jit(solution)/shard_map/ppermute | solution.py:30
  8.7 12.2 %collective-permute-start.1 = (bf16[2,128,256]{2,1,0:T(8,128)(2,1)S(1)}, bf16[2,128,256]{2,1,0:T(8,128)(2,1)S(1)}, u32[]{:S(2)}, u32[]{:S(2)}) collective-permute-start(bf16[2,128,256]{2,1,0:T(8,128)(2,1)S(1)} %pad_maximum_fusion.2), channel_id=1, source_target_pairs={{0,8},{4,12},{8,0},{12,4},{16,24},{20,28},{24,16},{28,20},{1,9},{5... | collective-permute-start | bytes 393224 | tf_op jit(solution)/shard_map/ppermute | solution.py:30
  11.5 17.1 %collective-permute-start.6 = (bf16[1,128,256]{2,1,0:T(8,128)(2,1)S(1)}, bf16[1,128,256]{2,1,0:T(8,128)(2,1)S(1)}, u32[]{:S(2)}, u32[]{:S(2)}) collective-permute-start(bf16[1,128,256]{2,1,0:T(8,128)(2,1)S(1)} %bitcast.29), channel_id=1, source_target_pairs={{0,16},{4,20},{8,24},{12,28},{16,0},{20,4},{24,8},{28,12},{1,17},{... | collective-permute-start | bytes 196616 | tf_op jit(solution)/shard_map/ppermute | solution.py:30
  14.3 6.6 %collective-permute-start.4 = (bf16[2,128,256]{2,1,0:T(8,128)(2,1)S(1)}, bf16[2,128,256]{2,1,0:T(8,128)(2,1)S(1)}, u32[]{:S(2)}, u32[]{:S(2)}) collective-permute-start(bf16[2,128,256]{2,1,0:T(8,128)(2,1)S(1)} %pad_maximum_fusion.3), channel_id=1, source_target_pairs={{0,8},{4,12},{8,0},{12,4},{16,24},{20,28},{24,16},{28,20},{1,9},{5... | collective-permute-start | bytes 393224 | tf_op jit(solution)/shard_map/ppermute | solution.py:30
  15.6 13.1 %collective-permute-start.8 = (bf16[1,128,256]{2,1,0:T(8,128)(2,1)S(1)}, bf16[1,128,256]{2,1,0:T(8,128)(2,1)S(1)}, u32[]{:S(2)}, u32[]{:S(2)}) collective-permute-start(bf16[1,128,256]{2,1,0:T(8,128)(2,1)S(1)} %bitcast.32), channel_id=1, source_target_pairs={{0,16},{4,20},{8,24},{12,28},{16,0},{20,4},{24,8},{28,12},{1,17},{... | collective-permute-start | bytes 196616 | tf_op jit(solution)/shard_map/ppermute | solution.py:30
  21.0 9.8 %collective-permute-start.2 = (bf16[4,128,256]{2,1,0:T(8,128)(2,1)S(1)}, bf16[4,128,256]{2,1,0:T(8,128)(2,1)S(1)}, u32[]{:S(2)}, u32[]{:S(2)}) collective-permute-start(bf16[4,128,256]{2,1,0:T(8,128)(2,1)S(1)} %get-tuple-element.191.refs_0_), channel_id=1, source_target_pairs={{0,4},{4,0},{8,12},{12,8},{16,20},{20,16},{24,28},{28,24},{1,5},{5... | collective-permute-start | bytes 786440 | tf_op jit(solution)/shard_map/ppermute | solution.py:30
  22.8 14.4 %collective-permute-start.5 = (bf16[4,128,256]{2,1,0:T(8,128)(2,1)S(1)}, bf16[4,128,256]{2,1,0:T(8,128)(2,1)S(1)}, u32[]{:S(2)}, u32[]{:S(2)}) collective-permute-start(bf16[4,128,256]{2,1,0:T(8,128)(2,1)S(1)} %get-tuple-element.103.refs_0_), channel_id=1, source_target_pairs={{0,4},{4,0},{8,12},{12,8},{16,20},{20,16},{24,28},{28,24},{1,5},{5... | collective-permute-start | bytes 786440 | tf_op jit(solution)/shard_map/ppermute | solution.py:30
  28.7 8.4 %collective-permute-start.7 = (bf16[2,128,256]{2,1,0:T(8,128)(2,1)S(1)}, bf16[2,128,256]{2,1,0:T(8,128)(2,1)S(1)}, u32[]{:S(2)}, u32[]{:S(2)}) collective-permute-start(bf16[2,128,256]{2,1,0:T(8,128)(2,1)S(1)} %pad_maximum_fusion.4), channel_id=1, source_target_pairs={{0,8},{4,12},{8,0},{12,4},{16,24},{20,28},{24,16},{28,20},{1,9},{5... | collective-permute-start | bytes 393224 | tf_op jit(solution)/shard_map/ppermute | solution.py:30
  29.8 7.3 %collective-permute-start.9 = (bf16[2,128,256]{2,1,0:T(8,128)(2,1)S(1)}, bf16[2,128,256]{2,1,0:T(8,128)(2,1)S(1)}, u32[]{:S(2)}, u32[]{:S(2)}) collective-permute-start(bf16[2,128,256]{2,1,0:T(8,128)(2,1)S(1)} %pad_maximum_fusion.5), channel_id=1, source_target_pairs={{0,8},{4,12},{8,0},{12,4},{16,24},{20,28},{24,16},{28,20},{1,9},{5... | collective-permute-start | bytes 393224 | tf_op jit(solution)/shard_map/ppermute | solution.py:30
  37.2 12.2 %collective-permute-start.15 = (bf16[4,128,256]{2,1,0:T(8,128)(2,1)S(1)}, bf16[4,128,256]{2,1,0:T(8,128)(2,1)S(1)}, u32[]{:S(2)}, u32[]{:S(2)}) collective-permute-start(bf16[4,128,256]{2,1,0:T(8,128)(2,1)S(1)} %constant_dynamic-update-slice_fusion.refs_0_), channel_id=1, source_target_pairs={{0,4},{4,0},{8,12},{12,8},{16,20},{20,16},{24,28},{28,24},{1,5},{5... | collective-permute-start | bytes 786440 | tf_op jit(solution)/shard_map/ppermute | solution.py:30
  39.1 1.5 %collective-permute-start.13 = (bf16[32,3328]{1,0:T(8,128)(2,1)S(1)}, bf16[32,3328]{1,0:T(8,128)(2,1)S(1)}, u32[]{:S(2)}, u32[]{:S(2)}) collective-permute-start(bf16[32,3328]{1,0:T(8,128)(2,1)S(1)} %get-tuple-element.175), channel_id=1, source_target_pairs={{0,1},{1,0},{2,3},{3,2},{4,5},{5,4},{6,7},{7,6},{8,9},{9,8},{10,11... | collective-permute-start | bytes 638984 | tf_op jit(solution)/shard_map/ppermute | solution.py:30
  39.1 1.8 %collective-permute-start.12 = (bf16[32,3328]{1,0:T(8,128)(2,1)S(1)}, bf16[32,3328]{1,0:T(8,128)(2,1)S(1)}, u32[]{:S(2)}, u32[]{:S(2)}) collective-permute-start(bf16[32,3328]{1,0:T(8,128)(2,1)S(1)} %get-tuple-element.176), channel_id=1, source_target_pairs={{0,1},{1,0},{2,3},{3,2},{4,5},{5,4},{6,7},{7,6},{8,9},{9,8},{10,11... | collective-permute-start | bytes 638984 | tf_op jit(solution)/shard_map/ppermute | solution.py:30
  39.6 1.6 %collective-permute-start.11 = (bf16[32,3328]{1,0:T(8,128)(2,1)S(1)}, bf16[32,3328]{1,0:T(8,128)(2,1)S(1)}, u32[]{:S(2)}, u32[]{:S(2)}) collective-permute-start(bf16[32,3328]{1,0:T(8,128)(2,1)S(1)} %get-tuple-element.177), channel_id=1, source_target_pairs={{0,1},{1,0},{2,3},{3,2},{4,5},{5,4},{6,7},{7,6},{8,9},{9,8},{10,11... | collective-permute-start | bytes 638984 | tf_op jit(solution)/shard_map/ppermute | solution.py:30
  39.7 1.8 %collective-permute-start.10 = (bf16[32,3328]{1,0:T(8,128)(2,1)S(1)}, bf16[32,3328]{1,0:T(8,128)(2,1)S(1)}, u32[]{:S(2)}, u32[]{:S(2)}) collective-permute-start(bf16[32,3328]{1,0:T(8,128)(2,1)S(1)} %get-tuple-element.178), channel_id=1, source_target_pairs={{0,1},{1,0},{2,3},{3,2},{4,5},{5,4},{6,7},{7,6},{8,9},{9,8},{10,11... | collective-permute-start | bytes 638984 | tf_op jit(solution)/shard_map/ppermute | solution.py:30
  41.8 12.8 %collective-permute-start.14 = (bf16[1,2,32,3328]{3,2,1,0:T(8,128)(2,1)S(1)}, bf16[1,2,32,3328]{3,2,1,0:T(8,128)(2,1)S(1)}, u32[]{:S(2)}, u32[]{:S(2)}) collective-permute-start(bf16[1,2,32,3328]{3,2,1,0:T(8,128)(2,1)S(1)} %get-tuple-element.102), channel_id=1, source_target_pairs={{0,2},{1,3},{2,0},{3,1},{4,6},{5,7},{6,4},{7,5},{8,10},{9,11},{10,... | collective-permute-start | bytes 1277960 | tf_op jit(solution)/shard_map/ppermute | solution.py:30
  49.6 1.5 %collective-permute-start.22 = (bf16[16,3328]{1,0:T(8,128)(2,1)S(1)}, bf16[16,3328]{1,0:T(8,128)(2,1)S(1)}, u32[]{:S(2)}, u32[]{:S(2)}) collective-permute-start(bf16[16,3328]{1,0:T(8,128)(2,1)S(1)} %get-tuple-element.168), channel_id=1, source_target_pairs={{0,1},{1,0},{2,3},{3,2},{4,5},{5,4},{6,7},{7,6},{8,9},{9,8},{10,11... | collective-permute-start | bytes 319496 | tf_op jit(solution)/shard_map/ppermute | solution.py:30
  50.1 11.0 %collective-permute-start.24 = (bf16[4,128,256]{2,1,0:T(8,128)(2,1)S(1)}, bf16[4,128,256]{2,1,0:T(8,128)(2,1)S(1)}, u32[]{:S(2)}, u32[]{:S(2)}) collective-permute-start(bf16[4,128,256]{2,1,0:T(8,128)(2,1)S(1)} %constant_dynamic-update-slice_fusion.3.refs_0_), channel_id=1, source_target_pairs={{0,4},{4,0},{8,12},{12,8},{16,20},{20,16},{24,28},{28,24},{1,5},{5... | collective-permute-start | bytes 786440 | tf_op jit(solution)/shard_map/ppermute | solution.py:30
  54.0 16.7 %collective-permute-start.34 = (bf16[1,2,32,3328]{3,2,1,0:T(8,128)(2,1)S(1)}, bf16[1,2,32,3328]{3,2,1,0:T(8,128)(2,1)S(1)}, u32[]{:S(2)}, u32[]{:S(2)}) collective-permute-start(bf16[1,2,32,3328]{3,2,1,0:T(8,128)(2,1)S(1)} %get-tuple-element.109), channel_id=1, source_target_pairs={{0,2},{1,3},{2,0},{3,1},{4,6},{5,7},{6,4},{7,5},{8,10},{9,11},{10,... | collective-permute-start | bytes 1277960 | tf_op jit(solution)/shard_map/ppermute | solution.py:30
  61.7 2.5 %collective-permute-start.30 = (bf16[16,3328]{1,0:T(8,128)(2,1)S(1)}, bf16[16,3328]{1,0:T(8,128)(2,1)S(1)}, u32[]{:S(2)}, u32[]{:S(2)}) collective-permute-start(bf16[16,3328]{1,0:T(8,128)(2,1)S(1)} %get-tuple-element.161), channel_id=1, source_target_pairs={{0,1},{1,0},{2,3},{3,2},{4,5},{5,4},{6,7},{7,6},{8,9},{9,8},{10,11... | collective-permute-start | bytes 319496 | tf_op jit(solution)/shard_map/ppermute | solution.py:30
  61.8 2.5 %collective-permute-start.29 = (bf16[16,3328]{1,0:T(8,128)(2,1)S(1)}, bf16[16,3328]{1,0:T(8,128)(2,1)S(1)}, u32[]{:S(2)}, u32[]{:S(2)}) collective-permute-start(bf16[16,3328]{1,0:T(8,128)(2,1)S(1)} %get-tuple-element.162), channel_id=1, source_target_pairs={{0,1},{1,0},{2,3},{3,2},{4,5},{5,4},{6,7},{7,6},{8,9},{9,8},{10,11... | collective-permute-start | bytes 319496 | tf_op jit(solution)/shard_map/ppermute | solution.py:30
  62.5 2.2 %collective-permute-start.28 = (bf16[16,3328]{1,0:T(8,128)(2,1)S(1)}, bf16[16,3328]{1,0:T(8,128)(2,1)S(1)}, u32[]{:S(2)}, u32[]{:S(2)}) collective-permute-start(bf16[16,3328]{1,0:T(8,128)(2,1)S(1)} %get-tuple-element.163), channel_id=1, source_target_pairs={{0,1},{1,0},{2,3},{3,2},{4,5},{5,4},{6,7},{7,6},{8,9},{9,8},{10,11... | collective-permute-start | bytes 319496 | tf_op jit(solution)/shard_map/ppermute | solution.py:30
  62.7 8.3 %collective-permute-start.35 = (bf16[32,3328]{1,0:T(8,128)(2,1)S(1)}, bf16[32,3328]{1,0:T(8,128)(2,1)S(1)}, u32[]{:S(2)}, u32[]{:S(2)}) collective-permute-start(bf16[32,3328]{1,0:T(8,128)(2,1)S(1)} %gated.4.refs_0_), channel_id=1, source_target_pairs={{0,2},{1,3},{2,0},{3,1},{4,6},{5,7},{6,4},{7,5},{8,10},{9,11},{10,... | collective-permute-start | bytes 638984 | tf_op jit(solution)/shard_map/ppermute | solution.py:30
  66.3 20.9 %collective-permute-start.33 = (bf16[1,2,32,3328]{3,2,1,0:T(8,128)(2,1)S(1)}, bf16[1,2,32,3328]{3,2,1,0:T(8,128)(2,1)S(1)}, u32[]{:S(2)}, u32[]{:S(2)}) collective-permute-start(bf16[1,2,32,3328]{3,2,1,0:T(8,128)(2,1)S(1)} %get-tuple-element.118), channel_id=1, source_target_pairs={{0,2},{1,3},{2,0},{3,1},{4,6},{5,7},{6,4},{7,5},{8,10},{9,11},{10,... | collective-permute-start | bytes 1277960 | tf_op jit(solution)/shard_map/ppermute | solution.py:30
  78.2 2.3 %collective-permute-start.41 = (bf16[16,3328]{1,0:T(8,128)(2,1)S(1)}, bf16[16,3328]{1,0:T(8,128)(2,1)S(1)}, u32[]{:S(2)}, u32[]{:S(2)}) collective-permute-start(bf16[16,3328]{1,0:T(8,128)(2,1)S(1)} %get-tuple-element.153), channel_id=1, source_target_pairs={{0,1},{1,0},{2,3},{3,2},{4,5},{5,4},{6,7},{7,6},{8,9},{9,8},{10,11... | collective-permute-start | bytes 319496 | tf_op jit(solution)/shard_map/ppermute | solution.py:30
  78.3 2.3 %collective-permute-start.40 = (bf16[16,3328]{1,0:T(8,128)(2,1)S(1)}, bf16[16,3328]{1,0:T(8,128)(2,1)S(1)}, u32[]{:S(2)}, u32[]{:S(2)}) collective-permute-start(bf16[16,3328]{1,0:T(8,128)(2,1)S(1)} %get-tuple-element.154), channel_id=1, source_target_pairs={{0,1},{1,0},{2,3},{3,2},{4,5},{5,4},{6,7},{7,6},{8,9},{9,8},{10,11... | collective-permute-start | bytes 319496 | tf_op jit(solution)/shard_map/ppermute | solution.py:30
  79.0 2.0 %collective-permute-start.39 = (bf16[16,3328]{1,0:T(8,128)(2,1)S(1)}, bf16[16,3328]{1,0:T(8,128)(2,1)S(1)}, u32[]{:S(2)}, u32[]{:S(2)}) collective-permute-start(bf16[16,3328]{1,0:T(8,128)(2,1)S(1)} %get-tuple-element.155), channel_id=1, source_target_pairs={{0,1},{1,0},{2,3},{3,2},{4,5},{5,4},{6,7},{7,6},{8,9},{9,8},{10,11... | collective-permute-start | bytes 319496 | tf_op jit(solution)/shard_map/ppermute | solution.py:30
  79.1 8.1 %collective-permute-start.44 = (bf16[32,3328]{1,0:T(8,128)(2,1)S(1)}, bf16[32,3328]{1,0:T(8,128)(2,1)S(1)}, u32[]{:S(2)}, u32[]{:S(2)}) collective-permute-start(bf16[32,3328]{1,0:T(8,128)(2,1)S(1)} %gated.5.refs_4_), channel_id=1, source_target_pairs={{0,2},{1,3},{2,0},{3,1},{4,6},{5,7},{6,4},{7,5},{8,10},{9,11},{10,... | collective-permute-start | bytes 638984 | tf_op jit(solution)/shard_map/ppermute | solution.py:30
  82.6 13.8 %collective-permute-start.50 = (bf16[1,2,32,3328]{3,2,1,0:T(8,128)(2,1)S(1)}, bf16[1,2,32,3328]{3,2,1,0:T(8,128)(2,1)S(1)}, u32[]{:S(2)}, u32[]{:S(2)}) collective-permute-start(bf16[1,2,32,3328]{3,2,1,0:T(8,128)(2,1)S(1)} %get-tuple-element.125), channel_id=1, source_target_pairs={{0,2},{1,3},{2,0},{3,1},{4,6},{5,7},{6,4},{7,5},{8,10},{9,11},{10,... | collective-permute-start | bytes 1277960 | tf_op jit(solution)/shard_map/ppermute | solution.py:30
  87.7 2.8 %collective-permute-start.46 = (bf16[32,3328]{1,0:T(8,128)(2,1)S(1)}, bf16[32,3328]{1,0:T(8,128)(2,1)S(1)}, u32[]{:S(2)}, u32[]{:S(2)}) collective-permute-start(bf16[32,3328]{1,0:T(8,128)(2,1)S(1)} %collective-permute-done.35.refs_1_), channel_id=1, source_target_pairs={{0,1},{1,0},{2,3},{3,2},{4,5},{5,4},{6,7},{7,6},{8,9},{9,8},{10,11... | collective-permute-start | bytes 638984 | tf_op jit(solution)/shard_map/ppermute | solution.py:30
  88.2 2.3 %collective-permute-start.47 = (bf16[32,3328]{1,0:T(8,128)(2,1)S(1)}, bf16[32,3328]{1,0:T(8,128)(2,1)S(1)}, u32[]{:S(2)}, u32[]{:S(2)}) collective-permute-start(bf16[32,3328]{1,0:T(8,128)(2,1)S(1)} %gated.5.refs_4_), channel_id=1, source_target_pairs={{0,1},{1,0},{2,3},{3,2},{4,5},{5,4},{6,7},{7,6},{8,9},{9,8},{10,11... | collective-permute-start | bytes 638984 | tf_op jit(solution)/shard_map/ppermute | solution.py:30
  88.3 2.7 %collective-permute-start.48 = (bf16[32,3328]{1,0:T(8,128)(2,1)S(1)}, bf16[32,3328]{1,0:T(8,128)(2,1)S(1)}, u32[]{:S(2)}, u32[]{:S(2)}) collective-permute-start(bf16[32,3328]{1,0:T(8,128)(2,1)S(1)} %collective-permute-done.44.refs_5_), channel_id=1, source_target_pairs={{0,1},{1,0},{2,3},{3,2},{4,5},{5,4},{6,7},{7,6},{8,9},{9,8},{10,11... | collective-permute-start | bytes 638984 | tf_op jit(solution)/shard_map/ppermute | solution.py:30
  89.1 11.8 %collective-permute-start.51 = (bf16[32,3328]{1,0:T(8,128)(2,1)S(1)}, bf16[32,3328]{1,0:T(8,128)(2,1)S(1)}, u32[]{:S(2)}, u32[]{:S(2)}) collective-permute-start(bf16[32,3328]{1,0:T(8,128)(2,1)S(1)} %gated.6.refs_0_), channel_id=1, source_target_pairs={{0,2},{1,3},{2,0},{3,1},{4,6},{5,7},{6,4},{7,5},{8,10},{9,11},{10,... | collective-permute-start | bytes 638984 | tf_op jit(solution)/shard_map/ppermute | solution.py:30
  90.4 11.8 %collective-permute-start.53 = (bf16[16,3328]{1,0:T(8,128)(2,1)S(1)}, bf16[16,3328]{1,0:T(8,128)(2,1)S(1)}, u32[]{:S(2)}, u32[]{:S(2)}) collective-permute-start(bf16[16,3328]{1,0:T(8,128)(2,1)S(1)} %get-tuple-element.189), channel_id=1, source_target_pairs={{0,1},{1,0},{2,3},{3,2},{4,5},{5,4},{6,7},{7,6},{8,9},{9,8},{10,11... | collective-permute-start | bytes 319496 | tf_op jit(solution)/shard_map/ppermute | solution.py:30
  90.5 11.9 %collective-permute-start.52 = (bf16[16,3328]{1,0:T(8,128)(2,1)S(1)}, bf16[16,3328]{1,0:T(8,128)(2,1)S(1)}, u32[]{:S(2)}, u32[]{:S(2)}) collective-permute-start(bf16[16,3328]{1,0:T(8,128)(2,1)S(1)} %get-tuple-element.190), channel_id=1, source_target_pairs={{0,1},{1,0},{2,3},{3,2},{4,5},{5,4},{6,7},{7,6},{8,9},{9,8},{10,11... | collective-permute-start | bytes 319496 | tf_op jit(solution)/shard_map/ppermute | solution.py:30
  96.7 11.6 %collective-permute-start.58 = (bf16[32,3328]{1,0:T(8,128)(2,1)S(1)}, bf16[32,3328]{1,0:T(8,128)(2,1)S(1)}, u32[]{:S(2)}, u32[]{:S(2)}) collective-permute-start(bf16[32,3328]{1,0:T(8,128)(2,1)S(1)} %gated.7.refs_0_), channel_id=1, source_target_pairs={{0,2},{1,3},{2,0},{3,1},{4,6},{5,7},{6,4},{7,5},{8,10},{9,11},{10,... | collective-permute-start | bytes 638984 | tf_op jit(solution)/shard_map/ppermute | solution.py:30
  98.1 10.6 %collective-permute-start.49 = (bf16[2,256,256]{2,1,0:T(8,128)(2,1)S(1)}, bf16[2,256,256]{2,1,0:T(8,128)(2,1)S(1)}, u32[]{:S(2)}, u32[]{:S(2)}) collective-permute-start(bf16[2,256,256]{2,1,0:T(8,128)(2,1)S(1)} %get-tuple-element.181), channel_id=1, source_target_pairs={{0,4},{4,0},{8,12},{12,8},{16,20},{20,16},{24,28},{28,24},{1,5},{5... | collective-permute-start | bytes 786440 | tf_op jit(solution)/shard_map/ppermute | solution.py:30
  100.9 10.2 %collective-permute-start.56 = (bf16[2,256,256]{2,1,0:T(8,128)(2,1)S(1)}, bf16[2,256,256]{2,1,0:T(8,128)(2,1)S(1)}, u32[]{:S(2)}, u32[]{:S(2)}) collective-permute-start(bf16[2,256,256]{2,1,0:T(8,128)(2,1)S(1)} %get-tuple-element.182), channel_id=1, source_target_pairs={{0,4},{4,0},{8,12},{12,8},{16,20},{20,16},{24,28},{28,24},{1,5},{5... | collective-permute-start | bytes 786440 | tf_op jit(solution)/shard_map/ppermute | solution.py:30
  107.3 9.8 %collective-permute-start.63 = (bf16[4,128,256]{2,1,0:T(8,128)(2,1)S(1)}, bf16[4,128,256]{2,1,0:T(8,128)(2,1)S(1)}, u32[]{:S(2)}, u32[]{:S(2)}) collective-permute-start(bf16[4,128,256]{2,1,0:T(8,128)(2,1)S(1)} %get-tuple-element.138), channel_id=1, source_target_pairs={{0,8},{4,12},{8,0},{12,4},{16,24},{20,28},{24,16},{28,20},{1,9},{5... | collective-permute-start | bytes 786440 | tf_op jit(solution)/shard_map/ppermute | solution.py:30
  108.2 3.9 %collective-permute-start.59 = (bf16[32,3328]{1,0:T(8,128)(2,1)S(1)}, bf16[32,3328]{1,0:T(8,128)(2,1)S(1)}, u32[]{:S(2)}, u32[]{:S(2)}) collective-permute-start(bf16[32,3328]{1,0:T(8,128)(2,1)S(1)} %gated.7.refs_0_), channel_id=1, source_target_pairs={{0,1},{1,0},{2,3},{3,2},{4,5},{5,4},{6,7},{7,6},{8,9},{9,8},{10,11... | collective-permute-start | bytes 638984 | tf_op jit(solution)/shard_map/ppermute | solution.py:30
  108.3 3.9 %collective-permute-start.60 = (bf16[32,3328]{1,0:T(8,128)(2,1)S(1)}, bf16[32,3328]{1,0:T(8,128)(2,1)S(1)}, u32[]{:S(2)}, u32[]{:S(2)}) collective-permute-start(bf16[32,3328]{1,0:T(8,128)(2,1)S(1)} %collective-permute-done.58.refs_1_), channel_id=1, source_target_pairs={{0,1},{1,0},{2,3},{3,2},{4,5},{5,4},{6,7},{7,6},{8,9},{9,8},{10,11... | collective-permute-start | bytes 638984 | tf_op jit(solution)/shard_map/ppermute | solution.py:30
  111.3 10.3 %collective-permute-start.57 = (bf16[2,256,256]{2,1,0:T(8,128)(2,1)S(1)}, bf16[2,256,256]{2,1,0:T(8,128)(2,1)S(1)}, u32[]{:S(2)}, u32[]{:S(2)}) collective-permute-start(bf16[2,256,256]{2,1,0:T(8,128)(2,1)S(1)} %get-tuple-element.180), channel_id=1, source_target_pairs={{0,8},{4,12},{8,0},{12,4},{16,24},{20,28},{24,16},{28,20},{1,9},{5... | collective-permute-start | bytes 786440 | tf_op jit(solution)/shard_map/ppermute | solution.py:30
  115.7 6.4 %collective-permute-start.61 = (bf16[4,128,256]{2,1,0:T(8,128)(2,1)S(1)}, bf16[4,128,256]{2,1,0:T(8,128)(2,1)S(1)}, u32[]{:S(2)}, u32[]{:S(2)}) collective-permute-start(bf16[4,128,256]{2,1,0:T(8,128)(2,1)S(1)} %get-tuple-element.142), channel_id=1, source_target_pairs={{0,4},{4,0},{8,12},{12,8},{16,20},{20,16},{24,28},{28,24},{1,5},{5... | collective-permute-start | bytes 786440 | tf_op jit(solution)/shard_map/ppermute | solution.py:30
  122.2 5.0 %collective-permute-start.64 = (bf16[2,128,256]{2,1,0:T(8,128)(2,1)S(1)}, bf16[2,128,256]{2,1,0:T(8,128)(2,1)S(1)}, u32[]{:S(2)}, u32[]{:S(2)}) collective-permute-start(bf16[2,128,256]{2,1,0:T(8,128)(2,1)S(1)} %get-tuple-element.150), channel_id=1, source_target_pairs={{0,4},{4,0},{8,12},{12,8},{16,20},{20,16},{24,28},{28,24},{1,5},{5... | collective-permute-start | bytes 393224 | tf_op jit(solution)/shard_map/ppermute | solution.py:30
  123.7 6.9 %collective-permute-start.66 = (bf16[2,128,256]{2,1,0:T(8,128)(2,1)S(1)}, bf16[2,128,256]{2,1,0:T(8,128)(2,1)S(1)}, u32[]{:S(2)}, u32[]{:S(2)}) collective-permute-start(bf16[2,128,256]{2,1,0:T(8,128)(2,1)S(1)} %slice.197), channel_id=1, source_target_pairs={{0,8},{4,12},{8,0},{12,4},{16,24},{20,28},{24,16},{28,20},{1,9},{5... | collective-permute-start | bytes 393224 | tf_op jit(solution)/shard_map/ppermute | solution.py:30
  125.0 11.3 %collective-permute-start.62 = (bf16[1,256,256]{2,1,0:T(8,128)(2,1)S(1)}, bf16[1,256,256]{2,1,0:T(8,128)(2,1)S(1)}, u32[]{:S(2)}, u32[]{:S(2)}) collective-permute-start(bf16[1,256,256]{2,1,0:T(8,128)(2,1)S(1)} %get-tuple-element.146), channel_id=1, source_target_pairs={{0,16},{4,20},{8,24},{12,28},{16,0},{20,4},{24,8},{28,12},{1,17},{... | collective-permute-start | bytes 393224 | tf_op jit(solution)/shard_map/ppermute | solution.py:30
  127.3 9.7 %collective-permute-start.65 = (bf16[1,128,256]{2,1,0:T(8,128)(2,1)S(1)}, bf16[1,128,256]{2,1,0:T(8,128)(2,1)S(1)}, u32[]{:S(2)}, u32[]{:S(2)}) collective-permute-start(bf16[1,128,256]{2,1,0:T(8,128)(2,1)S(1)} %slice.202), channel_id=1, source_target_pairs={{0,16},{4,20},{8,24},{12,28},{16,0},{20,4},{24,8},{28,12},{1,17},{... | collective-permute-start | bytes 196616 | tf_op jit(solution)/shard_map/ppermute | solution.py:30
  130.6 7.0 %collective-permute-start.67 = (bf16[1,128,256]{2,1,0:T(8,128)(2,1)S(1)}, bf16[1,128,256]{2,1,0:T(8,128)(2,1)S(1)}, u32[]{:S(2)}, u32[]{:S(2)}) collective-permute-start(bf16[1,128,256]{2,1,0:T(8,128)(2,1)S(1)} %slice.205), channel_id=1, source_target_pairs={{0,16},{4,20},{8,24},{12,28},{16,0},{20,4},{24,8},{28,12},{1,17},{... | collective-permute-start | bytes 196616 | tf_op jit(solution)/shard_map/ppermute | solution.py:30
  (21 other events, 28.2 us)

commit v4 on v3

--- a/solution.py
+++ b/solution.py
@@ -409,7 +409,7 @@
             gather_tokens(k, wide_bits - 1, gate[0])
         gate.append(decode_part(after(gw, gate[0], tok[0][0]), gs, 1, 2))
         for k in (2, 3):
-            tok[k] = [after(tok[k][0], tok[0][0])]
+            tok[k] = [after(tok[k][0], gate[1])]
         for k in (0, 1):
             gather_tokens(k, 1, gate[1])
         up = [decode_part(after(uw, tok[0][0], tok[1][0]), us, 0, 1)]
@@ -439,16 +439,17 @@
             gated(k, *others)
         for j in (0, 1):
             hidden[j] = [after(g, hidden[2][0]) for g in hidden[j]]
-            gather_hidden(j, 1)
+            gather_hidden(j, 2)
         finish([0, 1], down_w, hidden[2][0])
         gated(3, parts[0][1])
-        gather_hidden(2, 2)
+        gather_hidden(2, 1)
         finish(2, down_w, hidden[3][0])
-        scatter(0, wide_bits - 1, parts[2][1], split=True)
-        gather_hidden(3, 1)
-        finish(3, down_w, *parts[0])
-        scatter(0, wide_bits - 2, parts[3][1])
+        hidden[3][1] = after(hidden[3][1], parts[2][1])
+        gather_hidden(3, 2)
+        finish(3, down_w, parts[2][1])
+        scatter(0, wide_bits - 1, parts[3][1], split=True)
         scatter(2, wide_bits - 1, parts[3][1])
+        scatter(0, wide_bits - 2)
         scatter(3, wide_bits - 1)
         for k in (0, 2):
             parts[k] = tuple(after(p, parts[3][1]) for p in parts[k])

time: 139 us -> 136 us (0.978)
  waiting for transfers between devices: 25.4 us -> 22.9 us
    ppermute x68 -> x72, waiting for transfers between devices: 25.4 us -> 22.9 us  [flip(): return lax.ppermute(array, axis, [(i, i ^ mask) for i in range(size)])]
    ppermute x68 -> x72, starting transfers between devices: 51.1 us -> 50.5 us  [flip(): return lax.ppermute(array, axis, [(i, i ^ mask) for i in range(size)])]
  transfers between devices with their start and end apart: 68 -> 72, of which waited for: 35 -> 32; matrix products, arithmetic and copies ran while one was open for 1% -> 1% of each run, Pallas kernels for 42% -> 43%
where the time goes in v4:
time: 136 us; the launch traced here: 135 us
  Pallas kernels  59.4 us (44%)
  starting transfers between devices  50.5 us (37%)
  waiting for transfers between devices  22.9 us (17%)
  local copies, waits for them, and re-layouts  1.42 us (1%)
    ppermute x72, starting transfers between devices, flip(): return lax.ppermute(array, axis, [(i, i ^ mask) for i in range(size)])  50.5 us
    pallas_call x4, Pallas kernels, gate_up(): pl.pallas_call(functools.partial(gate_up_kernel, len(shards), len(gate),...  24.6 us
    ppermute x72, waiting for transfers between devices, flip(): return lax.ppermute(array, axis, [(i, i ^ mask) for i in range(size)])  22.9 us
    pallas_call x5, Pallas kernels, decode_part(): pl.pallas_call(functools.partial(decode_kernel, part * size, block), in_s...  19.2 us
    pallas_call x3, Pallas kernels, down(): pl.pallas_call(functools.partial(down_kernel, len(hidden), len(weights),...  12.3 us
  transfers between devices with their start and end apart: 72, of which 32 were waited for; matrix products, arithmetic and copies ran while one was open for 1% of the time, Pallas kernels for 43%

profile of v4, /device:TPU:0, one launch (start us, length us, event | category | flops | bytes accessed | tf_op | source)
XLA Modules:
  0.0 135.4 jit_solution(10037097960656994779)
XLA Ops:
  0.0 0.9 copy-done
  1.0 4.1 %collective-permute-start = (bf16[1,128,256]{2,1,0:T(8,128)(2,1)S(1)}, bf16[1,128,256]{2,1,0:T(8,128)(2,1)S(1)}, u32[]{:S(2)}, u32[]{:S(2)}) collective-permute-start(bf16[1,128,256]{2,1,0:T(8,128)(2,1)S(1)} %bitcast.23), channel_id=1, source_target_pairs={{0,16},{4,20},{8,24},{12,28},{16,0},{20,4},{24,8},{28,12},{1,17},{... | collective-permute-start | bytes 196616 | tf_op jit(solution)/shard_map/ppermute | solution.py:30
  5.2 3.2 %decode.5.refs_2_ = bf16[1024,3328]{1,0:T(8,128)(2,1)S(1)} custom-call(bf16[2048,3328]{1,0:T(8,128)(2,1)} %w_ref.1, f32[16,3328]{1,0:T(8,128)} %sc_ref.6), custom_call_target="tpu_custom_call" | custom-call | flops 1024 | bytes 1024 | tf_op jit(solution)/shard_map/decode/pallas_call | solution.py:82
  8.7 2.1 %collective-permute-start.1 = (bf16[2,128,256]{2,1,0:T(8,128)(2,1)S(1)}, bf16[2,128,256]{2,1,0:T(8,128)(2,1)S(1)}, u32[]{:S(2)}, u32[]{:S(2)}) collective-permute-start(bf16[2,128,256]{2,1,0:T(8,128)(2,1)S(1)} %pad_maximum_fusion.2), channel_id=1, source_target_pairs={{0,8},{4,12},{8,0},{12,4},{16,24},{20,28},{24,16},{28,20},{1,9},{5... | collective-permute-start | bytes 393224 | tf_op jit(solution)/shard_map/ppermute | solution.py:30
  10.9 0.7 collective-permute-done.3
  11.6 0.6 collective-permute-start.4
  12.2 3.2 %decode.6.refs_3_ = bf16[1024,3328]{1,0:T(8,128)(2,1)S(1)} custom-call(bf16[2048,3328]{1,0:T(8,128)(2,1)} %w_ref.1, f32[16,3328]{1,0:T(8,128)} %sc_ref.6), custom_call_target="tpu_custom_call" | custom-call | flops 1024 | bytes 1024 | tf_op jit(solution)/shard_map/decode/pallas_call | solution.py:82
  15.4 3.4 %collective-permute-start.6 = (bf16[1,128,256]{2,1,0:T(8,128)(2,1)S(1)}, bf16[1,128,256]{2,1,0:T(8,128)(2,1)S(1)}, u32[]{:S(2)}, u32[]{:S(2)}) collective-permute-start(bf16[1,128,256]{2,1,0:T(8,128)(2,1)S(1)} %bitcast.29), channel_id=1, source_target_pairs={{0,16},{4,20},{8,24},{12,28},{16,0},{20,4},{24,8},{28,12},{1,17},{... | collective-permute-start | bytes 196616 | tf_op jit(solution)/shard_map/ppermute | solution.py:30
  19.0 1.6 %collective-permute-start.2 = (bf16[4,128,256]{2,1,0:T(8,128)(2,1)S(1)}, bf16[4,128,256]{2,1,0:T(8,128)(2,1)S(1)}, u32[]{:S(2)}, u32[]{:S(2)}) collective-permute-start(bf16[4,128,256]{2,1,0:T(8,128)(2,1)S(1)} %get-tuple-element.197.refs_0_), channel_id=1, source_target_pairs={{0,4},{4,0},{8,12},{12,8},{16,20},{20,16},{24,28},{28,24},{1,5},{5... | collective-permute-start | bytes 786440 | tf_op jit(solution)/shard_map/ppermute | solution.py:30
  21.1 5.6 %decode.7.refs_4_ = bf16[2048,3328]{1,0:T(8,128)(2,1)S(1)} custom-call(bf16[2048,3328]{1,0:T(8,128)(2,1)} %w_ref.2, f32[16,3328]{1,0:T(8,128)} %sc_ref.7), custom_call_target="tpu_custom_call" | custom-call | flops 1024 | bytes 1024 | tf_op jit(solution)/shard_map/decode/pallas_call | solution.py:82
  26.8 1.0 collective-permute-start.7
  27.8 1.1 collective-permute-start.9
  28.9 6.3 %gate_up.4 = (bf16[2,2,32,3328]{3,2,1,0:T(8,128)(2,1)S(1)}, bf16[2,2,32,3328]{3,2,1,0:T(8,128)(2,1)S(1)}) custom-call(s32[1]{0:T(128)} %bitcast.1.place_ref, bf16[4,128,256]{2,1,0:T(8,128)(2,1)S(1)} %get-tuple-element.197.refs_0_, bf16[4,128,256]{2,1,0:T(8,128)(2,1)S(1)} %collective-permute-done.2.refs_1_, bf16[1024,3328]{1,0:T(8,128)(2,1)S(1)} %decode.5.refs_2_, ...), custom_call_target="tpu_custom_call" | custom-call | flops 1024 | bytes 1024 | tf_op jit(solution)/shard_map/gate_up/pallas_call | solution.py:149
  35.3 1.6 %collective-permute-start.15 = (bf16[4,128,256]{2,1,0:T(8,128)(2,1)S(1)}, bf16[4,128,256]{2,1,0:T(8,128)(2,1)S(1)}, u32[]{:S(2)}, u32[]{:S(2)}) collective-permute-start(bf16[4,128,256]{2,1,0:T(8,128)(2,1)S(1)} %constant_dynamic-update-slice_fusion.refs_0_), channel_id=1, source_target_pairs={{0,4},{4,0},{8,12},{12,8},{16,20},{20,16},{24,28},{28,24},{1,5},{5... | collective-permute-start | bytes 786440 | tf_op jit(solution)/shard_map/ppermute | solution.py:30
  39.6 1.6 %collective-permute-start.14 = (bf16[1,2,32,3328]{3,2,1,0:T(8,128)(2,1)S(1)}, bf16[1,2,32,3328]{3,2,1,0:T(8,128)(2,1)S(1)}, u32[]{:S(2)}, u32[]{:S(2)}) collective-permute-start(bf16[1,2,32,3328]{3,2,1,0:T(8,128)(2,1)S(1)} %get-tuple-element.102), channel_id=1, source_target_pairs={{0,2},{1,3},{2,0},{3,1},{4,6},{5,7},{6,4},{7,5},{8,10},{9,11},{10,... | collective-permute-start | bytes 1277960 | tf_op jit(solution)/shard_map/ppermute | solution.py:30
  41.2 6.1 %gate_up.5 = (bf16[2,2,32,3328]{3,2,1,0:T(8,128)(2,1)S(1)}, bf16[2,2,32,3328]{3,2,1,0:T(8,128)(2,1)S(1)}) custom-call(s32[1]{0:T(128)} %bitcast.1.place_ref, bf16[4,128,256]{2,1,0:T(8,128)(2,1)S(1)} %get-tuple-element.103.refs_0_, bf16[4,128,256]{2,1,0:T(8,128)(2,1)S(1)} %collective-permute-done.5.refs_1_, bf16[1024,3328]{1,0:T(8,128)(2,1)S(1)} %decode.5.refs_2_, ...), custom_call_target="tpu_custom_call" | custom-call | flops 1024 | bytes 1024 | tf_op jit(solution)/shard_map/gate_up/pallas_call | solution.py:149
  51.9 0.6 collective-permute-start.34
  52.9 6.1 %gate_up.6 = (bf16[2,2,32,3328]{3,2,1,0:T(8,128)(2,1)S(1)}, bf16[2,2,32,3328]{3,2,1,0:T(8,128)(2,1)S(1)}) custom-call(s32[1]{0:T(128)} %bitcast.1.place_ref, bf16[4,128,256]{2,1,0:T(8,128)(2,1)S(1)} %constant_dynamic-update-slice_fusion.refs_0_, bf16[4,128,256]{2,1,0:T(8,128)(2,1)S(1)} %collective-permute-done.15.refs_1_, ...), custom_call_target="tpu_custom_call" | custom-call | flops 1024 | bytes 1024 | tf_op jit(solution)/shard_map/gate_up/pallas_call | solution.py:149
  60.6 1.5 %collective-permute-start.35 = (bf16[32,3328]{1,0:T(8,128)(2,1)S(1)}, bf16[32,3328]{1,0:T(8,128)(2,1)S(1)}, u32[]{:S(2)}, u32[]{:S(2)}) collective-permute-start(bf16[32,3328]{1,0:T(8,128)(2,1)S(1)} %gated.4.refs_0_), channel_id=1, source_target_pairs={{0,2},{1,3},{2,0},{3,1},{4,6},{5,7},{6,4},{7,5},{8,10},{9,11},{10,... | collective-permute-start | bytes 638984 | tf_op jit(solution)/shard_map/ppermute | solution.py:30
  62.7 0.7 collective-permute-done.27.refs_2_
  64.2 0.7 collective-permute-start.33
  64.9 3.6 %decode.8.refs_12_.refs_4_.refs_6_ = bf16[1664,2048]{1,0:T(8,128)(2,1)S(1)} custom-call(bf16[3328,2048]{1,0:T(8,128)(2,1)} %w_ref.4, f32[26,2048]{1,0:T(8,128)} %sc_ref.9), custom_call_target="tpu_custom_call" | custom-call | flops 1024 | bytes 1024 | tf_op jit(solution)/shard_map/decode/pallas_call | solution.py:82
  69.2 6.1 %gate_up.7 = (bf16[2,2,32,3328]{3,2,1,0:T(8,128)(2,1)S(1)}, bf16[2,2,32,3328]{3,2,1,0:T(8,128)(2,1)S(1)}) custom-call(s32[1]{0:T(128)} %bitcast.1.place_ref, bf16[4,128,256]{2,1,0:T(8,128)(2,1)S(1)} %constant_dynamic-update-slice_fusion.3.refs_0_, bf16[4,128,256]{2,1,0:T(8,128)(2,1)S(1)} %collective-permute-done.24.refs_1_, ...), custom_call_target="tpu_custom_call" | custom-call | flops 1024 | bytes 1024 | tf_op jit(solution)/shard_map/gate_up/pallas_call | solution.py:149
  76.9 1.4 %collective-permute-start.44 = (bf16[32,3328]{1,0:T(8,128)(2,1)S(1)}, bf16[32,3328]{1,0:T(8,128)(2,1)S(1)}, u32[]{:S(2)}, u32[]{:S(2)}) collective-permute-start(bf16[32,3328]{1,0:T(8,128)(2,1)S(1)} %gated.5.refs_6_), channel_id=1, source_target_pairs={{0,2},{1,3},{2,0},{3,1},{4,6},{5,7},{6,4},{7,5},{8,10},{9,11},{10,... | collective-permute-start | bytes 638984 | tf_op jit(solution)/shard_map/ppermute | solution.py:30
  78.9 0.7 collective-permute-done.38.refs_2_
  80.4 0.7 collective-permute-start.54
  81.2 3.6 %decode.9.refs_13_.refs_5_.refs_7_ = bf16[1664,2048]{1,0:T(8,128)(2,1)S(1)} custom-call(bf16[3328,2048]{1,0:T(8,128)(2,1)} %w_ref.4, f32[26,2048]{1,0:T(8,128)} %sc_ref.9), custom_call_target="tpu_custom_call" | custom-call | flops 1024 | bytes 1024 | tf_op jit(solution)/shard_map/decode/pallas_call | solution.py:82
  88.3 1.4 %collective-permute-start.55 = (bf16[32,3328]{1,0:T(8,128)(2,1)S(1)}, bf16[32,3328]{1,0:T(8,128)(2,1)S(1)}, u32[]{:S(2)}, u32[]{:S(2)}) collective-permute-start(bf16[32,3328]{1,0:T(8,128)(2,1)S(1)} %gated.6.refs_0_), channel_id=1, source_target_pairs={{0,2},{1,3},{2,0},{3,1},{4,6},{5,7},{6,4},{7,5},{8,10},{9,11},{10,... | collective-permute-start | bytes 638984 | tf_op jit(solution)/shard_map/ppermute | solution.py:30
  89.7 5.3 %down.3 = (bf16[4,256,256]{2,1,0:T(8,128)(2,1)S(1)}, bf16[4,256,256]{2,1,0:T(8,128)(2,1)S(1)}) custom-call(s32[1]{0:T(128)} %bitcast.1.place_ref, bf16[32,3328]{1,0:T(8,128)(2,1)S(1)} %gated.4.refs_0_, bf16[32,3328]{1,0:T(8,128)(2,1)S(1)} %collective-permute-done.35.refs_1_, bf16[16,3328]{1,0:T(8,128)(2,1)S(1)} %collective-permute-done.45.refs_2_, ...), custom_call_target="tpu_custom_call" | custom-call | flops 1024 | bytes 1024 | tf_op jit(solution)/shard_map/down/pallas_call | solution.py:196
  95.0 1.6 %collective-permute-start.53 = (bf16[2,256,256]{2,1,0:T(8,128)(2,1)S(1)}, bf16[2,256,256]{2,1,0:T(8,128)(2,1)S(1)}, u32[]{:S(2)}, u32[]{:S(2)}) collective-permute-start(bf16[2,256,256]{2,1,0:T(8,128)(2,1)S(1)} %get-tuple-element.179), channel_id=1, source_target_pairs={{0,4},{4,0},{8,12},{12,8},{16,20},{20,16},{24,28},{28,24},{1,5},{5... | collective-permute-start | bytes 786440 | tf_op jit(solution)/shard_map/ppermute | solution.py:30
  97.5 0.7 collective-permute-start.58
  98.8 0.9 collective-permute-done.57.refs_3_
  99.8 3.5 %down.4 = (bf16[4,128,256]{2,1,0:T(8,128)(2,1)S(1)}, bf16[4,128,256]{2,1,0:T(8,128)(2,1)S(1)}) custom-call(s32[1]{0:T(128)} %bitcast.1.place_ref, bf16[32,3328]{1,0:T(8,128)(2,1)S(1)} %gated.6.refs_0_, bf16[32,3328]{1,0:T(8,128)(2,1)S(1)} %collective-permute-done.55.refs_1_, bf16[32,3328]{1,0:T(8,128)(2,1)S(1)} %collective-permute-done.56.refs_2_, ...), custom_call_target="tpu_custom_call" | custom-call | flops 1024 | bytes 1024 | tf_op jit(solution)/shard_map/down/pallas_call | solution.py:196
  103.3 0.9 collective-permute-done.58.refs_1_
  104.8 1.1 collective-permute-start.67
  105.9 3.5 %down.5 = (bf16[4,128,256]{2,1,0:T(8,128)(2,1)S(1)}, bf16[4,128,256]{2,1,0:T(8,128)(2,1)S(1)}) custom-call(s32[1]{0:T(128)} %bitcast.1.place_ref, bf16[32,3328]{1,0:T(8,128)(2,1)S(1)} %gated.7.refs_0_, bf16[32,3328]{1,0:T(8,128)(2,1)S(1)} %collective-permute-done.58.refs_1_, bf16[16,3328]{1,0:T(8,128)(2,1)S(1)} %collective-permute-done.59.refs_2_, ...), custom_call_target="tpu_custom_call" | custom-call | flops 1024 | bytes 1024 | tf_op jit(solution)/shard_map/down/pallas_call | solution.py:196
  109.5 1.6 %collective-permute-start.65 = (bf16[4,128,256]{2,1,0:T(8,128)(2,1)S(1)}, bf16[4,128,256]{2,1,0:T(8,128)(2,1)S(1)}, u32[]{:S(2)}, u32[]{:S(2)}) collective-permute-start(bf16[4,128,256]{2,1,0:T(8,128)(2,1)S(1)} %get-tuple-element.141), channel_id=1, source_target_pairs={{0,4},{4,0},{8,12},{12,8},{16,20},{20,16},{24,28},{28,24},{1,5},{5... | collective-permute-start | bytes 786440 | tf_op jit(solution)/shard_map/ppermute | solution.py:30
  111.1 1.0 collective-permute-start.64
  112.1 1.0 collective-permute-done.67
  113.2 4.7 %collective-permute-done.65 = bf16[4,128,256]{2,1,0:T(8,128)(2,1)S(1)} collective-permute-done((bf16[4,128,256]{2,1,0:T(8,128)(2,1)S(1)}, bf16[4,128,256]{2,1,0:T(8,128)(2,1)S(1)}, u32[]{:S(2)}, u32[]{:S(2)}) %collective-permute-start.65) | collective-permute-done | bytes 262176 | tf_op jit(solution)/shard_map/ppermute | solution.py:30
  118.0 1.2 collective-permute-start.70
  119.2 1.5 %collective-permute-start.68 = (bf16[2,128,256]{2,1,0:T(8,128)(2,1)S(1)}, bf16[2,128,256]{2,1,0:T(8,128)(2,1)S(1)}, u32[]{:S(2)}, u32[]{:S(2)}) collective-permute-start(bf16[2,128,256]{2,1,0:T(8,128)(2,1)S(1)} %get-tuple-element.150), channel_id=1, source_target_pairs={{0,4},{4,0},{8,12},{12,8},{16,20},{20,16},{24,28},{28,24},{1,5},{5... | collective-permute-start | bytes 393224 | tf_op jit(solution)/shard_map/ppermute | solution.py:30
  120.8 2.6 %collective-permute-start.66 = (bf16[1,256,256]{2,1,0:T(8,128)(2,1)S(1)}, bf16[1,256,256]{2,1,0:T(8,128)(2,1)S(1)}, u32[]{:S(2)}, u32[]{:S(2)}) collective-permute-start(bf16[1,256,256]{2,1,0:T(8,128)(2,1)S(1)} %get-tuple-element.146), channel_id=1, source_target_pairs={{0,16},{4,20},{8,24},{12,28},{16,0},{20,4},{24,8},{28,12},{1,17},{... | collective-permute-start | bytes 393224 | tf_op jit(solution)/shard_map/ppermute | solution.py:30
  123.5 3.9 %collective-permute-start.71 = (bf16[1,128,256]{2,1,0:T(8,128)(2,1)S(1)}, bf16[1,128,256]{2,1,0:T(8,128)(2,1)S(1)}, u32[]{:S(2)}, u32[]{:S(2)}) collective-permute-start(bf16[1,128,256]{2,1,0:T(8,128)(2,1)S(1)} %slice.205), channel_id=1, source_target_pairs={{0,16},{4,20},{8,24},{12,28},{16,0},{20,4},{24,8},{28,12},{1,17},{... | collective-permute-start | bytes 196616 | tf_op jit(solution)/shard_map/ppermute | solution.py:30
  127.5 5.6 %collective-permute-done.66 = bf16[1,256,256]{2,1,0:T(8,128)(2,1)S(1)} collective-permute-done((bf16[1,256,256]{2,1,0:T(8,128)(2,1)S(1)}, bf16[1,256,256]{2,1,0:T(8,128)(2,1)S(1)}, u32[]{:S(2)}, u32[]{:S(2)}) %collective-permute-start.66) | collective-permute-done | bytes 131104 | tf_op jit(solution)/shard_map/ppermute | solution.py:30
  133.2 0.8 collective-permute-done.71
  133.9 0.7 collective-permute-done.69
  134.6 0.7 collect.1
  (156 shorter events, 21.8 us)
Async XLA Ops:
  1.0 7.8 %collective-permute-start = (bf16[1,128,256]{2,1,0:T(8,128)(2,1)S(1)}, bf16[1,128,256]{2,1,0:T(8,128)(2,1)S(1)}, u32[]{:S(2)}, u32[]{:S(2)}) collective-permute-start(bf16[1,128,256]{2,1,0:T(8,128)(2,1)S(1)} %bitcast.23), channel_id=1, source_target_pairs={{0,16},{4,20},{8,24},{12,28},{16,0},{20,4},{24,8},{28,12},{1,17},{... | collective-permute-start | bytes 196616 | tf_op jit(solution)/shard_map/ppermute | solution.py:30
  5.1 6.5 %collective-permute-start.3 = (bf16[1,128,256]{2,1,0:T(8,128)(2,1)S(1)}, bf16[1,128,256]{2,1,0:T(8,128)(2,1)S(1)}, u32[]{:S(2)}, u32[]{:S(2)}) collective-permute-start(bf16[1,128,256]{2,1,0:T(8,128)(2,1)S(1)} %bitcast.26), channel_id=1, source_target_pairs={{0,16},{4,20},{8,24},{12,28},{16,0},{20,4},{24,8},{28,12},{1,17},{... | collective-permute-start | bytes 196616 | tf_op jit(solution)/shard_map/ppermute | solution.py:30
  8.7 10.2 %collective-permute-start.1 = (bf16[2,128,256]{2,1,0:T(8,128)(2,1)S(1)}, bf16[2,128,256]{2,1,0:T(8,128)(2,1)S(1)}, u32[]{:S(2)}, u32[]{:S(2)}) collective-permute-start(bf16[2,128,256]{2,1,0:T(8,128)(2,1)S(1)} %pad_maximum_fusion.2), channel_id=1, source_target_pairs={{0,8},{4,12},{8,0},{12,4},{16,24},{20,28},{24,16},{28,20},{1,9},{5... | collective-permute-start | bytes 393224 | tf_op jit(solution)/shard_map/ppermute | solution.py:30
  11.6 7.4 %collective-permute-start.4 = (bf16[2,128,256]{2,1,0:T(8,128)(2,1)S(1)}, bf16[2,128,256]{2,1,0:T(8,128)(2,1)S(1)}, u32[]{:S(2)}, u32[]{:S(2)}) collective-permute-start(bf16[2,128,256]{2,1,0:T(8,128)(2,1)S(1)} %pad_maximum_fusion.3), channel_id=1, source_target_pairs={{0,8},{4,12},{8,0},{12,4},{16,24},{20,28},{24,16},{28,20},{1,9},{5... | collective-permute-start | bytes 393224 | tf_op jit(solution)/shard_map/ppermute | solution.py:30
  15.4 11.3 %collective-permute-start.6 = (bf16[1,128,256]{2,1,0:T(8,128)(2,1)S(1)}, bf16[1,128,256]{2,1,0:T(8,128)(2,1)S(1)}, u32[]{:S(2)}, u32[]{:S(2)}) collective-permute-start(bf16[1,128,256]{2,1,0:T(8,128)(2,1)S(1)} %bitcast.29), channel_id=1, source_target_pairs={{0,16},{4,20},{8,24},{12,28},{16,0},{20,4},{24,8},{28,12},{1,17},{... | collective-permute-start | bytes 196616 | tf_op jit(solution)/shard_map/ppermute | solution.py:30
  18.9 7.8 %collective-permute-start.8 = (bf16[1,128,256]{2,1,0:T(8,128)(2,1)S(1)}, bf16[1,128,256]{2,1,0:T(8,128)(2,1)S(1)}, u32[]{:S(2)}, u32[]{:S(2)}) collective-permute-start(bf16[1,128,256]{2,1,0:T(8,128)(2,1)S(1)} %bitcast.32), channel_id=1, source_target_pairs={{0,16},{4,20},{8,24},{12,28},{16,0},{20,4},{24,8},{28,12},{1,17},{... | collective-permute-start | bytes 196616 | tf_op jit(solution)/shard_map/ppermute | solution.py:30
  19.0 9.8 %collective-permute-start.2 = (bf16[4,128,256]{2,1,0:T(8,128)(2,1)S(1)}, bf16[4,128,256]{2,1,0:T(8,128)(2,1)S(1)}, u32[]{:S(2)}, u32[]{:S(2)}) collective-permute-start(bf16[4,128,256]{2,1,0:T(8,128)(2,1)S(1)} %get-tuple-element.197.refs_0_), channel_id=1, source_target_pairs={{0,4},{4,0},{8,12},{12,8},{16,20},{20,16},{24,28},{28,24},{1,5},{5... | collective-permute-start | bytes 786440 | tf_op jit(solution)/shard_map/ppermute | solution.py:30
  20.6 14.6 %collective-permute-start.5 = (bf16[4,128,256]{2,1,0:T(8,128)(2,1)S(1)}, bf16[4,128,256]{2,1,0:T(8,128)(2,1)S(1)}, u32[]{:S(2)}, u32[]{:S(2)}) collective-permute-start(bf16[4,128,256]{2,1,0:T(8,128)(2,1)S(1)} %get-tuple-element.103.refs_0_), channel_id=1, source_target_pairs={{0,4},{4,0},{8,12},{12,8},{16,20},{20,16},{24,28},{28,24},{1,5},{5... | collective-permute-start | bytes 786440 | tf_op jit(solution)/shard_map/ppermute | solution.py:30
  26.8 8.4 %collective-permute-start.7 = (bf16[2,128,256]{2,1,0:T(8,128)(2,1)S(1)}, bf16[2,128,256]{2,1,0:T(8,128)(2,1)S(1)}, u32[]{:S(2)}, u32[]{:S(2)}) collective-permute-start(bf16[2,128,256]{2,1,0:T(8,128)(2,1)S(1)} %pad_maximum_fusion.4), channel_id=1, source_target_pairs={{0,8},{4,12},{8,0},{12,4},{16,24},{20,28},{24,16},{28,20},{1,9},{5... | collective-permute-start | bytes 393224 | tf_op jit(solution)/shard_map/ppermute | solution.py:30
  27.8 7.4 %collective-permute-start.9 = (bf16[2,128,256]{2,1,0:T(8,128)(2,1)S(1)}, bf16[2,128,256]{2,1,0:T(8,128)(2,1)S(1)}, u32[]{:S(2)}, u32[]{:S(2)}) collective-permute-start(bf16[2,128,256]{2,1,0:T(8,128)(2,1)S(1)} %pad_maximum_fusion.5), channel_id=1, source_target_pairs={{0,8},{4,12},{8,0},{12,4},{16,24},{20,28},{24,16},{28,20},{1,9},{5... | collective-permute-start | bytes 393224 | tf_op jit(solution)/shard_map/ppermute | solution.py:30
  35.3 12.0 %collective-permute-start.15 = (bf16[4,128,256]{2,1,0:T(8,128)(2,1)S(1)}, bf16[4,128,256]{2,1,0:T(8,128)(2,1)S(1)}, u32[]{:S(2)}, u32[]{:S(2)}) collective-permute-start(bf16[4,128,256]{2,1,0:T(8,128)(2,1)S(1)} %constant_dynamic-update-slice_fusion.refs_0_), channel_id=1, source_target_pairs={{0,4},{4,0},{8,12},{12,8},{16,20},{20,16},{24,28},{28,24},{1,5},{5... | collective-permute-start | bytes 786440 | tf_op jit(solution)/shard_map/ppermute | solution.py:30
  36.9 1.5 %collective-permute-start.13 = (bf16[32,3328]{1,0:T(8,128)(2,1)S(1)}, bf16[32,3328]{1,0:T(8,128)(2,1)S(1)}, u32[]{:S(2)}, u32[]{:S(2)}) collective-permute-start(bf16[32,3328]{1,0:T(8,128)(2,1)S(1)} %get-tuple-element.175), channel_id=1, source_target_pairs={{0,1},{1,0},{2,3},{3,2},{4,5},{5,4},{6,7},{7,6},{8,9},{9,8},{10,11... | collective-permute-start | bytes 638984 | tf_op jit(solution)/shard_map/ppermute | solution.py:30
  37.0 1.8 %collective-permute-start.12 = (bf16[32,3328]{1,0:T(8,128)(2,1)S(1)}, bf16[32,3328]{1,0:T(8,128)(2,1)S(1)}, u32[]{:S(2)}, u32[]{:S(2)}) collective-permute-start(bf16[32,3328]{1,0:T(8,128)(2,1)S(1)} %get-tuple-element.176), channel_id=1, source_target_pairs={{0,1},{1,0},{2,3},{3,2},{4,5},{5,4},{6,7},{7,6},{8,9},{9,8},{10,11... | collective-permute-start | bytes 638984 | tf_op jit(solution)/shard_map/ppermute | solution.py:30
  37.5 1.6 %collective-permute-start.11 = (bf16[32,3328]{1,0:T(8,128)(2,1)S(1)}, bf16[32,3328]{1,0:T(8,128)(2,1)S(1)}, u32[]{:S(2)}, u32[]{:S(2)}) collective-permute-start(bf16[32,3328]{1,0:T(8,128)(2,1)S(1)} %get-tuple-element.177), channel_id=1, source_target_pairs={{0,1},{1,0},{2,3},{3,2},{4,5},{5,4},{6,7},{7,6},{8,9},{9,8},{10,11... | collective-permute-start | bytes 638984 | tf_op jit(solution)/shard_map/ppermute | solution.py:30
  37.6 1.8 %collective-permute-start.10 = (bf16[32,3328]{1,0:T(8,128)(2,1)S(1)}, bf16[32,3328]{1,0:T(8,128)(2,1)S(1)}, u32[]{:S(2)}, u32[]{:S(2)}) collective-permute-start(bf16[32,3328]{1,0:T(8,128)(2,1)S(1)} %get-tuple-element.178), channel_id=1, source_target_pairs={{0,1},{1,0},{2,3},{3,2},{4,5},{5,4},{6,7},{7,6},{8,9},{9,8},{10,11... | collective-permute-start | bytes 638984 | tf_op jit(solution)/shard_map/ppermute | solution.py:30
  39.6 12.9 %collective-permute-start.14 = (bf16[1,2,32,3328]{3,2,1,0:T(8,128)(2,1)S(1)}, bf16[1,2,32,3328]{3,2,1,0:T(8,128)(2,1)S(1)}, u32[]{:S(2)}, u32[]{:S(2)}) collective-permute-start(bf16[1,2,32,3328]{3,2,1,0:T(8,128)(2,1)S(1)} %get-tuple-element.102), channel_id=1, source_target_pairs={{0,2},{1,3},{2,0},{3,1},{4,6},{5,7},{6,4},{7,5},{8,10},{9,11},{10,... | collective-permute-start | bytes 1277960 | tf_op jit(solution)/shard_map/ppermute | solution.py:30
  47.4 1.5 %collective-permute-start.22 = (bf16[16,3328]{1,0:T(8,128)(2,1)S(1)}, bf16[16,3328]{1,0:T(8,128)(2,1)S(1)}, u32[]{:S(2)}, u32[]{:S(2)}) collective-permute-start(bf16[16,3328]{1,0:T(8,128)(2,1)S(1)} %get-tuple-element.168), channel_id=1, source_target_pairs={{0,1},{1,0},{2,3},{3,2},{4,5},{5,4},{6,7},{7,6},{8,9},{9,8},{10,11... | collective-permute-start | bytes 319496 | tf_op jit(solution)/shard_map/ppermute | solution.py:30
  47.9 11.0 %collective-permute-start.24 = (bf16[4,128,256]{2,1,0:T(8,128)(2,1)S(1)}, bf16[4,128,256]{2,1,0:T(8,128)(2,1)S(1)}, u32[]{:S(2)}, u32[]{:S(2)}) collective-permute-start(bf16[4,128,256]{2,1,0:T(8,128)(2,1)S(1)} %constant_dynamic-update-slice_fusion.3.refs_0_), channel_id=1, source_target_pairs={{0,4},{4,0},{8,12},{12,8},{16,20},{20,16},{24,28},{28,24},{1,5},{5... | collective-permute-start | bytes 786440 | tf_op jit(solution)/shard_map/ppermute | solution.py:30
  51.9 16.7 %collective-permute-start.34 = (bf16[1,2,32,3328]{3,2,1,0:T(8,128)(2,1)S(1)}, bf16[1,2,32,3328]{3,2,1,0:T(8,128)(2,1)S(1)}, u32[]{:S(2)}, u32[]{:S(2)}) collective-permute-start(bf16[1,2,32,3328]{3,2,1,0:T(8,128)(2,1)S(1)} %get-tuple-element.109), channel_id=1, source_target_pairs={{0,2},{1,3},{2,0},{3,1},{4,6},{5,7},{6,4},{7,5},{8,10},{9,11},{10,... | collective-permute-start | bytes 1277960 | tf_op jit(solution)/shard_map/ppermute | solution.py:30
  59.6 2.5 %collective-permute-start.30 = (bf16[16,3328]{1,0:T(8,128)(2,1)S(1)}, bf16[16,3328]{1,0:T(8,128)(2,1)S(1)}, u32[]{:S(2)}, u32[]{:S(2)}) collective-permute-start(bf16[16,3328]{1,0:T(8,128)(2,1)S(1)} %get-tuple-element.161), channel_id=1, source_target_pairs={{0,1},{1,0},{2,3},{3,2},{4,5},{5,4},{6,7},{7,6},{8,9},{9,8},{10,11... | collective-permute-start | bytes 319496 | tf_op jit(solution)/shard_map/ppermute | solution.py:30
  59.7 2.5 %collective-permute-start.29 = (bf16[16,3328]{1,0:T(8,128)(2,1)S(1)}, bf16[16,3328]{1,0:T(8,128)(2,1)S(1)}, u32[]{:S(2)}, u32[]{:S(2)}) collective-permute-start(bf16[16,3328]{1,0:T(8,128)(2,1)S(1)} %get-tuple-element.162), channel_id=1, source_target_pairs={{0,1},{1,0},{2,3},{3,2},{4,5},{5,4},{6,7},{7,6},{8,9},{9,8},{10,11... | collective-permute-start | bytes 319496 | tf_op jit(solution)/shard_map/ppermute | solution.py:30
  60.4 2.2 %collective-permute-start.28 = (bf16[16,3328]{1,0:T(8,128)(2,1)S(1)}, bf16[16,3328]{1,0:T(8,128)(2,1)S(1)}, u32[]{:S(2)}, u32[]{:S(2)}) collective-permute-start(bf16[16,3328]{1,0:T(8,128)(2,1)S(1)} %get-tuple-element.163), channel_id=1, source_target_pairs={{0,1},{1,0},{2,3},{3,2},{4,5},{5,4},{6,7},{7,6},{8,9},{9,8},{10,11... | collective-permute-start | bytes 319496 | tf_op jit(solution)/shard_map/ppermute | solution.py:30
  60.6 8.2 %collective-permute-start.35 = (bf16[32,3328]{1,0:T(8,128)(2,1)S(1)}, bf16[32,3328]{1,0:T(8,128)(2,1)S(1)}, u32[]{:S(2)}, u32[]{:S(2)}) collective-permute-start(bf16[32,3328]{1,0:T(8,128)(2,1)S(1)} %gated.4.refs_0_), channel_id=1, source_target_pairs={{0,2},{1,3},{2,0},{3,1},{4,6},{5,7},{6,4},{7,5},{8,10},{9,11},{10,... | collective-permute-start | bytes 638984 | tf_op jit(solution)/shard_map/ppermute | solution.py:30
  64.2 20.8 %collective-permute-start.33 = (bf16[1,2,32,3328]{3,2,1,0:T(8,128)(2,1)S(1)}, bf16[1,2,32,3328]{3,2,1,0:T(8,128)(2,1)S(1)}, u32[]{:S(2)}, u32[]{:S(2)}) collective-permute-start(bf16[1,2,32,3328]{3,2,1,0:T(8,128)(2,1)S(1)} %get-tuple-element.118), channel_id=1, source_target_pairs={{0,2},{1,3},{2,0},{3,1},{4,6},{5,7},{6,4},{7,5},{8,10},{9,11},{10,... | collective-permute-start | bytes 1277960 | tf_op jit(solution)/shard_map/ppermute | solution.py:30
  76.0 2.3 %collective-permute-start.41 = (bf16[16,3328]{1,0:T(8,128)(2,1)S(1)}, bf16[16,3328]{1,0:T(8,128)(2,1)S(1)}, u32[]{:S(2)}, u32[]{:S(2)}) collective-permute-start(bf16[16,3328]{1,0:T(8,128)(2,1)S(1)} %get-tuple-element.153), channel_id=1, source_target_pairs={{0,1},{1,0},{2,3},{3,2},{4,5},{5,4},{6,7},{7,6},{8,9},{9,8},{10,11... | collective-permute-start | bytes 319496 | tf_op jit(solution)/shard_map/ppermute | solution.py:30
  76.1 2.3 %collective-permute-start.40 = (bf16[16,3328]{1,0:T(8,128)(2,1)S(1)}, bf16[16,3328]{1,0:T(8,128)(2,1)S(1)}, u32[]{:S(2)}, u32[]{:S(2)}) collective-permute-start(bf16[16,3328]{1,0:T(8,128)(2,1)S(1)} %get-tuple-element.154), channel_id=1, source_target_pairs={{0,1},{1,0},{2,3},{3,2},{4,5},{5,4},{6,7},{7,6},{8,9},{9,8},{10,11... | collective-permute-start | bytes 319496 | tf_op jit(solution)/shard_map/ppermute | solution.py:30
  76.8 2.0 %collective-permute-start.39 = (bf16[16,3328]{1,0:T(8,128)(2,1)S(1)}, bf16[16,3328]{1,0:T(8,128)(2,1)S(1)}, u32[]{:S(2)}, u32[]{:S(2)}) collective-permute-start(bf16[16,3328]{1,0:T(8,128)(2,1)S(1)} %get-tuple-element.155), channel_id=1, source_target_pairs={{0,1},{1,0},{2,3},{3,2},{4,5},{5,4},{6,7},{7,6},{8,9},{9,8},{10,11... | collective-permute-start | bytes 319496 | tf_op jit(solution)/shard_map/ppermute | solution.py:30
  76.9 8.1 %collective-permute-start.44 = (bf16[32,3328]{1,0:T(8,128)(2,1)S(1)}, bf16[32,3328]{1,0:T(8,128)(2,1)S(1)}, u32[]{:S(2)}, u32[]{:S(2)}) collective-permute-start(bf16[32,3328]{1,0:T(8,128)(2,1)S(1)} %gated.5.refs_6_), channel_id=1, source_target_pairs={{0,2},{1,3},{2,0},{3,1},{4,6},{5,7},{6,4},{7,5},{8,10},{9,11},{10,... | collective-permute-start | bytes 638984 | tf_op jit(solution)/shard_map/ppermute | solution.py:30
  80.4 16.7 %collective-permute-start.54 = (bf16[1,2,32,3328]{3,2,1,0:T(8,128)(2,1)S(1)}, bf16[1,2,32,3328]{3,2,1,0:T(8,128)(2,1)S(1)}, u32[]{:S(2)}, u32[]{:S(2)}) collective-permute-start(bf16[1,2,32,3328]{3,2,1,0:T(8,128)(2,1)S(1)} %get-tuple-element.125), channel_id=1, source_target_pairs={{0,2},{1,3},{2,0},{3,1},{4,6},{5,7},{6,4},{7,5},{8,10},{9,11},{10,... | collective-permute-start | bytes 1277960 | tf_op jit(solution)/shard_map/ppermute | solution.py:30
  87.4 2.2 %collective-permute-start.52 = (bf16[16,3328]{1,0:T(8,128)(2,1)S(1)}, bf16[16,3328]{1,0:T(8,128)(2,1)S(1)}, u32[]{:S(2)}, u32[]{:S(2)}) collective-permute-start(bf16[16,3328]{1,0:T(8,128)(2,1)S(1)} %get-tuple-element.189), channel_id=1, source_target_pairs={{0,1},{1,0},{2,3},{3,2},{4,5},{5,4},{6,7},{7,6},{8,9},{9,8},{10,11... | collective-permute-start | bytes 319496 | tf_op jit(solution)/shard_map/ppermute | solution.py:30
  87.6 2.1 %collective-permute-start.51 = (bf16[16,3328]{1,0:T(8,128)(2,1)S(1)}, bf16[16,3328]{1,0:T(8,128)(2,1)S(1)}, u32[]{:S(2)}, u32[]{:S(2)}) collective-permute-start(bf16[16,3328]{1,0:T(8,128)(2,1)S(1)} %get-tuple-element.190), channel_id=1, source_target_pairs={{0,1},{1,0},{2,3},{3,2},{4,5},{5,4},{6,7},{7,6},{8,9},{9,8},{10,11... | collective-permute-start | bytes 319496 | tf_op jit(solution)/shard_map/ppermute | solution.py:30
  88.1 10.1 %collective-permute-start.56 = (bf16[32,3328]{1,0:T(8,128)(2,1)S(1)}, bf16[32,3328]{1,0:T(8,128)(2,1)S(1)}, u32[]{:S(2)}, u32[]{:S(2)}) collective-permute-start(bf16[32,3328]{1,0:T(8,128)(2,1)S(1)} %gated.6.refs_0_), channel_id=1, source_target_pairs={{0,1},{1,0},{2,3},{3,2},{4,5},{5,4},{6,7},{7,6},{8,9},{9,8},{10,11... | collective-permute-start | bytes 638984 | tf_op jit(solution)/shard_map/ppermute | solution.py:30
  88.3 9.9 %collective-permute-start.55 = (bf16[32,3328]{1,0:T(8,128)(2,1)S(1)}, bf16[32,3328]{1,0:T(8,128)(2,1)S(1)}, u32[]{:S(2)}, u32[]{:S(2)}) collective-permute-start(bf16[32,3328]{1,0:T(8,128)(2,1)S(1)} %gated.6.refs_0_), channel_id=1, source_target_pairs={{0,2},{1,3},{2,0},{3,1},{4,6},{5,7},{6,4},{7,5},{8,10},{9,11},{10,... | collective-permute-start | bytes 638984 | tf_op jit(solution)/shard_map/ppermute | solution.py:30
  95.0 16.0 %collective-permute-start.53 = (bf16[2,256,256]{2,1,0:T(8,128)(2,1)S(1)}, bf16[2,256,256]{2,1,0:T(8,128)(2,1)S(1)}, u32[]{:S(2)}, u32[]{:S(2)}) collective-permute-start(bf16[2,256,256]{2,1,0:T(8,128)(2,1)S(1)} %get-tuple-element.179), channel_id=1, source_target_pairs={{0,4},{4,0},{8,12},{12,8},{16,20},{20,16},{24,28},{28,24},{1,5},{5... | collective-permute-start | bytes 786440 | tf_op jit(solution)/shard_map/ppermute | solution.py:30
  96.6 14.5 %collective-permute-start.63 = (bf16[2,256,256]{2,1,0:T(8,128)(2,1)S(1)}, bf16[2,256,256]{2,1,0:T(8,128)(2,1)S(1)}, u32[]{:S(2)}, u32[]{:S(2)}) collective-permute-start(bf16[2,256,256]{2,1,0:T(8,128)(2,1)S(1)} %get-tuple-element.180), channel_id=1, source_target_pairs={{0,4},{4,0},{8,12},{12,8},{16,20},{20,16},{24,28},{28,24},{1,5},{5... | collective-permute-start | bytes 786440 | tf_op jit(solution)/shard_map/ppermute | solution.py:30
  97.5 6.7 %collective-permute-start.58 = (bf16[32,3328]{1,0:T(8,128)(2,1)S(1)}, bf16[32,3328]{1,0:T(8,128)(2,1)S(1)}, u32[]{:S(2)}, u32[]{:S(2)}) collective-permute-start(bf16[32,3328]{1,0:T(8,128)(2,1)S(1)} %gated.7.refs_0_), channel_id=1, source_target_pairs={{0,2},{1,3},{2,0},{3,1},{4,6},{5,7},{6,4},{7,5},{8,10},{9,11},{10,... | collective-permute-start | bytes 638984 | tf_op jit(solution)/shard_map/ppermute | solution.py:30
  98.2 6.1 %collective-permute-start.60 = (bf16[16,3328]{1,0:T(8,128)(2,1)S(1)}, bf16[16,3328]{1,0:T(8,128)(2,1)S(1)}, u32[]{:S(2)}, u32[]{:S(2)}) collective-permute-start(bf16[16,3328]{1,0:T(8,128)(2,1)S(1)} %get-tuple-element.187), channel_id=1, source_target_pairs={{0,1},{1,0},{2,3},{3,2},{4,5},{5,4},{6,7},{7,6},{8,9},{9,8},{10,11... | collective-permute-start | bytes 319496 | tf_op jit(solution)/shard_map/ppermute | solution.py:30
  99.7 5.1 %collective-permute-start.59 = (bf16[16,3328]{1,0:T(8,128)(2,1)S(1)}, bf16[16,3328]{1,0:T(8,128)(2,1)S(1)}, u32[]{:S(2)}, u32[]{:S(2)}) collective-permute-start(bf16[16,3328]{1,0:T(8,128)(2,1)S(1)} %get-tuple-element.188), channel_id=1, source_target_pairs={{0,1},{1,0},{2,3},{3,2},{4,5},{5,4},{6,7},{7,6},{8,9},{9,8},{10,11... | collective-permute-start | bytes 319496 | tf_op jit(solution)/shard_map/ppermute | solution.py:30
  104.2 1.7 %collective-permute-start.62 = (bf16[16,3328]{1,0:T(8,128)(2,1)S(1)}, bf16[16,3328]{1,0:T(8,128)(2,1)S(1)}, u32[]{:S(2)}, u32[]{:S(2)}) collective-permute-start(bf16[16,3328]{1,0:T(8,128)(2,1)S(1)} %get-tuple-element.185), channel_id=1, source_target_pairs={{0,1},{1,0},{2,3},{3,2},{4,5},{5,4},{6,7},{7,6},{8,9},{9,8},{10,11... | collective-permute-start | bytes 319496 | tf_op jit(solution)/shard_map/ppermute | solution.py:30
  104.3 1.6 %collective-permute-start.61 = (bf16[16,3328]{1,0:T(8,128)(2,1)S(1)}, bf16[16,3328]{1,0:T(8,128)(2,1)S(1)}, u32[]{:S(2)}, u32[]{:S(2)}) collective-permute-start(bf16[16,3328]{1,0:T(8,128)(2,1)S(1)} %get-tuple-element.186), channel_id=1, source_target_pairs={{0,1},{1,0},{2,3},{3,2},{4,5},{5,4},{6,7},{7,6},{8,9},{9,8},{10,11... | collective-permute-start | bytes 319496 | tf_op jit(solution)/shard_map/ppermute | solution.py:30
  104.8 8.3 %collective-permute-start.67 = (bf16[4,128,256]{2,1,0:T(8,128)(2,1)S(1)}, bf16[4,128,256]{2,1,0:T(8,128)(2,1)S(1)}, u32[]{:S(2)}, u32[]{:S(2)}) collective-permute-start(bf16[4,128,256]{2,1,0:T(8,128)(2,1)S(1)} %get-tuple-element.138), channel_id=1, source_target_pairs={{0,8},{4,12},{8,0},{12,4},{16,24},{20,28},{24,16},{28,20},{1,9},{5... | collective-permute-start | bytes 786440 | tf_op jit(solution)/shard_map/ppermute | solution.py:30
  109.5 8.4 %collective-permute-start.65 = (bf16[4,128,256]{2,1,0:T(8,128)(2,1)S(1)}, bf16[4,128,256]{2,1,0:T(8,128)(2,1)S(1)}, u32[]{:S(2)}, u32[]{:S(2)}) collective-permute-start(bf16[4,128,256]{2,1,0:T(8,128)(2,1)S(1)} %get-tuple-element.141), channel_id=1, source_target_pairs={{0,4},{4,0},{8,12},{12,8},{16,20},{20,16},{24,28},{28,24},{1,5},{5... | collective-permute-start | bytes 786440 | tf_op jit(solution)/shard_map/ppermute | solution.py:30
  111.1 9.6 %collective-permute-start.64 = (bf16[2,256,256]{2,1,0:T(8,128)(2,1)S(1)}, bf16[2,256,256]{2,1,0:T(8,128)(2,1)S(1)}, u32[]{:S(2)}, u32[]{:S(2)}) collective-permute-start(bf16[2,256,256]{2,1,0:T(8,128)(2,1)S(1)} %add_convert_fusion.3), channel_id=1, source_target_pairs={{0,8},{4,12},{8,0},{12,4},{16,24},{20,28},{24,16},{28,20},{1,9},{5... | collective-permute-start | bytes 786440 | tf_op jit(solution)/shard_map/ppermute | solution.py:30
  118.0 5.4 %collective-permute-start.70 = (bf16[2,128,256]{2,1,0:T(8,128)(2,1)S(1)}, bf16[2,128,256]{2,1,0:T(8,128)(2,1)S(1)}, u32[]{:S(2)}, u32[]{:S(2)}) collective-permute-start(bf16[2,128,256]{2,1,0:T(8,128)(2,1)S(1)} %slice.197), channel_id=1, source_target_pairs={{0,8},{4,12},{8,0},{12,4},{16,24},{20,28},{24,16},{28,20},{1,9},{5... | collective-permute-start | bytes 393224 | tf_op jit(solution)/shard_map/ppermute | solution.py:30
  119.2 8.2 %collective-permute-start.68 = (bf16[2,128,256]{2,1,0:T(8,128)(2,1)S(1)}, bf16[2,128,256]{2,1,0:T(8,128)(2,1)S(1)}, u32[]{:S(2)}, u32[]{:S(2)}) collective-permute-start(bf16[2,128,256]{2,1,0:T(8,128)(2,1)S(1)} %get-tuple-element.150), channel_id=1, source_target_pairs={{0,4},{4,0},{8,12},{12,8},{16,20},{20,16},{24,28},{28,24},{1,5},{5... | collective-permute-start | bytes 393224 | tf_op jit(solution)/shard_map/ppermute | solution.py:30
  120.8 12.3 %collective-permute-start.66 = (bf16[1,256,256]{2,1,0:T(8,128)(2,1)S(1)}, bf16[1,256,256]{2,1,0:T(8,128)(2,1)S(1)}, u32[]{:S(2)}, u32[]{:S(2)}) collective-permute-start(bf16[1,256,256]{2,1,0:T(8,128)(2,1)S(1)} %get-tuple-element.146), channel_id=1, source_target_pairs={{0,16},{4,20},{8,24},{12,28},{16,0},{20,4},{24,8},{28,12},{1,17},{... | collective-permute-start | bytes 393224 | tf_op jit(solution)/shard_map/ppermute | solution.py:30
  123.5 10.4 %collective-permute-start.71 = (bf16[1,128,256]{2,1,0:T(8,128)(2,1)S(1)}, bf16[1,128,256]{2,1,0:T(8,128)(2,1)S(1)}, u32[]{:S(2)}, u32[]{:S(2)}) collective-permute-start(bf16[1,128,256]{2,1,0:T(8,128)(2,1)S(1)} %slice.205), channel_id=1, source_target_pairs={{0,16},{4,20},{8,24},{12,28},{16,0},{20,4},{24,8},{28,12},{1,17},{... | collective-permute-start | bytes 196616 | tf_op jit(solution)/shard_map/ppermute | solution.py:30
  127.4 7.2 %collective-permute-start.69 = (bf16[1,128,256]{2,1,0:T(8,128)(2,1)S(1)}, bf16[1,128,256]{2,1,0:T(8,128)(2,1)S(1)}, u32[]{:S(2)}, u32[]{:S(2)}) collective-permute-start(bf16[1,128,256]{2,1,0:T(8,128)(2,1)S(1)} %slice.202), channel_id=1, source_target_pairs={{0,16},{4,20},{8,24},{12,28},{16,0},{20,4},{24,8},{28,12},{1,17},{... | collective-permute-start | bytes 196616 | tf_op jit(solution)/shard_map/ppermute | solution.py:30
  (25 other events, 33.6 us)

commit v5 on v4

--- a/solution.py
+++ b/solution.py
@@ -410,9 +410,9 @@
         gate.append(decode_part(after(gw, gate[0], tok[0][0]), gs, 1, 2))
         for k in (2, 3):
             tok[k] = [after(tok[k][0], gate[1])]
-        for k in (0, 1):
-            gather_tokens(k, 1, gate[1])
-        up = [decode_part(after(uw, tok[0][0], tok[1][0]), us, 0, 1)]
+        gather_tokens(0, 1, gate[1])
+        up = [decode_part(after(uw, tok[0][0]), us, 0, 1)]
+        gather_tokens(1, 1, up[0])
         for k in (2, 3):
             gather_tokens(k, wide_bits - 1, up[0])
         gather_tokens(0, 0, up[0])

time: 136 us -> 136 us (level)
  no operation moved by 1% of the time
where the time goes in v5:
time: 136 us; the launch traced here: 135 us
  Pallas kernels  59.4 us (44%)
  starting transfers between devices  50.5 us (37%)
  waiting for transfers between devices  23 us (17%)
  local copies, waits for them, and re-layouts  1.41 us (1%)
    ppermute x72, starting transfers between devices, flip(): return lax.ppermute(array, axis, [(i, i ^ mask) for i in range(size)])  50.5 us
    pallas_call x4, Pallas kernels, gate_up(): pl.pallas_call(functools.partial(gate_up_kernel, len(shards), len(gate),...  24.6 us
    ppermute x72, waiting for transfers between devices, flip(): return lax.ppermute(array, axis, [(i, i ^ mask) for i in range(size)])  23 us
    pallas_call x5, Pallas kernels, decode_part(): pl.pallas_call(functools.partial(decode_kernel, part * size, block), in_s...  19.2 us
    pallas_call x3, Pallas kernels, down(): pl.pallas_call(functools.partial(down_kernel, len(hidden), len(weights),...  12.3 us
  transfers between devices with their start and end apart: 72, of which 32 were waited for; matrix products, arithmetic and copies ran while one was open for 1% of the time, Pallas kernels for 43%

profile of v5, /device:TPU:0, one launch (start us, length us, event | category | flops | bytes accessed | tf_op | source)
XLA Modules:
  0.0 135.4 jit_solution(12887349484055888539)
XLA Ops:
  0.0 0.9 copy-done
  1.0 4.1 %collective-permute-start = (bf16[1,128,256]{2,1,0:T(8,128)(2,1)S(1)}, bf16[1,128,256]{2,1,0:T(8,128)(2,1)S(1)}, u32[]{:S(2)}, u32[]{:S(2)}) collective-permute-start(bf16[1,128,256]{2,1,0:T(8,128)(2,1)S(1)} %bitcast.32), channel_id=1, source_target_pairs={{0,16},{4,20},{8,24},{12,28},{16,0},{20,4},{24,8},{28,12},{1,17},{... | collective-permute-start | bytes 196616 | tf_op jit(solution)/shard_map/ppermute | solution.py:30
  5.2 3.2 %decode.5.refs_2_ = bf16[1024,3328]{1,0:T(8,128)(2,1)S(1)} custom-call(bf16[2048,3328]{1,0:T(8,128)(2,1)} %w_ref.1, f32[16,3328]{1,0:T(8,128)} %sc_ref.6), custom_call_target="tpu_custom_call" | custom-call | flops 1024 | bytes 1024 | tf_op jit(solution)/shard_map/decode/pallas_call | solution.py:82
  8.7 2.1 %collective-permute-start.1 = (bf16[2,128,256]{2,1,0:T(8,128)(2,1)S(1)}, bf16[2,128,256]{2,1,0:T(8,128)(2,1)S(1)}, u32[]{:S(2)}, u32[]{:S(2)}) collective-permute-start(bf16[2,128,256]{2,1,0:T(8,128)(2,1)S(1)} %pad_maximum_fusion.2), channel_id=1, source_target_pairs={{0,8},{4,12},{8,0},{12,4},{16,24},{20,28},{24,16},{28,20},{1,9},{5... | collective-permute-start | bytes 393224 | tf_op jit(solution)/shard_map/ppermute | solution.py:30
  10.9 0.7 collective-permute-done.3
  11.6 3.2 %decode.6.refs_3_ = bf16[1024,3328]{1,0:T(8,128)(2,1)S(1)} custom-call(bf16[2048,3328]{1,0:T(8,128)(2,1)} %w_ref.1, f32[16,3328]{1,0:T(8,128)} %sc_ref.6), custom_call_target="tpu_custom_call" | custom-call | flops 1024 | bytes 1024 | tf_op jit(solution)/shard_map/decode/pallas_call | solution.py:82
  14.8 2.8 %collective-permute-start.6 = (bf16[1,128,256]{2,1,0:T(8,128)(2,1)S(1)}, bf16[1,128,256]{2,1,0:T(8,128)(2,1)S(1)}, u32[]{:S(2)}, u32[]{:S(2)}) collective-permute-start(bf16[1,128,256]{2,1,0:T(8,128)(2,1)S(1)} %bitcast.23), channel_id=1, source_target_pairs={{0,16},{4,20},{8,24},{12,28},{16,0},{20,4},{24,8},{28,12},{1,17},{... | collective-permute-start | bytes 196616 | tf_op jit(solution)/shard_map/ppermute | solution.py:30
  17.6 1.2 collective-permute-start.4
  19.0 1.6 %collective-permute-start.2 = (bf16[4,128,256]{2,1,0:T(8,128)(2,1)S(1)}, bf16[4,128,256]{2,1,0:T(8,128)(2,1)S(1)}, u32[]{:S(2)}, u32[]{:S(2)}) collective-permute-start(bf16[4,128,256]{2,1,0:T(8,128)(2,1)S(1)} %pad_maximum_fusion.refs_0_), channel_id=1, source_target_pairs={{0,4},{4,0},{8,12},{12,8},{16,20},{20,16},{24,28},{28,24},{1,5},{5... | collective-permute-start | bytes 786440 | tf_op jit(solution)/shard_map/ppermute | solution.py:30
  20.5 5.6 %decode.7.refs_4_ = bf16[2048,3328]{1,0:T(8,128)(2,1)S(1)} custom-call(bf16[2048,3328]{1,0:T(8,128)(2,1)} %w_ref.2, f32[16,3328]{1,0:T(8,128)} %sc_ref.7), custom_call_target="tpu_custom_call" | custom-call | flops 1024 | bytes 1024 | tf_op jit(solution)/shard_map/decode/pallas_call | solution.py:82
  26.8 1.0 collective-permute-start.7
  27.8 1.1 collective-permute-start.9
  28.9 6.3 %gate_up.4 = (bf16[2,2,32,3328]{3,2,1,0:T(8,128)(2,1)S(1)}, bf16[2,2,32,3328]{3,2,1,0:T(8,128)(2,1)S(1)}) custom-call(s32[1]{0:T(128)} %bitcast.1.place_ref, bf16[4,128,256]{2,1,0:T(8,128)(2,1)S(1)} %pad_maximum_fusion.refs_0_, bf16[4,128,256]{2,1,0:T(8,128)(2,1)S(1)} %collective-permute-done.2.refs_1_, bf16[1024,3328]{1,0:T(8,128)(2,1)S(1)} %decode.5.refs_2_, ...), custom_call_target="tpu_custom_call" | custom-call | flops 1024 | bytes 1024 | tf_op jit(solution)/shard_map/gate_up/pallas_call | solution.py:149
  35.3 1.6 %collective-permute-start.15 = (bf16[4,128,256]{2,1,0:T(8,128)(2,1)S(1)}, bf16[4,128,256]{2,1,0:T(8,128)(2,1)S(1)}, u32[]{:S(2)}, u32[]{:S(2)}) collective-permute-start(bf16[4,128,256]{2,1,0:T(8,128)(2,1)S(1)} %get-tuple-element.111.refs_0_), channel_id=1, source_target_pairs={{0,4},{4,0},{8,12},{12,8},{16,20},{20,16},{24,28},{28,24},{1,5},{5... | collective-permute-start | bytes 786440 | tf_op jit(solution)/shard_map/ppermute | solution.py:30
  39.6 1.6 %collective-permute-start.14 = (bf16[1,2,32,3328]{3,2,1,0:T(8,128)(2,1)S(1)}, bf16[1,2,32,3328]{3,2,1,0:T(8,128)(2,1)S(1)}, u32[]{:S(2)}, u32[]{:S(2)}) collective-permute-start(bf16[1,2,32,3328]{3,2,1,0:T(8,128)(2,1)S(1)} %get-tuple-element.102), channel_id=1, source_target_pairs={{0,2},{1,3},{2,0},{3,1},{4,6},{5,7},{6,4},{7,5},{8,10},{9,11},{10,... | collective-permute-start | bytes 1277960 | tf_op jit(solution)/shard_map/ppermute | solution.py:30
  41.2 6.1 %gate_up.5 = (bf16[2,2,32,3328]{3,2,1,0:T(8,128)(2,1)S(1)}, bf16[2,2,32,3328]{3,2,1,0:T(8,128)(2,1)S(1)}) custom-call(s32[1]{0:T(128)} %bitcast.1.place_ref, bf16[4,128,256]{2,1,0:T(8,128)(2,1)S(1)} %pad_maximum_fusion.1.refs_0_, bf16[4,128,256]{2,1,0:T(8,128)(2,1)S(1)} %collective-permute-done.5.refs_1_, bf16[1024,3328]{1,0:T(8,128)(2,1)S(1)} %decode.5.refs_2_, ...), custom_call_target="tpu_custom_call" | custom-call | flops 1024 | bytes 1024 | tf_op jit(solution)/shard_map/gate_up/pallas_call | solution.py:149
  51.9 0.6 collective-permute-start.34
  52.9 6.1 %gate_up.6 = (bf16[2,2,32,3328]{3,2,1,0:T(8,128)(2,1)S(1)}, bf16[2,2,32,3328]{3,2,1,0:T(8,128)(2,1)S(1)}) custom-call(s32[1]{0:T(128)} %bitcast.1.place_ref, bf16[4,128,256]{2,1,0:T(8,128)(2,1)S(1)} %get-tuple-element.111.refs_0_, bf16[4,128,256]{2,1,0:T(8,128)(2,1)S(1)} %collective-permute-done.15.refs_1_, bf16[1024,3328]{1,0:T(8,128)(2,1)S(1)} %decode.5.refs_2_, ...), custom_call_target="tpu_custom_call" | custom-call | flops 1024 | bytes 1024 | tf_op jit(solution)/shard_map/gate_up/pallas_call | solution.py:149
  60.6 1.5 %collective-permute-start.35 = (bf16[32,3328]{1,0:T(8,128)(2,1)S(1)}, bf16[32,3328]{1,0:T(8,128)(2,1)S(1)}, u32[]{:S(2)}, u32[]{:S(2)}) collective-permute-start(bf16[32,3328]{1,0:T(8,128)(2,1)S(1)} %gated.4.refs_0_), channel_id=1, source_target_pairs={{0,2},{1,3},{2,0},{3,1},{4,6},{5,7},{6,4},{7,5},{8,10},{9,11},{10,... | collective-permute-start | bytes 638984 | tf_op jit(solution)/shard_map/ppermute | solution.py:30
  62.7 0.7 collective-permute-done.27.refs_2_
  64.2 0.7 collective-permute-start.33
  64.9 3.6 %decode.8.refs_12_.refs_4_.refs_6_ = bf16[1664,2048]{1,0:T(8,128)(2,1)S(1)} custom-call(bf16[3328,2048]{1,0:T(8,128)(2,1)} %w_ref.4, f32[26,2048]{1,0:T(8,128)} %sc_ref.9), custom_call_target="tpu_custom_call" | custom-call | flops 1024 | bytes 1024 | tf_op jit(solution)/shard_map/decode/pallas_call | solution.py:82
  69.2 6.1 %gate_up.7 = (bf16[2,2,32,3328]{3,2,1,0:T(8,128)(2,1)S(1)}, bf16[2,2,32,3328]{3,2,1,0:T(8,128)(2,1)S(1)}) custom-call(s32[1]{0:T(128)} %bitcast.1.place_ref, bf16[4,128,256]{2,1,0:T(8,128)(2,1)S(1)} %get-tuple-element.122.refs_0_, bf16[4,128,256]{2,1,0:T(8,128)(2,1)S(1)} %collective-permute-done.24.refs_1_, bf16[1024,3328]{1,0:T(8,128)(2,1)S(1)} %decode.5.refs_2_, ...), custom_call_target="tpu_custom_call" | custom-call | flops 1024 | bytes 1024 | tf_op jit(solution)/shard_map/gate_up/pallas_call | solution.py:149
  76.9 1.4 %collective-permute-start.44 = (bf16[32,3328]{1,0:T(8,128)(2,1)S(1)}, bf16[32,3328]{1,0:T(8,128)(2,1)S(1)}, u32[]{:S(2)}, u32[]{:S(2)}) collective-permute-start(bf16[32,3328]{1,0:T(8,128)(2,1)S(1)} %gated.5.refs_6_), channel_id=1, source_target_pairs={{0,2},{1,3},{2,0},{3,1},{4,6},{5,7},{6,4},{7,5},{8,10},{9,11},{10,... | collective-permute-start | bytes 638984 | tf_op jit(solution)/shard_map/ppermute | solution.py:30
  78.9 0.7 collective-permute-done.38.refs_2_
  80.4 0.7 collective-permute-start.54
  81.2 3.6 %decode.9.refs_13_.refs_5_.refs_7_ = bf16[1664,2048]{1,0:T(8,128)(2,1)S(1)} custom-call(bf16[3328,2048]{1,0:T(8,128)(2,1)} %w_ref.4, f32[26,2048]{1,0:T(8,128)} %sc_ref.9), custom_call_target="tpu_custom_call" | custom-call | flops 1024 | bytes 1024 | tf_op jit(solution)/shard_map/decode/pallas_call | solution.py:82
  88.3 1.4 %collective-permute-start.55 = (bf16[32,3328]{1,0:T(8,128)(2,1)S(1)}, bf16[32,3328]{1,0:T(8,128)(2,1)S(1)}, u32[]{:S(2)}, u32[]{:S(2)}) collective-permute-start(bf16[32,3328]{1,0:T(8,128)(2,1)S(1)} %gated.6.refs_0_), channel_id=1, source_target_pairs={{0,2},{1,3},{2,0},{3,1},{4,6},{5,7},{6,4},{7,5},{8,10},{9,11},{10,... | collective-permute-start | bytes 638984 | tf_op jit(solution)/shard_map/ppermute | solution.py:30
  89.7 5.3 %down.3 = (bf16[4,256,256]{2,1,0:T(8,128)(2,1)S(1)}, bf16[4,256,256]{2,1,0:T(8,128)(2,1)S(1)}) custom-call(s32[1]{0:T(128)} %bitcast.1.place_ref, bf16[32,3328]{1,0:T(8,128)(2,1)S(1)} %gated.4.refs_0_, bf16[32,3328]{1,0:T(8,128)(2,1)S(1)} %collective-permute-done.35.refs_1_, bf16[16,3328]{1,0:T(8,128)(2,1)S(1)} %collective-permute-done.45.refs_2_, ...), custom_call_target="tpu_custom_call" | custom-call | flops 1024 | bytes 1024 | tf_op jit(solution)/shard_map/down/pallas_call | solution.py:196
  95.0 1.6 %collective-permute-start.53 = (bf16[2,256,256]{2,1,0:T(8,128)(2,1)S(1)}, bf16[2,256,256]{2,1,0:T(8,128)(2,1)S(1)}, u32[]{:S(2)}, u32[]{:S(2)}) collective-permute-start(bf16[2,256,256]{2,1,0:T(8,128)(2,1)S(1)} %get-tuple-element.179), channel_id=1, source_target_pairs={{0,4},{4,0},{8,12},{12,8},{16,20},{20,16},{24,28},{28,24},{1,5},{5... | collective-permute-start | bytes 786440 | tf_op jit(solution)/shard_map/ppermute | solution.py:30
  97.5 0.7 collective-permute-start.58
  98.8 0.9 collective-permute-done.57.refs_3_
  99.8 3.5 %down.4 = (bf16[4,128,256]{2,1,0:T(8,128)(2,1)S(1)}, bf16[4,128,256]{2,1,0:T(8,128)(2,1)S(1)}) custom-call(s32[1]{0:T(128)} %bitcast.1.place_ref, bf16[32,3328]{1,0:T(8,128)(2,1)S(1)} %gated.6.refs_0_, bf16[32,3328]{1,0:T(8,128)(2,1)S(1)} %collective-permute-done.55.refs_1_, bf16[32,3328]{1,0:T(8,128)(2,1)S(1)} %collective-permute-done.56.refs_2_, ...), custom_call_target="tpu_custom_call" | custom-call | flops 1024 | bytes 1024 | tf_op jit(solution)/shard_map/down/pallas_call | solution.py:196
  103.3 0.9 collective-permute-done.58.refs_1_
  104.8 1.1 collective-permute-start.67
  106.0 3.5 %down.5 = (bf16[4,128,256]{2,1,0:T(8,128)(2,1)S(1)}, bf16[4,128,256]{2,1,0:T(8,128)(2,1)S(1)}) custom-call(s32[1]{0:T(128)} %bitcast.1.place_ref, bf16[32,3328]{1,0:T(8,128)(2,1)S(1)} %gated.7.refs_0_, bf16[32,3328]{1,0:T(8,128)(2,1)S(1)} %collective-permute-done.58.refs_1_, bf16[16,3328]{1,0:T(8,128)(2,1)S(1)} %collective-permute-done.59.refs_2_, ...), custom_call_target="tpu_custom_call" | custom-call | flops 1024 | bytes 1024 | tf_op jit(solution)/shard_map/down/pallas_call | solution.py:196
  109.5 1.6 %collective-permute-start.65 = (bf16[4,128,256]{2,1,0:T(8,128)(2,1)S(1)}, bf16[4,128,256]{2,1,0:T(8,128)(2,1)S(1)}, u32[]{:S(2)}, u32[]{:S(2)}) collective-permute-start(bf16[4,128,256]{2,1,0:T(8,128)(2,1)S(1)} %get-tuple-element.141), channel_id=1, source_target_pairs={{0,4},{4,0},{8,12},{12,8},{16,20},{20,16},{24,28},{28,24},{1,5},{5... | collective-permute-start | bytes 786440 | tf_op jit(solution)/shard_map/ppermute | solution.py:30
  111.1 1.0 collective-permute-start.64
  112.1 1.0 collective-permute-done.67
  113.2 4.7 %collective-permute-done.65 = bf16[4,128,256]{2,1,0:T(8,128)(2,1)S(1)} collective-permute-done((bf16[4,128,256]{2,1,0:T(8,128)(2,1)S(1)}, bf16[4,128,256]{2,1,0:T(8,128)(2,1)S(1)}, u32[]{:S(2)}, u32[]{:S(2)}) %collective-permute-start.65) | collective-permute-done | bytes 262176 | tf_op jit(solution)/shard_map/ppermute | solution.py:30
  118.0 1.2 collective-permute-start.70
  119.2 1.5 %collective-permute-start.68 = (bf16[2,128,256]{2,1,0:T(8,128)(2,1)S(1)}, bf16[2,128,256]{2,1,0:T(8,128)(2,1)S(1)}, u32[]{:S(2)}, u32[]{:S(2)}) collective-permute-start(bf16[2,128,256]{2,1,0:T(8,128)(2,1)S(1)} %get-tuple-element.150), channel_id=1, source_target_pairs={{0,4},{4,0},{8,12},{12,8},{16,20},{20,16},{24,28},{28,24},{1,5},{5... | collective-permute-start | bytes 393224 | tf_op jit(solution)/shard_map/ppermute | solution.py:30
  120.8 2.6 %collective-permute-start.66 = (bf16[1,256,256]{2,1,0:T(8,128)(2,1)S(1)}, bf16[1,256,256]{2,1,0:T(8,128)(2,1)S(1)}, u32[]{:S(2)}, u32[]{:S(2)}) collective-permute-start(bf16[1,256,256]{2,1,0:T(8,128)(2,1)S(1)} %get-tuple-element.146), channel_id=1, source_target_pairs={{0,16},{4,20},{8,24},{12,28},{16,0},{20,4},{24,8},{28,12},{1,17},{... | collective-permute-start | bytes 393224 | tf_op jit(solution)/shard_map/ppermute | solution.py:30
  123.5 3.9 %collective-permute-start.71 = (bf16[1,128,256]{2,1,0:T(8,128)(2,1)S(1)}, bf16[1,128,256]{2,1,0:T(8,128)(2,1)S(1)}, u32[]{:S(2)}, u32[]{:S(2)}) collective-permute-start(bf16[1,128,256]{2,1,0:T(8,128)(2,1)S(1)} %slice.205), channel_id=1, source_target_pairs={{0,16},{4,20},{8,24},{12,28},{16,0},{20,4},{24,8},{28,12},{1,17},{... | collective-permute-start | bytes 196616 | tf_op jit(solution)/shard_map/ppermute | solution.py:30
  127.5 5.6 %collective-permute-done.66 = bf16[1,256,256]{2,1,0:T(8,128)(2,1)S(1)} collective-permute-done((bf16[1,256,256]{2,1,0:T(8,128)(2,1)S(1)}, bf16[1,256,256]{2,1,0:T(8,128)(2,1)S(1)}, u32[]{:S(2)}, u32[]{:S(2)}) %collective-permute-start.66) | collective-permute-done | bytes 131104 | tf_op jit(solution)/shard_map/ppermute | solution.py:30
  133.2 0.8 collective-permute-done.71
  133.9 0.7 collective-permute-done.69
  134.6 0.7 collect.1
  (156 shorter events, 21.9 us)
Async XLA Ops:
  1.0 7.8 %collective-permute-start = (bf16[1,128,256]{2,1,0:T(8,128)(2,1)S(1)}, bf16[1,128,256]{2,1,0:T(8,128)(2,1)S(1)}, u32[]{:S(2)}, u32[]{:S(2)}) collective-permute-start(bf16[1,128,256]{2,1,0:T(8,128)(2,1)S(1)} %bitcast.32), channel_id=1, source_target_pairs={{0,16},{4,20},{8,24},{12,28},{16,0},{20,4},{24,8},{28,12},{1,17},{... | collective-permute-start | bytes 196616 | tf_op jit(solution)/shard_map/ppermute | solution.py:30
  5.1 6.5 %collective-permute-start.3 = (bf16[1,128,256]{2,1,0:T(8,128)(2,1)S(1)}, bf16[1,128,256]{2,1,0:T(8,128)(2,1)S(1)}, u32[]{:S(2)}, u32[]{:S(2)}) collective-permute-start(bf16[1,128,256]{2,1,0:T(8,128)(2,1)S(1)} %bitcast.29), channel_id=1, source_target_pairs={{0,16},{4,20},{8,24},{12,28},{16,0},{20,4},{24,8},{28,12},{1,17},{... | collective-permute-start | bytes 196616 | tf_op jit(solution)/shard_map/ppermute | solution.py:30
  8.7 10.2 %collective-permute-start.1 = (bf16[2,128,256]{2,1,0:T(8,128)(2,1)S(1)}, bf16[2,128,256]{2,1,0:T(8,128)(2,1)S(1)}, u32[]{:S(2)}, u32[]{:S(2)}) collective-permute-start(bf16[2,128,256]{2,1,0:T(8,128)(2,1)S(1)} %pad_maximum_fusion.2), channel_id=1, source_target_pairs={{0,8},{4,12},{8,0},{12,4},{16,24},{20,28},{24,16},{28,20},{1,9},{5... | collective-permute-start | bytes 393224 | tf_op jit(solution)/shard_map/ppermute | solution.py:30
  14.8 11.3 %collective-permute-start.6 = (bf16[1,128,256]{2,1,0:T(8,128)(2,1)S(1)}, bf16[1,128,256]{2,1,0:T(8,128)(2,1)S(1)}, u32[]{:S(2)}, u32[]{:S(2)}) collective-permute-start(bf16[1,128,256]{2,1,0:T(8,128)(2,1)S(1)} %bitcast.23), channel_id=1, source_target_pairs={{0,16},{4,20},{8,24},{12,28},{16,0},{20,4},{24,8},{28,12},{1,17},{... | collective-permute-start | bytes 196616 | tf_op jit(solution)/shard_map/ppermute | solution.py:30
  17.6 8.6 %collective-permute-start.4 = (bf16[2,128,256]{2,1,0:T(8,128)(2,1)S(1)}, bf16[2,128,256]{2,1,0:T(8,128)(2,1)S(1)}, u32[]{:S(2)}, u32[]{:S(2)}) collective-permute-start(bf16[2,128,256]{2,1,0:T(8,128)(2,1)S(1)} %pad_maximum_fusion.3), channel_id=1, source_target_pairs={{0,8},{4,12},{8,0},{12,4},{16,24},{20,28},{24,16},{28,20},{1,9},{5... | collective-permute-start | bytes 393224 | tf_op jit(solution)/shard_map/ppermute | solution.py:30
  18.8 7.3 %collective-permute-start.8 = (bf16[1,128,256]{2,1,0:T(8,128)(2,1)S(1)}, bf16[1,128,256]{2,1,0:T(8,128)(2,1)S(1)}, u32[]{:S(2)}, u32[]{:S(2)}) collective-permute-start(bf16[1,128,256]{2,1,0:T(8,128)(2,1)S(1)} %bitcast.26), channel_id=1, source_target_pairs={{0,16},{4,20},{8,24},{12,28},{16,0},{20,4},{24,8},{28,12},{1,17},{... | collective-permute-start | bytes 196616 | tf_op jit(solution)/shard_map/ppermute | solution.py:30
  19.0 10.0 %collective-permute-start.2 = (bf16[4,128,256]{2,1,0:T(8,128)(2,1)S(1)}, bf16[4,128,256]{2,1,0:T(8,128)(2,1)S(1)}, u32[]{:S(2)}, u32[]{:S(2)}) collective-permute-start(bf16[4,128,256]{2,1,0:T(8,128)(2,1)S(1)} %pad_maximum_fusion.refs_0_), channel_id=1, source_target_pairs={{0,4},{4,0},{8,12},{12,8},{16,20},{20,16},{24,28},{28,24},{1,5},{5... | collective-permute-start | bytes 786440 | tf_op jit(solution)/shard_map/ppermute | solution.py:30
  26.2 9.0 %collective-permute-start.5 = (bf16[4,128,256]{2,1,0:T(8,128)(2,1)S(1)}, bf16[4,128,256]{2,1,0:T(8,128)(2,1)S(1)}, u32[]{:S(2)}, u32[]{:S(2)}) collective-permute-start(bf16[4,128,256]{2,1,0:T(8,128)(2,1)S(1)} %pad_maximum_fusion.1.refs_0_), channel_id=1, source_target_pairs={{0,4},{4,0},{8,12},{12,8},{16,20},{20,16},{24,28},{28,24},{1,5},{5... | collective-permute-start | bytes 786440 | tf_op jit(solution)/shard_map/ppermute | solution.py:30
  26.8 8.4 %collective-permute-start.7 = (bf16[2,128,256]{2,1,0:T(8,128)(2,1)S(1)}, bf16[2,128,256]{2,1,0:T(8,128)(2,1)S(1)}, u32[]{:S(2)}, u32[]{:S(2)}) collective-permute-start(bf16[2,128,256]{2,1,0:T(8,128)(2,1)S(1)} %pad_maximum_fusion.4), channel_id=1, source_target_pairs={{0,8},{4,12},{8,0},{12,4},{16,24},{20,28},{24,16},{28,20},{1,9},{5... | collective-permute-start | bytes 393224 | tf_op jit(solution)/shard_map/ppermute | solution.py:30
  27.8 7.4 %collective-permute-start.9 = (bf16[2,128,256]{2,1,0:T(8,128)(2,1)S(1)}, bf16[2,128,256]{2,1,0:T(8,128)(2,1)S(1)}, u32[]{:S(2)}, u32[]{:S(2)}) collective-permute-start(bf16[2,128,256]{2,1,0:T(8,128)(2,1)S(1)} %pad_maximum_fusion.5), channel_id=1, source_target_pairs={{0,8},{4,12},{8,0},{12,4},{16,24},{20,28},{24,16},{28,20},{1,9},{5... | collective-permute-start | bytes 393224 | tf_op jit(solution)/shard_map/ppermute | solution.py:30
  35.3 12.0 %collective-permute-start.15 = (bf16[4,128,256]{2,1,0:T(8,128)(2,1)S(1)}, bf16[4,128,256]{2,1,0:T(8,128)(2,1)S(1)}, u32[]{:S(2)}, u32[]{:S(2)}) collective-permute-start(bf16[4,128,256]{2,1,0:T(8,128)(2,1)S(1)} %get-tuple-element.111.refs_0_), channel_id=1, source_target_pairs={{0,4},{4,0},{8,12},{12,8},{16,20},{20,16},{24,28},{28,24},{1,5},{5... | collective-permute-start | bytes 786440 | tf_op jit(solution)/shard_map/ppermute | solution.py:30
  36.9 1.5 %collective-permute-start.13 = (bf16[32,3328]{1,0:T(8,128)(2,1)S(1)}, bf16[32,3328]{1,0:T(8,128)(2,1)S(1)}, u32[]{:S(2)}, u32[]{:S(2)}) collective-permute-start(bf16[32,3328]{1,0:T(8,128)(2,1)S(1)} %get-tuple-element.175), channel_id=1, source_target_pairs={{0,1},{1,0},{2,3},{3,2},{4,5},{5,4},{6,7},{7,6},{8,9},{9,8},{10,11... | collective-permute-start | bytes 638984 | tf_op jit(solution)/shard_map/ppermute | solution.py:30
  37.0 1.8 %collective-permute-start.12 = (bf16[32,3328]{1,0:T(8,128)(2,1)S(1)}, bf16[32,3328]{1,0:T(8,128)(2,1)S(1)}, u32[]{:S(2)}, u32[]{:S(2)}) collective-permute-start(bf16[32,3328]{1,0:T(8,128)(2,1)S(1)} %get-tuple-element.176), channel_id=1, source_target_pairs={{0,1},{1,0},{2,3},{3,2},{4,5},{5,4},{6,7},{7,6},{8,9},{9,8},{10,11... | collective-permute-start | bytes 638984 | tf_op jit(solution)/shard_map/ppermute | solution.py:30
  37.5 1.6 %collective-permute-start.11 = (bf16[32,3328]{1,0:T(8,128)(2,1)S(1)}, bf16[32,3328]{1,0:T(8,128)(2,1)S(1)}, u32[]{:S(2)}, u32[]{:S(2)}) collective-permute-start(bf16[32,3328]{1,0:T(8,128)(2,1)S(1)} %get-tuple-element.177), channel_id=1, source_target_pairs={{0,1},{1,0},{2,3},{3,2},{4,5},{5,4},{6,7},{7,6},{8,9},{9,8},{10,11... | collective-permute-start | bytes 638984 | tf_op jit(solution)/shard_map/ppermute | solution.py:30
  37.6 1.8 %collective-permute-start.10 = (bf16[32,3328]{1,0:T(8,128)(2,1)S(1)}, bf16[32,3328]{1,0:T(8,128)(2,1)S(1)}, u32[]{:S(2)}, u32[]{:S(2)}) collective-permute-start(bf16[32,3328]{1,0:T(8,128)(2,1)S(1)} %get-tuple-element.178), channel_id=1, source_target_pairs={{0,1},{1,0},{2,3},{3,2},{4,5},{5,4},{6,7},{7,6},{8,9},{9,8},{10,11... | collective-permute-start | bytes 638984 | tf_op jit(solution)/shard_map/ppermute | solution.py:30
  39.6 12.9 %collective-permute-start.14 = (bf16[1,2,32,3328]{3,2,1,0:T(8,128)(2,1)S(1)}, bf16[1,2,32,3328]{3,2,1,0:T(8,128)(2,1)S(1)}, u32[]{:S(2)}, u32[]{:S(2)}) collective-permute-start(bf16[1,2,32,3328]{3,2,1,0:T(8,128)(2,1)S(1)} %get-tuple-element.102), channel_id=1, source_target_pairs={{0,2},{1,3},{2,0},{3,1},{4,6},{5,7},{6,4},{7,5},{8,10},{9,11},{10,... | collective-permute-start | bytes 1277960 | tf_op jit(solution)/shard_map/ppermute | solution.py:30
  47.4 1.5 %collective-permute-start.22 = (bf16[16,3328]{1,0:T(8,128)(2,1)S(1)}, bf16[16,3328]{1,0:T(8,128)(2,1)S(1)}, u32[]{:S(2)}, u32[]{:S(2)}) collective-permute-start(bf16[16,3328]{1,0:T(8,128)(2,1)S(1)} %get-tuple-element.168), channel_id=1, source_target_pairs={{0,1},{1,0},{2,3},{3,2},{4,5},{5,4},{6,7},{7,6},{8,9},{9,8},{10,11... | collective-permute-start | bytes 319496 | tf_op jit(solution)/shard_map/ppermute | solution.py:30
  47.9 11.0 %collective-permute-start.24 = (bf16[4,128,256]{2,1,0:T(8,128)(2,1)S(1)}, bf16[4,128,256]{2,1,0:T(8,128)(2,1)S(1)}, u32[]{:S(2)}, u32[]{:S(2)}) collective-permute-start(bf16[4,128,256]{2,1,0:T(8,128)(2,1)S(1)} %get-tuple-element.122.refs_0_), channel_id=1, source_target_pairs={{0,4},{4,0},{8,12},{12,8},{16,20},{20,16},{24,28},{28,24},{1,5},{5... | collective-permute-start | bytes 786440 | tf_op jit(solution)/shard_map/ppermute | solution.py:30
  51.9 16.7 %collective-permute-start.34 = (bf16[1,2,32,3328]{3,2,1,0:T(8,128)(2,1)S(1)}, bf16[1,2,32,3328]{3,2,1,0:T(8,128)(2,1)S(1)}, u32[]{:S(2)}, u32[]{:S(2)}) collective-permute-start(bf16[1,2,32,3328]{3,2,1,0:T(8,128)(2,1)S(1)} %get-tuple-element.109), channel_id=1, source_target_pairs={{0,2},{1,3},{2,0},{3,1},{4,6},{5,7},{6,4},{7,5},{8,10},{9,11},{10,... | collective-permute-start | bytes 1277960 | tf_op jit(solution)/shard_map/ppermute | solution.py:30
  59.6 2.5 %collective-permute-start.30 = (bf16[16,3328]{1,0:T(8,128)(2,1)S(1)}, bf16[16,3328]{1,0:T(8,128)(2,1)S(1)}, u32[]{:S(2)}, u32[]{:S(2)}) collective-permute-start(bf16[16,3328]{1,0:T(8,128)(2,1)S(1)} %get-tuple-element.161), channel_id=1, source_target_pairs={{0,1},{1,0},{2,3},{3,2},{4,5},{5,4},{6,7},{7,6},{8,9},{9,8},{10,11... | collective-permute-start | bytes 319496 | tf_op jit(solution)/shard_map/ppermute | solution.py:30
  59.7 2.5 %collective-permute-start.29 = (bf16[16,3328]{1,0:T(8,128)(2,1)S(1)}, bf16[16,3328]{1,0:T(8,128)(2,1)S(1)}, u32[]{:S(2)}, u32[]{:S(2)}) collective-permute-start(bf16[16,3328]{1,0:T(8,128)(2,1)S(1)} %get-tuple-element.162), channel_id=1, source_target_pairs={{0,1},{1,0},{2,3},{3,2},{4,5},{5,4},{6,7},{7,6},{8,9},{9,8},{10,11... | collective-permute-start | bytes 319496 | tf_op jit(solution)/shard_map/ppermute | solution.py:30
  60.4 2.2 %collective-permute-start.28 = (bf16[16,3328]{1,0:T(8,128)(2,1)S(1)}, bf16[16,3328]{1,0:T(8,128)(2,1)S(1)}, u32[]{:S(2)}, u32[]{:S(2)}) collective-permute-start(bf16[16,3328]{1,0:T(8,128)(2,1)S(1)} %get-tuple-element.163), channel_id=1, source_target_pairs={{0,1},{1,0},{2,3},{3,2},{4,5},{5,4},{6,7},{7,6},{8,9},{9,8},{10,11... | collective-permute-start | bytes 319496 | tf_op jit(solution)/shard_map/ppermute | solution.py:30
  60.6 8.2 %collective-permute-start.35 = (bf16[32,3328]{1,0:T(8,128)(2,1)S(1)}, bf16[32,3328]{1,0:T(8,128)(2,1)S(1)}, u32[]{:S(2)}, u32[]{:S(2)}) collective-permute-start(bf16[32,3328]{1,0:T(8,128)(2,1)S(1)} %gated.4.refs_0_), channel_id=1, source_target_pairs={{0,2},{1,3},{2,0},{3,1},{4,6},{5,7},{6,4},{7,5},{8,10},{9,11},{10,... | collective-permute-start | bytes 638984 | tf_op jit(solution)/shard_map/ppermute | solution.py:30
  64.2 20.8 %collective-permute-start.33 = (bf16[1,2,32,3328]{3,2,1,0:T(8,128)(2,1)S(1)}, bf16[1,2,32,3328]{3,2,1,0:T(8,128)(2,1)S(1)}, u32[]{:S(2)}, u32[]{:S(2)}) collective-permute-start(bf16[1,2,32,3328]{3,2,1,0:T(8,128)(2,1)S(1)} %get-tuple-element.118), channel_id=1, source_target_pairs={{0,2},{1,3},{2,0},{3,1},{4,6},{5,7},{6,4},{7,5},{8,10},{9,11},{10,... | collective-permute-start | bytes 1277960 | tf_op jit(solution)/shard_map/ppermute | solution.py:30
  76.0 2.3 %collective-permute-start.41 = (bf16[16,3328]{1,0:T(8,128)(2,1)S(1)}, bf16[16,3328]{1,0:T(8,128)(2,1)S(1)}, u32[]{:S(2)}, u32[]{:S(2)}) collective-permute-start(bf16[16,3328]{1,0:T(8,128)(2,1)S(1)} %get-tuple-element.153), channel_id=1, source_target_pairs={{0,1},{1,0},{2,3},{3,2},{4,5},{5,4},{6,7},{7,6},{8,9},{9,8},{10,11... | collective-permute-start | bytes 319496 | tf_op jit(solution)/shard_map/ppermute | solution.py:30
  76.1 2.3 %collective-permute-start.40 = (bf16[16,3328]{1,0:T(8,128)(2,1)S(1)}, bf16[16,3328]{1,0:T(8,128)(2,1)S(1)}, u32[]{:S(2)}, u32[]{:S(2)}) collective-permute-start(bf16[16,3328]{1,0:T(8,128)(2,1)S(1)} %get-tuple-element.154), channel_id=1, source_target_pairs={{0,1},{1,0},{2,3},{3,2},{4,5},{5,4},{6,7},{7,6},{8,9},{9,8},{10,11... | collective-permute-start | bytes 319496 | tf_op jit(solution)/shard_map/ppermute | solution.py:30
  76.8 2.0 %collective-permute-start.39 = (bf16[16,3328]{1,0:T(8,128)(2,1)S(1)}, bf16[16,3328]{1,0:T(8,128)(2,1)S(1)}, u32[]{:S(2)}, u32[]{:S(2)}) collective-permute-start(bf16[16,3328]{1,0:T(8,128)(2,1)S(1)} %get-tuple-element.155), channel_id=1, source_target_pairs={{0,1},{1,0},{2,3},{3,2},{4,5},{5,4},{6,7},{7,6},{8,9},{9,8},{10,11... | collective-permute-start | bytes 319496 | tf_op jit(solution)/shard_map/ppermute | solution.py:30
  76.9 8.1 %collective-permute-start.44 = (bf16[32,3328]{1,0:T(8,128)(2,1)S(1)}, bf16[32,3328]{1,0:T(8,128)(2,1)S(1)}, u32[]{:S(2)}, u32[]{:S(2)}) collective-permute-start(bf16[32,3328]{1,0:T(8,128)(2,1)S(1)} %gated.5.refs_6_), channel_id=1, source_target_pairs={{0,2},{1,3},{2,0},{3,1},{4,6},{5,7},{6,4},{7,5},{8,10},{9,11},{10,... | collective-permute-start | bytes 638984 | tf_op jit(solution)/shard_map/ppermute | solution.py:30
  80.4 16.7 %collective-permute-start.54 = (bf16[1,2,32,3328]{3,2,1,0:T(8,128)(2,1)S(1)}, bf16[1,2,32,3328]{3,2,1,0:T(8,128)(2,1)S(1)}, u32[]{:S(2)}, u32[]{:S(2)}) collective-permute-start(bf16[1,2,32,3328]{3,2,1,0:T(8,128)(2,1)S(1)} %get-tuple-element.125), channel_id=1, source_target_pairs={{0,2},{1,3},{2,0},{3,1},{4,6},{5,7},{6,4},{7,5},{8,10},{9,11},{10,... | collective-permute-start | bytes 1277960 | tf_op jit(solution)/shard_map/ppermute | solution.py:30
  87.4 2.2 %collective-permute-start.52 = (bf16[16,3328]{1,0:T(8,128)(2,1)S(1)}, bf16[16,3328]{1,0:T(8,128)(2,1)S(1)}, u32[]{:S(2)}, u32[]{:S(2)}) collective-permute-start(bf16[16,3328]{1,0:T(8,128)(2,1)S(1)} %get-tuple-element.189), channel_id=1, source_target_pairs={{0,1},{1,0},{2,3},{3,2},{4,5},{5,4},{6,7},{7,6},{8,9},{9,8},{10,11... | collective-permute-start | bytes 319496 | tf_op jit(solution)/shard_map/ppermute | solution.py:30
  87.6 2.1 %collective-permute-start.51 = (bf16[16,3328]{1,0:T(8,128)(2,1)S(1)}, bf16[16,3328]{1,0:T(8,128)(2,1)S(1)}, u32[]{:S(2)}, u32[]{:S(2)}) collective-permute-start(bf16[16,3328]{1,0:T(8,128)(2,1)S(1)} %get-tuple-element.190), channel_id=1, source_target_pairs={{0,1},{1,0},{2,3},{3,2},{4,5},{5,4},{6,7},{7,6},{8,9},{9,8},{10,11... | collective-permute-start | bytes 319496 | tf_op jit(solution)/shard_map/ppermute | solution.py:30
  88.1 10.1 %collective-permute-start.56 = (bf16[32,3328]{1,0:T(8,128)(2,1)S(1)}, bf16[32,3328]{1,0:T(8,128)(2,1)S(1)}, u32[]{:S(2)}, u32[]{:S(2)}) collective-permute-start(bf16[32,3328]{1,0:T(8,128)(2,1)S(1)} %gated.6.refs_0_), channel_id=1, source_target_pairs={{0,1},{1,0},{2,3},{3,2},{4,5},{5,4},{6,7},{7,6},{8,9},{9,8},{10,11... | collective-permute-start | bytes 638984 | tf_op jit(solution)/shard_map/ppermute | solution.py:30
  88.3 9.9 %collective-permute-start.55 = (bf16[32,3328]{1,0:T(8,128)(2,1)S(1)}, bf16[32,3328]{1,0:T(8,128)(2,1)S(1)}, u32[]{:S(2)}, u32[]{:S(2)}) collective-permute-start(bf16[32,3328]{1,0:T(8,128)(2,1)S(1)} %gated.6.refs_0_), channel_id=1, source_target_pairs={{0,2},{1,3},{2,0},{3,1},{4,6},{5,7},{6,4},{7,5},{8,10},{9,11},{10,... | collective-permute-start | bytes 638984 | tf_op jit(solution)/shard_map/ppermute | solution.py:30
  95.0 16.0 %collective-permute-start.53 = (bf16[2,256,256]{2,1,0:T(8,128)(2,1)S(1)}, bf16[2,256,256]{2,1,0:T(8,128)(2,1)S(1)}, u32[]{:S(2)}, u32[]{:S(2)}) collective-permute-start(bf16[2,256,256]{2,1,0:T(8,128)(2,1)S(1)} %get-tuple-element.179), channel_id=1, source_target_pairs={{0,4},{4,0},{8,12},{12,8},{16,20},{20,16},{24,28},{28,24},{1,5},{5... | collective-permute-start | bytes 786440 | tf_op jit(solution)/shard_map/ppermute | solution.py:30
  96.6 14.5 %collective-permute-start.63 = (bf16[2,256,256]{2,1,0:T(8,128)(2,1)S(1)}, bf16[2,256,256]{2,1,0:T(8,128)(2,1)S(1)}, u32[]{:S(2)}, u32[]{:S(2)}) collective-permute-start(bf16[2,256,256]{2,1,0:T(8,128)(2,1)S(1)} %get-tuple-element.180), channel_id=1, source_target_pairs={{0,4},{4,0},{8,12},{12,8},{16,20},{20,16},{24,28},{28,24},{1,5},{5... | collective-permute-start | bytes 786440 | tf_op jit(solution)/shard_map/ppermute | solution.py:30
  97.5 6.7 %collective-permute-start.58 = (bf16[32,3328]{1,0:T(8,128)(2,1)S(1)}, bf16[32,3328]{1,0:T(8,128)(2,1)S(1)}, u32[]{:S(2)}, u32[]{:S(2)}) collective-permute-start(bf16[32,3328]{1,0:T(8,128)(2,1)S(1)} %gated.7.refs_0_), channel_id=1, source_target_pairs={{0,2},{1,3},{2,0},{3,1},{4,6},{5,7},{6,4},{7,5},{8,10},{9,11},{10,... | collective-permute-start | bytes 638984 | tf_op jit(solution)/shard_map/ppermute | solution.py:30
  98.2 6.1 %collective-permute-start.60 = (bf16[16,3328]{1,0:T(8,128)(2,1)S(1)}, bf16[16,3328]{1,0:T(8,128)(2,1)S(1)}, u32[]{:S(2)}, u32[]{:S(2)}) collective-permute-start(bf16[16,3328]{1,0:T(8,128)(2,1)S(1)} %get-tuple-element.187), channel_id=1, source_target_pairs={{0,1},{1,0},{2,3},{3,2},{4,5},{5,4},{6,7},{7,6},{8,9},{9,8},{10,11... | collective-permute-start | bytes 319496 | tf_op jit(solution)/shard_map/ppermute | solution.py:30
  99.7 5.1 %collective-permute-start.59 = (bf16[16,3328]{1,0:T(8,128)(2,1)S(1)}, bf16[16,3328]{1,0:T(8,128)(2,1)S(1)}, u32[]{:S(2)}, u32[]{:S(2)}) collective-permute-start(bf16[16,3328]{1,0:T(8,128)(2,1)S(1)} %get-tuple-element.188), channel_id=1, source_target_pairs={{0,1},{1,0},{2,3},{3,2},{4,5},{5,4},{6,7},{7,6},{8,9},{9,8},{10,11... | collective-permute-start | bytes 319496 | tf_op jit(solution)/shard_map/ppermute | solution.py:30
  104.2 1.7 %collective-permute-start.62 = (bf16[16,3328]{1,0:T(8,128)(2,1)S(1)}, bf16[16,3328]{1,0:T(8,128)(2,1)S(1)}, u32[]{:S(2)}, u32[]{:S(2)}) collective-permute-start(bf16[16,3328]{1,0:T(8,128)(2,1)S(1)} %get-tuple-element.185), channel_id=1, source_target_pairs={{0,1},{1,0},{2,3},{3,2},{4,5},{5,4},{6,7},{7,6},{8,9},{9,8},{10,11... | collective-permute-start | bytes 319496 | tf_op jit(solution)/shard_map/ppermute | solution.py:30
  104.3 1.6 %collective-permute-start.61 = (bf16[16,3328]{1,0:T(8,128)(2,1)S(1)}, bf16[16,3328]{1,0:T(8,128)(2,1)S(1)}, u32[]{:S(2)}, u32[]{:S(2)}) collective-permute-start(bf16[16,3328]{1,0:T(8,128)(2,1)S(1)} %get-tuple-element.186), channel_id=1, source_target_pairs={{0,1},{1,0},{2,3},{3,2},{4,5},{5,4},{6,7},{7,6},{8,9},{9,8},{10,11... | collective-permute-start | bytes 319496 | tf_op jit(solution)/shard_map/ppermute | solution.py:30
  104.8 8.3 %collective-permute-start.67 = (bf16[4,128,256]{2,1,0:T(8,128)(2,1)S(1)}, bf16[4,128,256]{2,1,0:T(8,128)(2,1)S(1)}, u32[]{:S(2)}, u32[]{:S(2)}) collective-permute-start(bf16[4,128,256]{2,1,0:T(8,128)(2,1)S(1)} %get-tuple-element.138), channel_id=1, source_target_pairs={{0,8},{4,12},{8,0},{12,4},{16,24},{20,28},{24,16},{28,20},{1,9},{5... | collective-permute-start | bytes 786440 | tf_op jit(solution)/shard_map/ppermute | solution.py:30
  109.5 8.4 %collective-permute-start.65 = (bf16[4,128,256]{2,1,0:T(8,128)(2,1)S(1)}, bf16[4,128,256]{2,1,0:T(8,128)(2,1)S(1)}, u32[]{:S(2)}, u32[]{:S(2)}) collective-permute-start(bf16[4,128,256]{2,1,0:T(8,128)(2,1)S(1)} %get-tuple-element.141), channel_id=1, source_target_pairs={{0,4},{4,0},{8,12},{12,8},{16,20},{20,16},{24,28},{28,24},{1,5},{5... | collective-permute-start | bytes 786440 | tf_op jit(solution)/shard_map/ppermute | solution.py:30
  111.1 9.6 %collective-permute-start.64 = (bf16[2,256,256]{2,1,0:T(8,128)(2,1)S(1)}, bf16[2,256,256]{2,1,0:T(8,128)(2,1)S(1)}, u32[]{:S(2)}, u32[]{:S(2)}) collective-permute-start(bf16[2,256,256]{2,1,0:T(8,128)(2,1)S(1)} %add_convert_fusion.3), channel_id=1, source_target_pairs={{0,8},{4,12},{8,0},{12,4},{16,24},{20,28},{24,16},{28,20},{1,9},{5... | collective-permute-start | bytes 786440 | tf_op jit(solution)/shard_map/ppermute | solution.py:30
  118.0 5.4 %collective-permute-start.70 = (bf16[2,128,256]{2,1,0:T(8,128)(2,1)S(1)}, bf16[2,128,256]{2,1,0:T(8,128)(2,1)S(1)}, u32[]{:S(2)}, u32[]{:S(2)}) collective-permute-start(bf16[2,128,256]{2,1,0:T(8,128)(2,1)S(1)} %slice.197), channel_id=1, source_target_pairs={{0,8},{4,12},{8,0},{12,4},{16,24},{20,28},{24,16},{28,20},{1,9},{5... | collective-permute-start | bytes 393224 | tf_op jit(solution)/shard_map/ppermute | solution.py:30
  119.2 8.2 %collective-permute-start.68 = (bf16[2,128,256]{2,1,0:T(8,128)(2,1)S(1)}, bf16[2,128,256]{2,1,0:T(8,128)(2,1)S(1)}, u32[]{:S(2)}, u32[]{:S(2)}) collective-permute-start(bf16[2,128,256]{2,1,0:T(8,128)(2,1)S(1)} %get-tuple-element.150), channel_id=1, source_target_pairs={{0,4},{4,0},{8,12},{12,8},{16,20},{20,16},{24,28},{28,24},{1,5},{5... | collective-permute-start | bytes 393224 | tf_op jit(solution)/shard_map/ppermute | solution.py:30
  120.8 12.3 %collective-permute-start.66 = (bf16[1,256,256]{2,1,0:T(8,128)(2,1)S(1)}, bf16[1,256,256]{2,1,0:T(8,128)(2,1)S(1)}, u32[]{:S(2)}, u32[]{:S(2)}) collective-permute-start(bf16[1,256,256]{2,1,0:T(8,128)(2,1)S(1)} %get-tuple-element.146), channel_id=1, source_target_pairs={{0,16},{4,20},{8,24},{12,28},{16,0},{20,4},{24,8},{28,12},{1,17},{... | collective-permute-start | bytes 393224 | tf_op jit(solution)/shard_map/ppermute | solution.py:30
  123.5 10.4 %collective-permute-start.71 = (bf16[1,128,256]{2,1,0:T(8,128)(2,1)S(1)}, bf16[1,128,256]{2,1,0:T(8,128)(2,1)S(1)}, u32[]{:S(2)}, u32[]{:S(2)}) collective-permute-start(bf16[1,128,256]{2,1,0:T(8,128)(2,1)S(1)} %slice.205), channel_id=1, source_target_pairs={{0,16},{4,20},{8,24},{12,28},{16,0},{20,4},{24,8},{28,12},{1,17},{... | collective-permute-start | bytes 196616 | tf_op jit(solution)/shard_map/ppermute | solution.py:30
  127.4 7.2 %collective-permute-start.69 = (bf16[1,128,256]{2,1,0:T(8,128)(2,1)S(1)}, bf16[1,128,256]{2,1,0:T(8,128)(2,1)S(1)}, u32[]{:S(2)}, u32[]{:S(2)}) collective-permute-start(bf16[1,128,256]{2,1,0:T(8,128)(2,1)S(1)} %slice.202), channel_id=1, source_target_pairs={{0,16},{4,20},{8,24},{12,28},{16,0},{20,4},{24,8},{28,12},{1,17},{... | collective-permute-start | bytes 196616 | tf_op jit(solution)/shard_map/ppermute | solution.py:30
  (25 other events, 33.6 us)
